TPU v7x, 32 devices: a whole 2x2x4 slice. The times are simulated.
32 devices in a mesh: row: 8 (over y, x, core), col: 4 (over z).
Axes of the slice: x: 2, y: 2, z: 4, core: 2. Of those that a mesh axis runs over, the one named last changes fastest.
Arguments:
- features: bfloat16 [4096, 512], P(('row', 'col')), may hold values from -6 to 6
- weight: bfloat16 [512, 512], replicated, may hold values from -0.25 to 0.25
- edge_tiles: bfloat16 [8, 4, 4, 3, 128, 128], P('row', 'col'), may hold values from -0.3125 to 0.3125
- tile_col: int32 [8, 4, 4, 3], P('row', 'col'), may hold values from 0 to 7, as said below
- tile_count: int32 [8, 4, 4], P('row', 'col'), may hold values from 0 to 3, as said below
- cotangent: bfloat16 [4096, 512], P(('row', 'col')), may hold values from -0.09375 to 0.09375
Outputs:
- activations: bfloat16 [4096, 512], P(('row', 'col'))
- weight_grad: float32 [512, 512], replicated
Inputs may be any that keep to these rules, and one draw needn't show every extreme that they name: `tile_col`: the live slots of one row block name different column blocks; slots that are not live hold arbitrary column blocks. Slots 0 to tile_count - 1 of a row block are live; the others hold arbitrary edge weights that are not part of the adjacency. Some row block holds 3 live slots.
All inputs are finite; a program needn't handle non-finite values.
Results may differ from a plain program's by a relative error of at most 0.024.
Values may be sent and summed in bfloat16 or wider, within the bound.
No kernel may reach another device: no remote copies, remote signals or barrier semaphores. Data moves between devices by JAX's collectives and lax.ppermute only.
A program may use at most 64 MiB of HBM per device.

v0:
```python
import jax
import jax.numpy as jnp
from jax import lax
from jax.sharding import PartitionSpec as P


def local(features, weight, edge_tiles, tile_col, tile_count, cotangent):
    block_rows = features.shape[0]
    width_in = features.shape[1]
    row_blocks = edge_tiles.shape[2]
    slot_total = edge_tiles.shape[3]
    gathered = lax.all_gather(features, "row", axis=0, tiled=True)
    node_blocks = gathered.reshape(-1, block_rows, width_in)
    local_tiles = edge_tiles[0, 0]
    column_ids = tile_col[0, 0]
    live_counts = tile_count[0, 0]
    running = jnp.zeros((row_blocks, block_rows, width_in), jnp.float32)
    for slot in range(slot_total):
        picked = node_blocks[column_ids[:, slot]]
        product = jnp.einsum(
            "aij,ajf->aif", local_tiles[:, slot], picked, preferred_element_type=jnp.float32
        )
        is_live = (slot < live_counts)[:, None, None]
        running = running + jnp.where(is_live, product, 0.0)
    rounded_terms = running.reshape(row_blocks * block_rows, width_in).astype(jnp.bfloat16)
    owned = lax.psum_scatter(rounded_terms, "col", scatter_dimension=0, tiled=True).astype(
        jnp.float32
    )
    aggregated = owned.astype(jnp.bfloat16)
    preact = jnp.dot(aggregated, weight, preferred_element_type=jnp.float32)
    sigmoid_pre = jax.nn.sigmoid(preact)
    activations = (preact * sigmoid_pre).astype(jnp.bfloat16)
    pre_grad = (
        cotangent.astype(jnp.float32) * sigmoid_pre * (1.0 + preact * (1.0 - sigmoid_pre))
    ).astype(jnp.bfloat16)
    grad_term = lax.dot_general(
        aggregated, pre_grad, (((0,), (0,)), ((), ())), preferred_element_type=jnp.float32
    )
    weight_grad = lax.psum(grad_term, ("row", "col"))
    return (activations, weight_grad)


def solution(mesh):
    return jax.shard_map(
        local,
        mesh=mesh,
        in_specs=(
            P(("row", "col"), None),
            P(),
            P("row", "col", None, None, None, None),
            P("row", "col", None, None),
            P("row", "col", None),
            P(("row", "col"), None),
        ),
        out_specs=(P(("row", "col"), None), P()),
        check_vma=False,
    )
```

profile of v0, /device:TPU:0, one launch (start us, length us, event | category | flops | bytes accessed | tf_op | source)
XLA Modules:
  0.0 205.4 jit_solution(8825244699783376444)
XLA Ops:
  7.2 0.0 copy-start
  7.2 0.0 all-gather.2.cloned.1.call-start
  7.2 0.7 all-gather.2.cloned.1.call-update
  7.9 0.0 reduce-scatter.2.cloned.1.call-start
  8.0 0.1 copy.10
  8.1 1.0 copy.13
  9.1 0.2 fusion.5
  9.3 0.0 copy-start.3
  9.3 0.6 copy-done.3
  10.0 26.2 %all-gather.2.cloned.1.call-done = bf16[1024,512]{1,0:T(8,128)(2,1)} async-done(((bf16[128,512]{1,0:T(8,128)(2,1)}), bf16[1024,512]{1,0:T(8,128)(2,1)}) %all-gather.2.cloned.1.call-update) | async-done | bytes 1048592 | tf_op jit(solution)/shard_map/all_gather | solution.py:12
  36.1 1.9 gather_fusion.2
  38.0 0.6 gather_fusion
  38.6 0.6 gather_fusion.1
  39.2 0.3 convolution_select_fusion.1
  39.5 0.3 convolution_select_fusion
  39.8 1.1 fusion.2
  40.9 0.0 reduce-scatter.2.cloned.1.call-update
  40.9 0.0 all-reduce.2.cloned.1.call-start
  41.0 21.7 %reduce-scatter.2.cloned.1.call-done = bf16[128,512]{1,0:T(8,128)(2,1)} async-done(((bf16[512,512]{1,0:T(8,128)(2,1)}), bf16[128,512]{1,0:T(8,128)(2,1)}) %reduce-scatter.2.cloned.1.call-update) | async-done | bytes 131088 | tf_op jit(solution)/shard_map/reduce_scatter | solution.py:26
  62.7 1.9 multiply_convert_fusion.1
  64.6 1.3 fusion.3
  66.0 0.0 all-reduce.2.cloned.1.call-update
  66.0 130.6 %all-reduce.2.cloned.1.call-done = f32[512,512]{1,0:T(8,128)} async-done(((f32[512,512]{1,0:T(8,128)}), f32[512,512]{1,0:T(8,128)}) %all-reduce.2.cloned.1.call-update) | async-done | bytes 1048592 | tf_op jit(solution)/shard_map/psum | solution.py:39
  196.6 2.3 %copy.15 = f32[512,512]{1,0:T(8,128)} copy(f32[512,512]{1,0:T(8,128)} %all-reduce.2.cloned.1.call-done) | data formatting | bytes 2097152
  (12 shorter events, 0.0 us)
Async XLA Ops:
  7.2 55.5 %copy-start = (bf16[512,512]{1,0:T(8,128)(2,1)S(1)}, bf16[512,512]{1,0:T(8,128)(2,1)}, u32[]{:S(2)}) copy-start(bf16[512,512]{1,0:T(8,128)(2,1)} %param.7) | copy-start | bytes 1572868
  7.2 0.8 copy-start.2
  7.2 28.9 %all-gather.2.cloned.1.call-start = ((), (), s32[]{:S(2)}) async-start(), calls=%async_computation.1 | async-start | bytes 1179648 | tf_op jit(solution)/shard_map/all_gather | solution.py:12
  7.9 54.8 %reduce-scatter.2.cloned.1.call-start = ((), (), s32[]{:S(2)}) async-start(), calls=%async_computation.2 | async-start | bytes 655360 | tf_op jit(solution)/shard_map/reduce_scatter | solution.py:26
  9.3 0.7 copy-start.3
  36.1 1.9 copy-start.1
  40.9 23.7 %copy-start.4 = (bf16[128,512]{1,0:T(8,128)(2,1)S(1)}, bf16[128,512]{1,0:T(8,128)(2,1)}, u32[]{:S(2)}) copy-start(bf16[128,512]{1,0:T(8,128)(2,1)} %param.11) | copy-start | bytes 393220
  40.9 155.6 %all-reduce.2.cloned.1.call-start = ((), (), s32[]{:S(2)}) async-start(), calls=%async_computation.3 | async-start | bytes 2097152 | tf_op jit(solution)/shard_map/psum | solution.py:39
  62.7 1.9 copy-start.5
Sparse Core Ops, SparseCore 0:
  9.9 26.1 all-gather.1
  41.0 21.6 reduce-scatter.1
  68.5 128.0 all-reduce.1
where the time goes:
time: 206 us; the launch traced here: 205 us
  waiting for transfers between devices  179 us (87%)
  between operations  13.8 us (7%)
  local copies, waits for them, and re-layouts  7.09 us (3%)
  matrix products  4.9 us (2%)
    psum x1, waiting for transfers between devices, local(): weight_grad = lax.psum(grad_term, ('row', 'col'))  131 us
    all_gather x1, waiting for transfers between devices, local(): gathered = lax.all_gather(features, 'row', axis=0, tiled=True)  26.2 us
    reduce_scatter x1, waiting for transfers between devices, local(): lax.psum_scatter(rounded_terms, 'col', scatter_dimension=0, tiled=True)  21.7 us
  transfers between devices with their start and end apart: 3, of which 3 were waited for; matrix products, arithmetic and copies ran while one was open for 1% of the time, Pallas kernels for 0%

commit v1 on v0

v1 whole, which is shorter than its diff:
```python
import jax
import jax.numpy as jnp
from jax import lax
from jax.sharding import PartitionSpec as P


def swap(value, axis, bits, size):
    return lax.ppermute(value, axis, [(i, i ^ bits) for i in range(size)])


def make_local(rows, cols):
    chips = rows // 2

    def local(features, weight, edge_tiles, tile_col, tile_count, cotangent):
        block, width = features.shape
        row_blocks, slots = edge_tiles.shape[2:4]
        my_row = lax.axis_index("row")
        my_col = lax.axis_index("col")
        core, chip = my_row % 2, my_row // 2

        even = [features] + [swap(features, "row", 2 * k, rows) for k in range(1, chips)]
        even = jnp.concatenate(even)
        odd = swap(even, "row", 1, rows)

        order = jnp.arange(row_blocks) ^ my_col
        tiles = edge_tiles[0, 0][order]
        counts = tile_count[0, 0][order]
        position = tile_col[0, 0][order] ^ my_row
        live = jnp.arange(slots)[None, :] < counts[:, None]
        position = jnp.where(live, position, rows)

        def dense(parity):
            places = 2 * jnp.arange(chips) + parity
            pick = position[:, :, None] == places[None, None, :]
            out = jnp.zeros((row_blocks, block, chips, block), jnp.bfloat16)
            for slot in range(slots):
                out = jnp.where(
                    pick[:, slot, None, :, None], tiles[:, slot, :, None, :], out
                )
            return out.reshape(row_blocks * block, chips * block)

        terms = jnp.dot(dense(0), even, preferred_element_type=jnp.float32)
        terms = terms + jnp.dot(dense(1), odd, preferred_element_type=jnp.float32)
        terms = terms.astype(jnp.bfloat16).reshape(row_blocks, block, width)

        got = [swap(terms[k], "col", k, cols) for k in range(1, cols)]
        total = terms[0].astype(jnp.float32)
        for part in got:
            total = total + part.astype(jnp.float32)
        aggregated = total.astype(jnp.bfloat16)

        preact = jnp.dot(aggregated, weight, preferred_element_type=jnp.float32)
        sigmoid_pre = jax.nn.sigmoid(preact)
        activations = (preact * sigmoid_pre).astype(jnp.bfloat16)
        pre_grad = (
            cotangent.astype(jnp.float32) * sigmoid_pre * (1.0 + preact * (1.0 - sigmoid_pre))
        ).astype(jnp.bfloat16)
        grad = lax.dot_general(
            aggregated, pre_grad, (((0,), (0,)), ((), ())), preferred_element_type=jnp.float32
        )

        hidden = weight.shape[1]
        half = width // 2
        piece = half // chips
        grad = grad.reshape(2, half, hidden)
        sent = lax.dynamic_index_in_dim(grad, 1 - core, 0, keepdims=False).astype(jnp.bfloat16)
        kept = lax.dynamic_index_in_dim(grad, core, 0, keepdims=False)
        kept = kept + swap(sent, "row", 1, rows).astype(jnp.float32)
        kept = kept.reshape(chips, piece, hidden)
        mine = lax.dynamic_index_in_dim(kept, chip, 0, keepdims=False)
        others = [
            lax.dynamic_index_in_dim(kept, chip ^ k, 0, keepdims=False).astype(jnp.bfloat16)
            for k in range(1, chips)
        ]
        for k in range(1, chips):
            mine = mine + swap(others[k - 1], "row", 2 * k, rows).astype(jnp.float32)
        mine = mine.astype(jnp.bfloat16)
        parts = [mine] + [swap(mine, "col", k, cols) for k in range(1, cols)]
        parts = [part.astype(jnp.float32) for part in parts]
        while len(parts) > 1:
            parts = [parts[i] + parts[i + 1] for i in range(0, len(parts), 2)]
        mine = parts[0].astype(jnp.bfloat16)
        kept = jnp.zeros((chips, piece, hidden), jnp.bfloat16)
        kept = lax.dynamic_update_index_in_dim(kept, mine, chip, 0)
        for k in range(1, chips):
            kept = lax.dynamic_update_index_in_dim(
                kept, swap(mine, "row", 2 * k, rows), chip ^ k, 0
            )
        kept = kept.reshape(half, hidden)
        other = swap(kept, "row", 1, rows)
        first = jnp.where(core == 0, kept, other)
        second = jnp.where(core == 0, other, kept)
        weight_grad = jnp.concatenate([first, second]).astype(jnp.float32)
        return (activations, weight_grad)

    return local


def solution(mesh):
    return jax.shard_map(
        make_local(mesh.shape["row"], mesh.shape["col"]),
        mesh=mesh,
        in_specs=(
            P(("row", "col"), None),
            P(),
            P("row", "col", None, None, None, None),
            P("row", "col", None, None),
            P("row", "col", None),
            P(("row", "col"), None),
        ),
        out_specs=(P(("row", "col"), None), P()),
        check_vma=False,
    )
```

time: 206 us -> 59.2 us (0.29)
  waiting for transfers between devices: 179 us -> 28 us
  starting transfers between devices: 0.12 us -> 21.2 us
  between operations: 13.8 us -> 0.93 us
  local copies, waits for them, and re-layouts: 7.09 us -> 4.34 us
  matrix products: 4.9 us -> 2.19 us
  other arithmetic: 0.2 us -> 2.36 us
    psum x1 -> x0, waiting for transfers between devices: 131 us -> none  [local(): weight_grad = lax.psum(grad_term, ('row', 'col'))]
    ppermute x0 -> x18, waiting for transfers between devices: none -> 28 us  [swap(): return lax.ppermute(value, axis, [(i, i ^ bits) for i in range(size)])]
    all_gather x1 -> x0, waiting for transfers between devices: 26.2 us -> none  [local(): gathered = lax.all_gather(features, 'row', axis=0, tiled=True)]
    reduce_scatter x1 -> x0, waiting for transfers between devices: 21.7 us -> none  [local(): lax.psum_scatter(rounded_terms, 'col', scatter_dimension=0, tiled=True)]
    ppermute x0 -> x18, starting transfers between devices: none -> 21.2 us  [swap(): return lax.ppermute(value, axis, [(i, i ^ bits) for i in range(size)])]
  transfers between devices with their start and end apart: 3 -> 18, of which waited for: 3 -> 13; matrix products, arithmetic and copies ran while one was open for 1% -> 5% of each run, Pallas kernels for 0% -> 0%
where the time goes in v1:
time: 59.2 us; the launch traced here: 59 us
  waiting for transfers between devices  28 us (47%)
  starting transfers between devices  21.2 us (36%)
  local copies, waits for them, and re-layouts  4.34 us (7%)
  other arithmetic  2.36 us (4%)
  matrix products  2.19 us (4%)
  between operations  0.93 us (2%)
    ppermute x18, waiting for transfers between devices, swap(): return lax.ppermute(value, axis, [(i, i ^ bits) for i in range(size)])  28 us
    ppermute x18, starting transfers between devices, swap(): return lax.ppermute(value, axis, [(i, i ^ bits) for i in range(size)])  21.2 us
    unnamed x16, local copies, waits for them, and re-layouts  2.23 us
  transfers between devices with their start and end apart: 18, of which 13 were waited for; matrix products, arithmetic and copies ran while one was open for 5% of the time, Pallas kernels for 0%

profile of v1, /device:TPU:0, one launch (start us, length us, event | category | flops | bytes accessed | tf_op | source)
XLA Modules:
  0.0 59.0 jit_solution(4500923297079424969)
XLA Ops:
  0.6 3.0 %collective-permute-start = (bf16[128,512]{1,0:T(8,128)(2,1)}, bf16[128,512]{1,0:T(8,128)(2,1)S(1)}, u32[]{:S(2)}, u32[]{:S(2)}) collective-permute-start(bf16[128,512]{1,0:T(8,128)(2,1)} %param.6), channel_id=1, source_target_pairs={{0,8},{4,12},{8,0},{12,4},{16,24},{20,28},{24,16},{28,20},{1,9},{5... | collective-permute-start | bytes 393224 | tf_op jit(solution)/shard_map/ppermute | solution.py:8
  3.6 1.5 %collective-permute-start.1 = (bf16[128,512]{1,0:T(8,128)(2,1)}, bf16[128,512]{1,0:T(8,128)(2,1)S(1)}, u32[]{:S(2)}, u32[]{:S(2)}) collective-permute-start(bf16[128,512]{1,0:T(8,128)(2,1)} %param.6), channel_id=1, source_target_pairs={{0,16},{4,20},{8,24},{12,28},{16,0},{20,4},{24,8},{28,12},{1,17},{... | collective-permute-start | bytes 393224 | tf_op jit(solution)/shard_map/ppermute | solution.py:8
  9.6 2.0 %collective-permute-done.1 = bf16[128,512]{1,0:T(8,128)(2,1)S(1)} collective-permute-done((bf16[128,512]{1,0:T(8,128)(2,1)}, bf16[128,512]{1,0:T(8,128)(2,1)S(1)}, u32[]{:S(2)}, u32[]{:S(2)}) %collective-permute-start.1) | collective-permute-done | bytes 131104 | tf_op jit(solution)/shard_map/ppermute | solution.py:8
  12.6 1.1 %collective-permute-done.3 = bf16[512,512]{1,0:T(8,128)(2,1)S(1)} collective-permute-done((bf16[512,512]{1,0:T(8,128)(2,1)S(1)}, bf16[512,512]{1,0:T(8,128)(2,1)S(1)}, u32[]{:S(2)}, u32[]{:S(2)}) %collective-permute-start.3) | collective-permute-done | bytes 524320 | tf_op jit(solution)/shard_map/ppermute | solution.py:8
  14.6 1.6 %collective-permute-start.4 = (bf16[128,512]{1,0:T(8,128)(2,1)S(1)}, bf16[128,512]{1,0:T(8,128)(2,1)S(1)}, u32[]{:S(2)}, u32[]{:S(2)}) collective-permute-start(bf16[128,512]{1,0:T(8,128)(2,1)S(1)} %get-tuple-element.9), channel_id=1, source_target_pairs={{0,1},{1,0},{2,3},{3,2},{4,5},{5,4},{6,7},{7,6},{8,9},{9,8},{10,11... | collective-permute-start | bytes 393224 | tf_op jit(solution)/shard_map/ppermute | solution.py:8
  16.2 2.6 %collective-permute-start.5 = (bf16[128,512]{1,0:T(8,128)(2,1)S(1)}, bf16[128,512]{1,0:T(8,128)(2,1)S(1)}, u32[]{:S(2)}, u32[]{:S(2)}) collective-permute-start(bf16[128,512]{1,0:T(8,128)(2,1)S(1)} %get-tuple-element.11), channel_id=1, source_target_pairs={{0,2},{1,3},{2,0},{3,1},{4,6},{5,7},{6,4},{7,5},{8,10},{9,11},{10,... | collective-permute-start | bytes 393224 | tf_op jit(solution)/shard_map/ppermute | solution.py:8
  19.0 3.1 %collective-permute-done.4 = bf16[128,512]{1,0:T(8,128)(2,1)S(1)} collective-permute-done((bf16[128,512]{1,0:T(8,128)(2,1)S(1)}, bf16[128,512]{1,0:T(8,128)(2,1)S(1)}, u32[]{:S(2)}, u32[]{:S(2)}) %collective-permute-start.4) | collective-permute-done | bytes 131104 | tf_op jit(solution)/shard_map/ppermute | solution.py:8
  22.1 7.0 %collective-permute-done.5 = bf16[128,512]{1,0:T(8,128)(2,1)S(1)} collective-permute-done((bf16[128,512]{1,0:T(8,128)(2,1)S(1)}, bf16[128,512]{1,0:T(8,128)(2,1)S(1)}, u32[]{:S(2)}, u32[]{:S(2)}) %collective-permute-start.5) | collective-permute-done | bytes 131104 | tf_op jit(solution)/shard_map/ppermute | solution.py:8
  29.2 0.9 %multiply_convert_fusion.1 = (bf16[128,512]{1,0:T(8,128)(2,1)}, f32[128,512]{1,0:T(8,128)S(1)}) fusion(bf16[128,512]{1,0:T(8,128)(2,1)S(1)} %add_convert_fusion, bf16[512,512]{1,0:T(8,128)(2,1)S(1)} %copy-done), kind=kOutput, calls=%fused_computation.17 | convolution fusion | flops 67436544 | bytes 1048576 | tf_op jit(solution)/shard_map/dot_general | solution.py:52
  30.7 1.5 %collective-permute-done.7 = bf16[256,512]{1,0:T(8,128)(2,1)S(1)} collective-permute-done((bf16[256,512]{1,0:T(8,128)(2,1)S(1)}, bf16[256,512]{1,0:T(8,128)(2,1)S(1)}, u32[]{:S(2)}, u32[]{:S(2)}) %collective-permute-start.7) | collective-permute-done | bytes 262176 | tf_op jit(solution)/shard_map/ppermute | solution.py:8
  32.3 1.5 %collective-permute-start.10 = (bf16[64,512]{1,0:T(8,128)(2,1)S(1)}, bf16[64,512]{1,0:T(8,128)(2,1)S(1)}, u32[]{:S(2)}, u32[]{:S(2)}) collective-permute-start(bf16[64,512]{1,0:T(8,128)(2,1)S(1)} %get-tuple-element.7), channel_id=1, source_target_pairs={{0,24},{4,28},{8,16},{12,20},{16,8},{20,12},{24,0},{28,4},{1,25},{... | collective-permute-start | bytes 196616 | tf_op jit(solution)/shard_map/ppermute | solution.py:8
  33.9 1.5 %collective-permute-start.8 = (bf16[64,512]{1,0:T(8,128)(2,1)S(1)}, bf16[64,512]{1,0:T(8,128)(2,1)S(1)}, u32[]{:S(2)}, u32[]{:S(2)}) collective-permute-start(bf16[64,512]{1,0:T(8,128)(2,1)S(1)} %get-tuple-element.6), channel_id=1, source_target_pairs={{0,8},{4,12},{8,0},{12,4},{16,24},{20,28},{24,16},{28,20},{1,9},{5... | collective-permute-start | bytes 196616 | tf_op jit(solution)/shard_map/ppermute | solution.py:8
  35.9 2.3 %collective-permute-done.10 = bf16[64,512]{1,0:T(8,128)(2,1)S(1)} collective-permute-done((bf16[64,512]{1,0:T(8,128)(2,1)S(1)}, bf16[64,512]{1,0:T(8,128)(2,1)S(1)}, u32[]{:S(2)}, u32[]{:S(2)}) %collective-permute-start.10) | collective-permute-done | bytes 65568 | tf_op jit(solution)/shard_map/ppermute | solution.py:8
  39.6 2.4 %collective-permute-start.11 = (bf16[64,512]{1,0:T(8,128)(2,1)S(1)}, bf16[64,512]{1,0:T(8,128)(2,1)S(1)}, u32[]{:S(2)}, u32[]{:S(2)}) collective-permute-start(bf16[64,512]{1,0:T(8,128)(2,1)S(1)} %fusion.10), channel_id=1, source_target_pairs={{0,1},{1,0},{2,3},{3,2},{4,5},{5,4},{6,7},{7,6},{8,9},{9,8},{10,11... | collective-permute-start | bytes 196616 | tf_op jit(solution)/shard_map/ppermute | solution.py:8
  42.0 1.1 %collective-permute-start.12 = (bf16[64,512]{1,0:T(8,128)(2,1)S(1)}, bf16[64,512]{1,0:T(8,128)(2,1)S(1)}, u32[]{:S(2)}, u32[]{:S(2)}) collective-permute-start(bf16[64,512]{1,0:T(8,128)(2,1)S(1)} %fusion.10), channel_id=1, source_target_pairs={{0,2},{1,3},{2,0},{3,1},{4,6},{5,7},{6,4},{7,5},{8,10},{9,11},{10,... | collective-permute-start | bytes 196616 | tf_op jit(solution)/shard_map/ppermute | solution.py:8
  43.1 1.4 %collective-permute-start.13 = (bf16[64,512]{1,0:T(8,128)(2,1)S(1)}, bf16[64,512]{1,0:T(8,128)(2,1)S(1)}, u32[]{:S(2)}, u32[]{:S(2)}) collective-permute-start(bf16[64,512]{1,0:T(8,128)(2,1)S(1)} %fusion.10), channel_id=1, source_target_pairs={{0,3},{1,2},{2,1},{3,0},{4,7},{5,6},{6,5},{7,4},{8,11},{9,10},{10,... | collective-permute-start | bytes 196616 | tf_op jit(solution)/shard_map/ppermute | solution.py:8
  44.5 4.7 %collective-permute-done.12 = bf16[64,512]{1,0:T(8,128)(2,1)S(1)} collective-permute-done((bf16[64,512]{1,0:T(8,128)(2,1)S(1)}, bf16[64,512]{1,0:T(8,128)(2,1)S(1)}, u32[]{:S(2)}, u32[]{:S(2)}) %collective-permute-start.12) | collective-permute-done | bytes 65568 | tf_op jit(solution)/shard_map/ppermute | solution.py:8
  49.3 1.0 %collective-permute-start.14 = (bf16[64,512]{1,0:T(8,128)(2,1)S(1)}, bf16[64,512]{1,0:T(8,128)(2,1)S(1)}, u32[]{:S(2)}, u32[]{:S(2)}) collective-permute-start(bf16[64,512]{1,0:T(8,128)(2,1)S(1)} %get-tuple-element.3), channel_id=1, source_target_pairs={{0,8},{4,12},{8,0},{12,4},{16,24},{20,28},{24,16},{28,20},{1,9},{5... | collective-permute-start | bytes 196616 | tf_op jit(solution)/shard_map/ppermute | solution.py:8
  50.2 0.8 %collective-permute-start.15 = (bf16[64,512]{1,0:T(8,128)(2,1)S(1)}, bf16[64,512]{1,0:T(8,128)(2,1)S(1)}, u32[]{:S(2)}, u32[]{:S(2)}) collective-permute-start(bf16[64,512]{1,0:T(8,128)(2,1)S(1)} %get-tuple-element.3), channel_id=1, source_target_pairs={{0,16},{4,20},{8,24},{12,28},{16,0},{20,4},{24,8},{28,12},{1,17},{... | collective-permute-start | bytes 196616 | tf_op jit(solution)/shard_map/ppermute | solution.py:8
  51.1 1.7 %collective-permute-start.16 = (bf16[64,512]{1,0:T(8,128)(2,1)S(1)}, bf16[64,512]{1,0:T(8,128)(2,1)S(1)}, u32[]{:S(2)}, u32[]{:S(2)}) collective-permute-start(bf16[64,512]{1,0:T(8,128)(2,1)S(1)} %get-tuple-element.3), channel_id=1, source_target_pairs={{0,24},{4,28},{8,16},{12,20},{16,8},{20,12},{24,0},{28,4},{1,25},{... | collective-permute-start | bytes 196616 | tf_op jit(solution)/shard_map/ppermute | solution.py:8
  53.6 0.9 %collective-permute-done.15 = bf16[64,512]{1,0:T(8,128)(2,1)S(1)} collective-permute-done((bf16[64,512]{1,0:T(8,128)(2,1)S(1)}, bf16[64,512]{1,0:T(8,128)(2,1)S(1)}, u32[]{:S(2)}, u32[]{:S(2)}) %collective-permute-start.15) | collective-permute-done | bytes 65568 | tf_op jit(solution)/shard_map/ppermute | solution.py:8
  54.5 1.7 %collective-permute-done.16 = bf16[64,512]{1,0:T(8,128)(2,1)S(1)} collective-permute-done((bf16[64,512]{1,0:T(8,128)(2,1)S(1)}, bf16[64,512]{1,0:T(8,128)(2,1)S(1)}, u32[]{:S(2)}, u32[]{:S(2)}) %collective-permute-start.16) | collective-permute-done | bytes 65568 | tf_op jit(solution)/shard_map/ppermute | solution.py:8
  56.3 1.5 %collective-permute-done.17 = bf16[256,512]{1,0:T(8,128)(2,1)S(1)} collective-permute-done((bf16[256,512]{1,0:T(8,128)(2,1)S(1)}, bf16[256,512]{1,0:T(8,128)(2,1)S(1)}, u32[]{:S(2)}, u32[]{:S(2)}) %collective-permute-start.17) | collective-permute-done | bytes 262176 | tf_op jit(solution)/shard_map/ppermute | solution.py:8
  57.9 1.1 %maximum_convert_fusion = f32[512,512]{1,0:T(8,128)} fusion(bf16[256,512]{1,0:T(8,128)(2,1)S(1)} %get-tuple-element.5, bf16[256,512]{1,0:T(8,128)(2,1)S(1)} %get-tuple-element.4), kind=kLoop, calls=%fused_computation.10 | loop fusion | flops 1048576 | bytes 1572864 | tf_op jit(solution)/shard_map/convert_element_type | solution.py:93
  (59 shorter events, 10.1 us)
Async XLA Ops:
  0.6 28.6 %copy-start = (bf16[512,512]{1,0:T(8,128)(2,1)S(1)}, bf16[512,512]{1,0:T(8,128)(2,1)}, u32[]{:S(2)}) copy-start(bf16[512,512]{1,0:T(8,128)(2,1)} %param.7) | copy-start | bytes 1572868
  0.6 8.9 %collective-permute-start = (bf16[128,512]{1,0:T(8,128)(2,1)}, bf16[128,512]{1,0:T(8,128)(2,1)S(1)}, u32[]{:S(2)}, u32[]{:S(2)}) collective-permute-start(bf16[128,512]{1,0:T(8,128)(2,1)} %param.6), channel_id=1, source_target_pairs={{0,8},{4,12},{8,0},{12,4},{16,24},{20,28},{24,16},{28,20},{1,9},{5... | collective-permute-start | bytes 393224 | tf_op jit(solution)/shard_map/ppermute | solution.py:8
  3.6 8.0 %collective-permute-start.1 = (bf16[128,512]{1,0:T(8,128)(2,1)}, bf16[128,512]{1,0:T(8,128)(2,1)S(1)}, u32[]{:S(2)}, u32[]{:S(2)}) collective-permute-start(bf16[128,512]{1,0:T(8,128)(2,1)} %param.6), channel_id=1, source_target_pairs={{0,16},{4,20},{8,24},{12,28},{16,0},{20,4},{24,8},{28,12},{1,17},{... | collective-permute-start | bytes 393224 | tf_op jit(solution)/shard_map/ppermute | solution.py:8
  5.2 6.5 %collective-permute-start.2 = (bf16[128,512]{1,0:T(8,128)(2,1)}, bf16[128,512]{1,0:T(8,128)(2,1)S(1)}, u32[]{:S(2)}, u32[]{:S(2)}) collective-permute-start(bf16[128,512]{1,0:T(8,128)(2,1)} %param.6), channel_id=1, source_target_pairs={{0,24},{4,28},{8,16},{12,20},{16,8},{20,12},{24,0},{28,4},{1,25},{... | collective-permute-start | bytes 393224 | tf_op jit(solution)/shard_map/ppermute | solution.py:8
  5.2 0.7 %copy-start.4 = (s32[1,1,4,3]{2,1,3,0:T(1,128)S(1)}, s32[1,1,4,3]{2,1,3,0:T(1,128)}, u32[]{:S(2)}) copy-start(s32[1,1,4,3]{2,1,3,0:T(1,128)} %param.9) | copy-start | bytes 148
  6.5 0.7 %copy-start.1 = (s32[1,1,4]{2,1,0:T(1,128)S(1)}, s32[1,1,4]{2,1,0:T(1,128)}, u32[]{:S(2)}) copy-start(s32[1,1,4]{2,1,0:T(1,128)} %param.10) | copy-start | bytes 52
  6.5 1.5 %copy-start.2 = (bf16[1,1,4,3,128,128]{5,4,3,2,1,0:T(8,128)(2,1)S(1)}, bf16[1,1,4,3,128,128]{5,4,3,2,1,0:T(8,128)(2,1)}, u32[]{:S(2)}) copy-start(bf16[1,1,4,3,128,128]{5,4,3,2,1,0:T(8,128)(2,1)} %param.8) | copy-start | bytes 1179652
  8.6 0.9 %copy-start.3 = (bf16[128,512]{1,0:T(8,128)(2,1)S(1)}, bf16[128,512]{1,0:T(8,128)(2,1)}, u32[]{:S(2)}) copy-start(bf16[128,512]{1,0:T(8,128)(2,1)} %param.6) | copy-start | bytes 393220
  11.7 2.0 %collective-permute-start.3 = (bf16[512,512]{1,0:T(8,128)(2,1)S(1)}, bf16[512,512]{1,0:T(8,128)(2,1)S(1)}, u32[]{:S(2)}, u32[]{:S(2)}) collective-permute-start(bf16[512,512]{1,0:T(8,128)(2,1)S(1)} %constant_dynamic-update-slice_fusion), channel_id=1, source_target_pairs={{0,4},{4,0},{8,12},{12,8},{16,20},{20,16},{24,28},{28,24},{1,5},{5... | collective-permute-start | bytes 1572872 | tf_op jit(solution)/shard_map/ppermute | solution.py:8
  14.6 7.5 %collective-permute-start.4 = (bf16[128,512]{1,0:T(8,128)(2,1)S(1)}, bf16[128,512]{1,0:T(8,128)(2,1)S(1)}, u32[]{:S(2)}, u32[]{:S(2)}) collective-permute-start(bf16[128,512]{1,0:T(8,128)(2,1)S(1)} %get-tuple-element.9), channel_id=1, source_target_pairs={{0,1},{1,0},{2,3},{3,2},{4,5},{5,4},{6,7},{7,6},{8,9},{9,8},{10,11... | collective-permute-start | bytes 393224 | tf_op jit(solution)/shard_map/ppermute | solution.py:8
  16.2 12.9 %collective-permute-start.5 = (bf16[128,512]{1,0:T(8,128)(2,1)S(1)}, bf16[128,512]{1,0:T(8,128)(2,1)S(1)}, u32[]{:S(2)}, u32[]{:S(2)}) collective-permute-start(bf16[128,512]{1,0:T(8,128)(2,1)S(1)} %get-tuple-element.11), channel_id=1, source_target_pairs={{0,2},{1,3},{2,0},{3,1},{4,6},{5,7},{6,4},{7,5},{8,10},{9,11},{10,... | collective-permute-start | bytes 393224 | tf_op jit(solution)/shard_map/ppermute | solution.py:8
  18.8 10.3 %collective-permute-start.6 = (bf16[128,512]{1,0:T(8,128)(2,1)S(1)}, bf16[128,512]{1,0:T(8,128)(2,1)S(1)}, u32[]{:S(2)}, u32[]{:S(2)}) collective-permute-start(bf16[128,512]{1,0:T(8,128)(2,1)S(1)} %get-tuple-element.10), channel_id=1, source_target_pairs={{0,3},{1,2},{2,1},{3,0},{4,7},{5,6},{6,5},{7,4},{8,11},{9,10},{10,... | collective-permute-start | bytes 393224 | tf_op jit(solution)/shard_map/ppermute | solution.py:8
  29.2 1.0 %copy-start.5 = (bf16[128,512]{1,0:T(8,128)(2,1)S(1)}, bf16[128,512]{1,0:T(8,128)(2,1)}, u32[]{:S(2)}) copy-start(bf16[128,512]{1,0:T(8,128)(2,1)} %param.11) | copy-start | bytes 393220
  30.6 1.6 %collective-permute-start.7 = (bf16[256,512]{1,0:T(8,128)(2,1)S(1)}, bf16[256,512]{1,0:T(8,128)(2,1)S(1)}, u32[]{:S(2)}, u32[]{:S(2)}) collective-permute-start(bf16[256,512]{1,0:T(8,128)(2,1)S(1)} %fusion.6), channel_id=1, source_target_pairs={{0,4},{4,0},{8,12},{12,8},{16,20},{20,16},{24,28},{28,24},{1,5},{5... | collective-permute-start | bytes 786440 | tf_op jit(solution)/shard_map/ppermute | solution.py:8
  32.3 5.8 %collective-permute-start.10 = (bf16[64,512]{1,0:T(8,128)(2,1)S(1)}, bf16[64,512]{1,0:T(8,128)(2,1)S(1)}, u32[]{:S(2)}, u32[]{:S(2)}) collective-permute-start(bf16[64,512]{1,0:T(8,128)(2,1)S(1)} %get-tuple-element.7), channel_id=1, source_target_pairs={{0,24},{4,28},{8,16},{12,20},{16,8},{20,12},{24,0},{28,4},{1,25},{... | collective-permute-start | bytes 196616 | tf_op jit(solution)/shard_map/ppermute | solution.py:8
  33.9 5.0 %collective-permute-start.8 = (bf16[64,512]{1,0:T(8,128)(2,1)S(1)}, bf16[64,512]{1,0:T(8,128)(2,1)S(1)}, u32[]{:S(2)}, u32[]{:S(2)}) collective-permute-start(bf16[64,512]{1,0:T(8,128)(2,1)S(1)} %get-tuple-element.6), channel_id=1, source_target_pairs={{0,8},{4,12},{8,0},{12,4},{16,24},{20,28},{24,16},{28,20},{1,9},{5... | collective-permute-start | bytes 196616 | tf_op jit(solution)/shard_map/ppermute | solution.py:8
  35.3 4.3 %collective-permute-start.9 = (bf16[64,512]{1,0:T(8,128)(2,1)S(1)}, bf16[64,512]{1,0:T(8,128)(2,1)S(1)}, u32[]{:S(2)}, u32[]{:S(2)}) collective-permute-start(bf16[64,512]{1,0:T(8,128)(2,1)S(1)} %get-tuple-element.8), channel_id=1, source_target_pairs={{0,16},{4,20},{8,24},{12,28},{16,0},{20,4},{24,8},{28,12},{1,17},{... | collective-permute-start | bytes 196616 | tf_op jit(solution)/shard_map/ppermute | solution.py:8
  39.6 4.8 %collective-permute-start.11 = (bf16[64,512]{1,0:T(8,128)(2,1)S(1)}, bf16[64,512]{1,0:T(8,128)(2,1)S(1)}, u32[]{:S(2)}, u32[]{:S(2)}) collective-permute-start(bf16[64,512]{1,0:T(8,128)(2,1)S(1)} %fusion.10), channel_id=1, source_target_pairs={{0,1},{1,0},{2,3},{3,2},{4,5},{5,4},{6,7},{7,6},{8,9},{9,8},{10,11... | collective-permute-start | bytes 196616 | tf_op jit(solution)/shard_map/ppermute | solution.py:8
  42.0 7.2 %collective-permute-start.12 = (bf16[64,512]{1,0:T(8,128)(2,1)S(1)}, bf16[64,512]{1,0:T(8,128)(2,1)S(1)}, u32[]{:S(2)}, u32[]{:S(2)}) collective-permute-start(bf16[64,512]{1,0:T(8,128)(2,1)S(1)} %fusion.10), channel_id=1, source_target_pairs={{0,2},{1,3},{2,0},{3,1},{4,6},{5,7},{6,4},{7,5},{8,10},{9,11},{10,... | collective-permute-start | bytes 196616 | tf_op jit(solution)/shard_map/ppermute | solution.py:8
  43.1 6.1 %collective-permute-start.13 = (bf16[64,512]{1,0:T(8,128)(2,1)S(1)}, bf16[64,512]{1,0:T(8,128)(2,1)S(1)}, u32[]{:S(2)}, u32[]{:S(2)}) collective-permute-start(bf16[64,512]{1,0:T(8,128)(2,1)S(1)} %fusion.10), channel_id=1, source_target_pairs={{0,3},{1,2},{2,1},{3,0},{4,7},{5,6},{6,5},{7,4},{8,11},{9,10},{10,... | collective-permute-start | bytes 196616 | tf_op jit(solution)/shard_map/ppermute | solution.py:8
  49.3 4.3 %collective-permute-start.14 = (bf16[64,512]{1,0:T(8,128)(2,1)S(1)}, bf16[64,512]{1,0:T(8,128)(2,1)S(1)}, u32[]{:S(2)}, u32[]{:S(2)}) collective-permute-start(bf16[64,512]{1,0:T(8,128)(2,1)S(1)} %get-tuple-element.3), channel_id=1, source_target_pairs={{0,8},{4,12},{8,0},{12,4},{16,24},{20,28},{24,16},{28,20},{1,9},{5... | collective-permute-start | bytes 196616 | tf_op jit(solution)/shard_map/ppermute | solution.py:8
  50.2 4.3 %collective-permute-start.15 = (bf16[64,512]{1,0:T(8,128)(2,1)S(1)}, bf16[64,512]{1,0:T(8,128)(2,1)S(1)}, u32[]{:S(2)}, u32[]{:S(2)}) collective-permute-start(bf16[64,512]{1,0:T(8,128)(2,1)S(1)} %get-tuple-element.3), channel_id=1, source_target_pairs={{0,16},{4,20},{8,24},{12,28},{16,0},{20,4},{24,8},{28,12},{1,17},{... | collective-permute-start | bytes 196616 | tf_op jit(solution)/shard_map/ppermute | solution.py:8
  51.1 5.2 %collective-permute-start.16 = (bf16[64,512]{1,0:T(8,128)(2,1)S(1)}, bf16[64,512]{1,0:T(8,128)(2,1)S(1)}, u32[]{:S(2)}, u32[]{:S(2)}) collective-permute-start(bf16[64,512]{1,0:T(8,128)(2,1)S(1)} %get-tuple-element.3), channel_id=1, source_target_pairs={{0,24},{4,28},{8,16},{12,20},{16,8},{20,12},{24,0},{28,4},{1,25},{... | collective-permute-start | bytes 196616 | tf_op jit(solution)/shard_map/ppermute | solution.py:8
  56.2 1.6 %collective-permute-start.17 = (bf16[256,512]{1,0:T(8,128)(2,1)S(1)}, bf16[256,512]{1,0:T(8,128)(2,1)S(1)}, u32[]{:S(2)}, u32[]{:S(2)}) collective-permute-start(bf16[256,512]{1,0:T(8,128)(2,1)S(1)} %bitcast.74), channel_id=1, source_target_pairs={{0,4},{4,0},{8,12},{12,8},{16,20},{20,16},{24,28},{28,24},{1,5},{5... | collective-permute-start | bytes 786440 | tf_op jit(solution)/shard_map/ppermute | solution.py:8

commit v2 on v1

v2 whole, which is shorter than its diff:
```python
import jax
import jax.numpy as jnp
from jax import lax
from jax.sharding import PartitionSpec as P


def make_local(rows, cols):
    chips = rows // 2
    alike = chips == cols

    def over_row(value, bits):
        return lax.ppermute(value, "row", [(i, i ^ bits) for i in range(rows)])

    def over_col(value, bits):
        return lax.ppermute(value, "col", [(i, i ^ bits) for i in range(cols)])

    def by_core(value, bits, flip):
        pairs = []
        for i in range(rows):
            for j in range(cols):
                if i % 2 == flip:
                    target = (i ^ (2 * bits)) * cols + j
                else:
                    target = i * cols + (j ^ bits)
                pairs.append((i * cols + j, target))
        return lax.ppermute(value, ("row", "col"), pairs)

    def local(features, weight, edge_tiles, tile_col, tile_count, cotangent):
        block, width = features.shape
        row_blocks, slots = edge_tiles.shape[2:4]
        my_row = lax.axis_index("row")
        my_col = lax.axis_index("col")
        core, chip = my_row % 2, my_row // 2

        far = [over_row(features, 2 * k) for k in range(chips - 1, 0, -1)]
        even = jnp.concatenate([features] + far)
        odd = over_row(even, 1)

        order = jnp.arange(row_blocks) ^ my_col
        tiles = edge_tiles[0, 0][order]
        counts = tile_count[0, 0][order]
        position = tile_col[0, 0][order] ^ my_row
        live = jnp.arange(slots)[None, :] < counts[:, None]
        position = jnp.where(live, position, rows)

        def dense(parity):
            places = 2 * (-jnp.arange(chips) % chips) + parity
            pick = position[:, :, None] == places[None, None, :]
            out = jnp.zeros((row_blocks, block, chips, block), jnp.bfloat16)
            for slot in range(slots):
                out = jnp.where(
                    pick[:, slot, None, :, None], tiles[:, slot, :, None, :], out
                )
            return out.reshape(row_blocks, block, chips * block)

        near_part = jnp.dot(
            dense(0).reshape(row_blocks * block, chips * block),
            even,
            preferred_element_type=jnp.float32,
        ).reshape(row_blocks, block, width)
        adjacency = dense(1)

        def term(k):
            part = jnp.dot(adjacency[k], odd, preferred_element_type=jnp.float32)
            return (near_part[k] + part).astype(jnp.bfloat16)

        got = [over_col(term(k), k) for k in range(cols - 1, 0, -1)]
        total = term(0).astype(jnp.float32)
        for part in got:
            total = total + part.astype(jnp.float32)
        aggregated = total.astype(jnp.bfloat16)

        preact = jnp.dot(aggregated, weight, preferred_element_type=jnp.float32)
        sigmoid_pre = jax.nn.sigmoid(preact)
        activations = (preact * sigmoid_pre).astype(jnp.bfloat16)
        pre_grad = (
            cotangent.astype(jnp.float32) * sigmoid_pre * (1.0 + preact * (1.0 - sigmoid_pre))
        ).astype(jnp.bfloat16)
        grad = lax.dot_general(
            aggregated, pre_grad, (((0,), (0,)), ((), ())), preferred_element_type=jnp.float32
        )

        hidden = weight.shape[1]
        half = width // 2
        grad = grad.reshape(2, half, hidden)
        sent = lax.dynamic_index_in_dim(grad, 1 - core, 0, keepdims=False).astype(jnp.bfloat16)
        kept = lax.dynamic_index_in_dim(grad, core, 0, keepdims=False)
        kept = kept + over_row(sent, 1).astype(jnp.float32)
        if alike:
            place = jnp.where(core == 0, chip, my_col)
            shares, first = chips, lambda value, k: by_core(value, k, 0)
            peers, second = cols, lambda value, k: by_core(value, k, 1)
        else:
            place = chip
            shares, first = chips, lambda value, k: over_row(value, 2 * k)
            peers, second = cols, over_col
        piece = half // shares
        kept = kept.reshape(shares, piece, hidden)
        mine = lax.dynamic_index_in_dim(kept, place, 0, keepdims=False)
        for k in range(1, shares):
            other = lax.dynamic_index_in_dim(kept, place ^ k, 0, keepdims=False)
            mine = mine + first(other.astype(jnp.bfloat16), k).astype(jnp.float32)
        mine = mine.astype(jnp.bfloat16)
        parts = [second(mine, k) for k in range(peers - 1, 0, -1)] + [mine]
        parts = [part.astype(jnp.float32) for part in parts]
        while len(parts) > 1:
            parts = [parts[i] + parts[i + 1] for i in range(0, len(parts), 2)]
        mine = parts[0].astype(jnp.bfloat16)
        kept = jnp.zeros((shares, piece, hidden), jnp.bfloat16)
        for k in range(shares - 1, 0, -1):
            kept = lax.dynamic_update_index_in_dim(kept, first(mine, k), place ^ k, 0)
        kept = lax.dynamic_update_index_in_dim(kept, mine, place, 0)
        kept = kept.reshape(half, hidden)
        other = over_row(kept, 1)
        weight_grad = jnp.zeros((2, half, hidden), jnp.float32)
        weight_grad = lax.dynamic_update_index_in_dim(
            weight_grad, kept.astype(jnp.float32), core, 0
        )
        weight_grad = lax.dynamic_update_index_in_dim(
            weight_grad, other.astype(jnp.float32), 1 - core, 0
        )
        return (activations, weight_grad.reshape(width, hidden))

    return local


def solution(mesh):
    return jax.shard_map(
        make_local(mesh.shape["row"], mesh.shape["col"]),
        mesh=mesh,
        in_specs=(
            P(("row", "col"), None),
            P(),
            P("row", "col", None, None, None, None),
            P("row", "col", None, None),
            P("row", "col", None),
            P(("row", "col"), None),
        ),
        out_specs=(P(("row", "col"), None), P()),
        check_vma=False,
    )
```

time: 59.2 us -> 56.3 us (0.951)
  waiting for transfers between devices: 28 us -> 24.6 us
  local copies, waits for them, and re-layouts: 4.34 us -> 5.65 us
  other arithmetic: 2.36 us -> 1.32 us
    ppermute x18, waiting for transfers between devices: 28 us -> 24.6 us  [the longest x9 9.95 us: by_core(): return lax.ppermute(value, ('row', 'col'), pairs)]
    convert_element_type x1, other arithmetic: 1.1 us -> 0.04 us  [local(): mine = parts[0].astype(jnp.bfloat16)]
    unnamed x16 -> x18, local copies, waits for them, and re-layouts: 2.23 us -> 3.26 us
    dot_general x2 -> x5, matrix products: 0.87 us -> 1.35 us  [the longest x4 0.91 us: term(): part = jnp.dot(adjacency[k], odd, preferred_element_type=jnp.float32)]
  transfers between devices with their start and end apart: 18 -> 18, of which waited for: 13 -> 15; matrix products, arithmetic and copies ran while one was open for 5% -> 8% of each run, Pallas kernels for 0% -> 0%
where the time goes in v2:
time: 56.3 us; the launch traced here: 56.2 us
  waiting for transfers between devices  24.6 us (44%)
  starting transfers between devices  21 us (37%)
  local copies, waits for them, and re-layouts  5.65 us (10%)
  matrix products  2.66 us (5%)
  other arithmetic  1.32 us (2%)
  between operations  1 us (2%)
    ppermute x9, starting transfers between devices, by_core(): return lax.ppermute(value, ('row', 'col'), pairs)  11.6 us
    ppermute x9, waiting for transfers between devices, by_core(): return lax.ppermute(value, ('row', 'col'), pairs)  9.95 us
    ppermute x3, waiting for transfers between devices, over_col(): return lax.ppermute(value, 'col', [(i, i ^ bits) for i in range(cols)])  9.76 us
    ppermute x6, waiting for transfers between devices, over_row(): return lax.ppermute(value, 'row', [(i, i ^ bits) for i in range(rows)])  4.86 us
    ppermute x6, starting transfers between devices, over_row(): return lax.ppermute(value, 'row', [(i, i ^ bits) for i in range(rows)])  4.82 us
    ppermute x3, starting transfers between devices, over_col(): return lax.ppermute(value, 'col', [(i, i ^ bits) for i in range(cols)])  4.58 us
    unnamed x18, local copies, waits for them, and re-layouts  3.26 us
  transfers between devices with their start and end apart: 18, of which 15 were waited for; matrix products, arithmetic and copies ran while one was open for 8% of the time, Pallas kernels for 0%

profile of v2, /device:TPU:0, one launch (start us, length us, event | category | flops | bytes accessed | tf_op | source)
XLA Modules:
  0.0 56.2 jit_solution(15658570230186327074)
XLA Ops:
  0.6 4.0 %collective-permute-start = (bf16[128,512]{1,0:T(8,128)(2,1)}, bf16[128,512]{1,0:T(8,128)(2,1)S(1)}, u32[]{:S(2)}, u32[]{:S(2)}) collective-permute-start(bf16[128,512]{1,0:T(8,128)(2,1)} %param.6), channel_id=1, source_target_pairs={{0,24},{4,28},{8,16},{12,20},{16,8},{20,12},{24,0},{28,4},{1,25},{... | collective-permute-start | bytes 393224 | tf_op jit(solution)/shard_map/ppermute | solution.py:12
  8.8 0.8 %copy-done.4 = bf16[128,512]{1,0:T(8,128)(2,1)S(1)} copy-done((bf16[128,512]{1,0:T(8,128)(2,1)S(1)}, bf16[128,512]{1,0:T(8,128)(2,1)}, u32[]{:S(2)}) %copy-start.4) | copy-done | bytes 131096
  9.7 1.4 %collective-permute-done.1 = bf16[128,512]{1,0:T(8,128)(2,1)S(1)} collective-permute-done((bf16[128,512]{1,0:T(8,128)(2,1)}, bf16[128,512]{1,0:T(8,128)(2,1)S(1)}, u32[]{:S(2)}, u32[]{:S(2)}) %collective-permute-start.1) | collective-permute-done | bytes 131104 | tf_op jit(solution)/shard_map/ppermute | solution.py:12
  11.5 0.8 %select_select_fusion = (bf16[4,128,4,128]{3,2,1,0:T(4,128)(2,1)S(1)}, bf16[4,128,4,128]{3,2,1,0:T(4,128)(2,1)S(1)}) fusion(pred[4,4]{1,0:T(4,128)(4,1)S(1)} %get-tuple-element.17, pred[4,4]{1,0:T(4,128)(4,1)S(1)} %get-tuple-element.18, pred[4,4]{1,0:T(4,128)(4,1)S(1)} %get-tuple-element.16, bf16[4,128,128]{2,1,0:T(8,128)(2,1)S(1)} %get-tuple-element.13, ...), kind=kLoop, calls=%fused_computation.10 | loop fusion | flops 1572864 | bytes 1441888 | tf_op jit(solution)/shard_map/jit(_where)/select_n | solution.py:51
  13.6 3.7 %collective-permute-start.4 = (bf16[128,512]{1,0:T(8,128)(2,1)S(1)}, bf16[128,512]{1,0:T(8,128)(2,1)S(1)}, u32[]{:S(2)}, u32[]{:S(2)}) collective-permute-start(bf16[128,512]{1,0:T(8,128)(2,1)S(1)} %fusion.6), channel_id=1, source_target_pairs={{0,3},{1,2},{2,1},{3,0},{4,7},{5,6},{6,5},{7,4},{8,11},{9,10},{10,... | collective-permute-start | bytes 393224 | tf_op jit(solution)/shard_map/ppermute | solution.py:15
  17.8 0.8 %collective-permute-start.6 = (bf16[128,512]{1,0:T(8,128)(2,1)S(1)}, bf16[128,512]{1,0:T(8,128)(2,1)S(1)}, u32[]{:S(2)}, u32[]{:S(2)}) collective-permute-start(bf16[128,512]{1,0:T(8,128)(2,1)S(1)} %fusion.4), channel_id=1, source_target_pairs={{0,1},{1,0},{2,3},{3,2},{4,5},{5,4},{6,7},{7,6},{8,9},{9,8},{10,11... | collective-permute-start | bytes 393224 | tf_op jit(solution)/shard_map/ppermute | solution.py:15
  18.9 3.0 %collective-permute-done.4 = bf16[128,512]{1,0:T(8,128)(2,1)S(1)} collective-permute-done((bf16[128,512]{1,0:T(8,128)(2,1)S(1)}, bf16[128,512]{1,0:T(8,128)(2,1)S(1)}, u32[]{:S(2)}, u32[]{:S(2)}) %collective-permute-start.4) | collective-permute-done | bytes 131104 | tf_op jit(solution)/shard_map/ppermute | solution.py:15
  21.9 6.7 %collective-permute-done.5 = bf16[128,512]{1,0:T(8,128)(2,1)S(1)} collective-permute-done((bf16[128,512]{1,0:T(8,128)(2,1)S(1)}, bf16[128,512]{1,0:T(8,128)(2,1)S(1)}, u32[]{:S(2)}, u32[]{:S(2)}) %collective-permute-start.5) | collective-permute-done | bytes 131104 | tf_op jit(solution)/shard_map/ppermute | solution.py:15
  28.8 0.9 %multiply_convert_fusion.1 = (bf16[128,512]{1,0:T(8,128)(2,1)}, f32[128,512]{1,0:T(8,128)S(1)}) fusion(bf16[128,512]{1,0:T(8,128)(2,1)S(1)} %add_convert_fusion, bf16[512,512]{1,0:T(8,128)(2,1)S(1)} %copy-done), kind=kOutput, calls=%fused_computation.22 | convolution fusion | flops 67436544 | bytes 1048576 | tf_op jit(solution)/shard_map/dot_general | solution.py:73
  30.3 1.5 %collective-permute-done.7 = bf16[256,512]{1,0:T(8,128)(2,1)S(1)} collective-permute-done((bf16[256,512]{1,0:T(8,128)(2,1)S(1)}, bf16[256,512]{1,0:T(8,128)(2,1)S(1)}, u32[]{:S(2)}, u32[]{:S(2)}) %collective-permute-start.7) | collective-permute-done | bytes 262176 | tf_op jit(solution)/shard_map/ppermute | solution.py:12
  31.8 1.8 %collective-permute-start.10 = (bf16[64,512]{1,0:T(8,128)(2,1)S(1)}, bf16[64,512]{1,0:T(8,128)(2,1)S(1)}, u32[]{:S(2)}, u32[]{:S(2)}) collective-permute-start(bf16[64,512]{1,0:T(8,128)(2,1)S(1)} %get-tuple-element.3), channel_id=1, source_target_pairs={{0,24},{1,25},{2,26},{3,27},{4,7},{5,6},{6,5},{7,4},{8,16},{9,17},... | collective-permute-start | bytes 196616 | tf_op jit(solution)/shard_map/ppermute | solution.py:26
  33.6 1.2 %collective-permute-start.8 = (bf16[64,512]{1,0:T(8,128)(2,1)S(1)}, bf16[64,512]{1,0:T(8,128)(2,1)S(1)}, u32[]{:S(2)}, u32[]{:S(2)}) collective-permute-start(bf16[64,512]{1,0:T(8,128)(2,1)S(1)} %get-tuple-element.2), channel_id=1, source_target_pairs={{0,8},{1,9},{2,10},{3,11},{4,5},{5,4},{6,7},{7,6},{8,0},{9,1},{10,... | collective-permute-start | bytes 196616 | tf_op jit(solution)/shard_map/ppermute | solution.py:26
  35.4 1.7 %collective-permute-done.10 = bf16[64,512]{1,0:T(8,128)(2,1)S(1)} collective-permute-done((bf16[64,512]{1,0:T(8,128)(2,1)S(1)}, bf16[64,512]{1,0:T(8,128)(2,1)S(1)}, u32[]{:S(2)}, u32[]{:S(2)}) %collective-permute-start.10) | collective-permute-done | bytes 65568 | tf_op jit(solution)/shard_map/ppermute | solution.py:26
  37.1 0.8 %collective-permute-done.8 = bf16[64,512]{1,0:T(8,128)(2,1)S(1)} collective-permute-done((bf16[64,512]{1,0:T(8,128)(2,1)S(1)}, bf16[64,512]{1,0:T(8,128)(2,1)S(1)}, u32[]{:S(2)}, u32[]{:S(2)}) %collective-permute-start.8) | collective-permute-done | bytes 65568 | tf_op jit(solution)/shard_map/ppermute | solution.py:26
  37.9 1.2 %collective-permute-done.9 = bf16[64,512]{1,0:T(8,128)(2,1)S(1)} collective-permute-done((bf16[64,512]{1,0:T(8,128)(2,1)S(1)}, bf16[64,512]{1,0:T(8,128)(2,1)S(1)}, u32[]{:S(2)}, u32[]{:S(2)}) %collective-permute-start.9) | collective-permute-done | bytes 65568 | tf_op jit(solution)/shard_map/ppermute | solution.py:26
  39.2 2.5 %collective-permute-start.11 = (bf16[64,512]{1,0:T(8,128)(2,1)S(1)}, bf16[64,512]{1,0:T(8,128)(2,1)S(1)}, u32[]{:S(2)}, u32[]{:S(2)}) collective-permute-start(bf16[64,512]{1,0:T(8,128)(2,1)S(1)} %fusion.29), channel_id=1, source_target_pairs={{0,3},{1,2},{2,1},{3,0},{4,28},{5,29},{6,30},{7,31},{8,11},{9,10},... | collective-permute-start | bytes 196616 | tf_op jit(solution)/shard_map/ppermute | solution.py:26
  41.7 1.9 %collective-permute-start.13 = (bf16[64,512]{1,0:T(8,128)(2,1)S(1)}, bf16[64,512]{1,0:T(8,128)(2,1)S(1)}, u32[]{:S(2)}, u32[]{:S(2)}) collective-permute-start(bf16[64,512]{1,0:T(8,128)(2,1)S(1)} %fusion.29), channel_id=1, source_target_pairs={{0,1},{1,0},{2,3},{3,2},{4,12},{5,13},{6,14},{7,15},{8,9},{9,8},{1... | collective-permute-start | bytes 196616 | tf_op jit(solution)/shard_map/ppermute | solution.py:26
  43.6 1.7 %collective-permute-done.11 = bf16[64,512]{1,0:T(8,128)(2,1)S(1)} collective-permute-done((bf16[64,512]{1,0:T(8,128)(2,1)S(1)}, bf16[64,512]{1,0:T(8,128)(2,1)S(1)}, u32[]{:S(2)}, u32[]{:S(2)}) %collective-permute-start.11) | collective-permute-done | bytes 65568 | tf_op jit(solution)/shard_map/ppermute | solution.py:26
  45.3 1.6 %collective-permute-done.12 = bf16[64,512]{1,0:T(8,128)(2,1)S(1)} collective-permute-done((bf16[64,512]{1,0:T(8,128)(2,1)S(1)}, bf16[64,512]{1,0:T(8,128)(2,1)S(1)}, u32[]{:S(2)}, u32[]{:S(2)}) %collective-permute-start.12) | collective-permute-done | bytes 65568 | tf_op jit(solution)/shard_map/ppermute | solution.py:26
  46.9 1.6 %collective-permute-start.14 = (bf16[64,512]{1,0:T(8,128)(2,1)S(1)}, bf16[64,512]{1,0:T(8,128)(2,1)S(1)}, u32[]{:S(2)}, u32[]{:S(2)}) collective-permute-start(bf16[64,512]{1,0:T(8,128)(2,1)S(1)} %add_convert_fusion.1), channel_id=1, source_target_pairs={{0,24},{1,25},{2,26},{3,27},{4,7},{5,6},{6,5},{7,4},{8,16},{9,17},... | collective-permute-start | bytes 196616 | tf_op jit(solution)/shard_map/ppermute | solution.py:26
  49.2 1.2 %collective-permute-start.16 = (bf16[64,512]{1,0:T(8,128)(2,1)S(1)}, bf16[64,512]{1,0:T(8,128)(2,1)S(1)}, u32[]{:S(2)}, u32[]{:S(2)}) collective-permute-start(bf16[64,512]{1,0:T(8,128)(2,1)S(1)} %add_convert_fusion.1), channel_id=1, source_target_pairs={{0,8},{1,9},{2,10},{3,11},{4,5},{5,4},{6,7},{7,6},{8,0},{9,1},{10,... | collective-permute-start | bytes 196616 | tf_op jit(solution)/shard_map/ppermute | solution.py:26
  50.5 1.7 %collective-permute-done.14 = bf16[64,512]{1,0:T(8,128)(2,1)S(1)} collective-permute-done((bf16[64,512]{1,0:T(8,128)(2,1)S(1)}, bf16[64,512]{1,0:T(8,128)(2,1)S(1)}, u32[]{:S(2)}, u32[]{:S(2)}) %collective-permute-start.14) | collective-permute-done | bytes 65568 | tf_op jit(solution)/shard_map/ppermute | solution.py:26
  53.8 1.3 %collective-permute-done.17 = bf16[256,512]{1,0:T(8,128)(2,1)S(1)} collective-permute-done((bf16[256,512]{1,0:T(8,128)(2,1)S(1)}, bf16[256,512]{1,0:T(8,128)(2,1)S(1)}, u32[]{:S(2)}, u32[]{:S(2)}) %collective-permute-start.17) | collective-permute-done | bytes 262176 | tf_op jit(solution)/shard_map/ppermute | solution.py:12
  55.2 1.0 %copy-done.2 = f32[2,256,512]{2,1,0:T(8,128)} copy-done((f32[2,256,512]{2,1,0:T(8,128)}, f32[2,256,512]{2,1,0:T(8,128)S(1)}, u32[]{:S(2)}) %copy-start.2) | copy-done | bytes 1048600
  (66 shorter events, 10.2 us)
Async XLA Ops:
  0.6 28.1 %copy-start = (bf16[512,512]{1,0:T(8,128)(2,1)S(1)}, bf16[512,512]{1,0:T(8,128)(2,1)}, u32[]{:S(2)}) copy-start(bf16[512,512]{1,0:T(8,128)(2,1)} %param.7) | copy-start | bytes 1572868
  0.6 9.1 %collective-permute-start = (bf16[128,512]{1,0:T(8,128)(2,1)}, bf16[128,512]{1,0:T(8,128)(2,1)S(1)}, u32[]{:S(2)}, u32[]{:S(2)}) collective-permute-start(bf16[128,512]{1,0:T(8,128)(2,1)} %param.6), channel_id=1, source_target_pairs={{0,24},{4,28},{8,16},{12,20},{16,8},{20,12},{24,0},{28,4},{1,25},{... | collective-permute-start | bytes 393224 | tf_op jit(solution)/shard_map/ppermute | solution.py:12
  4.6 6.5 %collective-permute-start.1 = (bf16[128,512]{1,0:T(8,128)(2,1)}, bf16[128,512]{1,0:T(8,128)(2,1)S(1)}, u32[]{:S(2)}, u32[]{:S(2)}) collective-permute-start(bf16[128,512]{1,0:T(8,128)(2,1)} %param.6), channel_id=1, source_target_pairs={{0,16},{4,20},{8,24},{12,28},{16,0},{20,4},{24,8},{28,12},{1,17},{... | collective-permute-start | bytes 393224 | tf_op jit(solution)/shard_map/ppermute | solution.py:12
  5.1 6.3 %collective-permute-start.2 = (bf16[128,512]{1,0:T(8,128)(2,1)}, bf16[128,512]{1,0:T(8,128)(2,1)S(1)}, u32[]{:S(2)}, u32[]{:S(2)}) collective-permute-start(bf16[128,512]{1,0:T(8,128)(2,1)} %param.6), channel_id=1, source_target_pairs={{0,8},{4,12},{8,0},{12,4},{16,24},{20,28},{24,16},{28,20},{1,9},{5... | collective-permute-start | bytes 393224 | tf_op jit(solution)/shard_map/ppermute | solution.py:12
  5.3 0.7 %copy-start.5 = (s32[1,1,4,3]{2,1,3,0:T(1,128)S(1)}, s32[1,1,4,3]{2,1,3,0:T(1,128)}, u32[]{:S(2)}) copy-start(s32[1,1,4,3]{2,1,3,0:T(1,128)} %param.9) | copy-start | bytes 148
  6.6 1.5 %copy-start.3 = (bf16[1,1,4,3,128,128]{5,4,3,2,1,0:T(8,128)(2,1)S(1)}, bf16[1,1,4,3,128,128]{5,4,3,2,1,0:T(8,128)(2,1)}, u32[]{:S(2)}) copy-start(bf16[1,1,4,3,128,128]{5,4,3,2,1,0:T(8,128)(2,1)} %param.8) | copy-start | bytes 1179652
  8.8 0.9 %copy-start.4 = (bf16[128,512]{1,0:T(8,128)(2,1)S(1)}, bf16[128,512]{1,0:T(8,128)(2,1)}, u32[]{:S(2)}) copy-start(bf16[128,512]{1,0:T(8,128)(2,1)} %param.6) | copy-start | bytes 393220
  11.4 2.0 %collective-permute-start.3 = (bf16[512,512]{1,0:T(8,128)(2,1)S(1)}, bf16[512,512]{1,0:T(8,128)(2,1)S(1)}, u32[]{:S(2)}, u32[]{:S(2)}) collective-permute-start(bf16[512,512]{1,0:T(8,128)(2,1)S(1)} %constant_dynamic-update-slice_fusion), channel_id=1, source_target_pairs={{0,4},{4,0},{8,12},{12,8},{16,20},{20,16},{24,28},{28,24},{1,5},{5... | collective-permute-start | bytes 1572872 | tf_op jit(solution)/shard_map/ppermute | solution.py:12
  13.6 8.3 %collective-permute-start.4 = (bf16[128,512]{1,0:T(8,128)(2,1)S(1)}, bf16[128,512]{1,0:T(8,128)(2,1)S(1)}, u32[]{:S(2)}, u32[]{:S(2)}) collective-permute-start(bf16[128,512]{1,0:T(8,128)(2,1)S(1)} %fusion.6), channel_id=1, source_target_pairs={{0,3},{1,2},{2,1},{3,0},{4,7},{5,6},{6,5},{7,4},{8,11},{9,10},{10,... | collective-permute-start | bytes 393224 | tf_op jit(solution)/shard_map/ppermute | solution.py:15
  17.5 11.1 %collective-permute-start.5 = (bf16[128,512]{1,0:T(8,128)(2,1)S(1)}, bf16[128,512]{1,0:T(8,128)(2,1)S(1)}, u32[]{:S(2)}, u32[]{:S(2)}) collective-permute-start(bf16[128,512]{1,0:T(8,128)(2,1)S(1)} %fusion.5), channel_id=1, source_target_pairs={{0,2},{1,3},{2,0},{3,1},{4,6},{5,7},{6,4},{7,5},{8,10},{9,11},{10,... | collective-permute-start | bytes 393224 | tf_op jit(solution)/shard_map/ppermute | solution.py:15
  17.8 10.8 %collective-permute-start.6 = (bf16[128,512]{1,0:T(8,128)(2,1)S(1)}, bf16[128,512]{1,0:T(8,128)(2,1)S(1)}, u32[]{:S(2)}, u32[]{:S(2)}) collective-permute-start(bf16[128,512]{1,0:T(8,128)(2,1)S(1)} %fusion.4), channel_id=1, source_target_pairs={{0,1},{1,0},{2,3},{3,2},{4,5},{5,4},{6,7},{7,6},{8,9},{9,8},{10,11... | collective-permute-start | bytes 393224 | tf_op jit(solution)/shard_map/ppermute | solution.py:15
  28.7 1.0 %copy-start.6 = (bf16[128,512]{1,0:T(8,128)(2,1)S(1)}, bf16[128,512]{1,0:T(8,128)(2,1)}, u32[]{:S(2)}) copy-start(bf16[128,512]{1,0:T(8,128)(2,1)} %param.11) | copy-start | bytes 393220
  30.1 1.6 %collective-permute-start.7 = (bf16[256,512]{1,0:T(8,128)(2,1)S(1)}, bf16[256,512]{1,0:T(8,128)(2,1)S(1)}, u32[]{:S(2)}, u32[]{:S(2)}) collective-permute-start(bf16[256,512]{1,0:T(8,128)(2,1)S(1)} %fusion.3), channel_id=1, source_target_pairs={{0,4},{4,0},{8,12},{12,8},{16,20},{20,16},{24,28},{28,24},{1,5},{5... | collective-permute-start | bytes 786440 | tf_op jit(solution)/shard_map/ppermute | solution.py:12
  31.8 5.2 %collective-permute-start.10 = (bf16[64,512]{1,0:T(8,128)(2,1)S(1)}, bf16[64,512]{1,0:T(8,128)(2,1)S(1)}, u32[]{:S(2)}, u32[]{:S(2)}) collective-permute-start(bf16[64,512]{1,0:T(8,128)(2,1)S(1)} %get-tuple-element.3), channel_id=1, source_target_pairs={{0,24},{1,25},{2,26},{3,27},{4,7},{5,6},{6,5},{7,4},{8,16},{9,17},... | collective-permute-start | bytes 196616 | tf_op jit(solution)/shard_map/ppermute | solution.py:26
  33.6 4.3 %collective-permute-start.8 = (bf16[64,512]{1,0:T(8,128)(2,1)S(1)}, bf16[64,512]{1,0:T(8,128)(2,1)S(1)}, u32[]{:S(2)}, u32[]{:S(2)}) collective-permute-start(bf16[64,512]{1,0:T(8,128)(2,1)S(1)} %get-tuple-element.2), channel_id=1, source_target_pairs={{0,8},{1,9},{2,10},{3,11},{4,5},{5,4},{6,7},{7,6},{8,0},{9,1},{10,... | collective-permute-start | bytes 196616 | tf_op jit(solution)/shard_map/ppermute | solution.py:26
  34.9 4.3 %collective-permute-start.9 = (bf16[64,512]{1,0:T(8,128)(2,1)S(1)}, bf16[64,512]{1,0:T(8,128)(2,1)S(1)}, u32[]{:S(2)}, u32[]{:S(2)}) collective-permute-start(bf16[64,512]{1,0:T(8,128)(2,1)S(1)} %get-tuple-element.4), channel_id=1, source_target_pairs={{0,16},{1,17},{2,18},{3,19},{4,6},{5,7},{6,4},{7,5},{8,24},{9,25},... | collective-permute-start | bytes 196616 | tf_op jit(solution)/shard_map/ppermute | solution.py:26
  39.2 6.1 %collective-permute-start.11 = (bf16[64,512]{1,0:T(8,128)(2,1)S(1)}, bf16[64,512]{1,0:T(8,128)(2,1)S(1)}, u32[]{:S(2)}, u32[]{:S(2)}) collective-permute-start(bf16[64,512]{1,0:T(8,128)(2,1)S(1)} %fusion.29), channel_id=1, source_target_pairs={{0,3},{1,2},{2,1},{3,0},{4,28},{5,29},{6,30},{7,31},{8,11},{9,10},... | collective-permute-start | bytes 196616 | tf_op jit(solution)/shard_map/ppermute | solution.py:26
  41.7 5.2 %collective-permute-start.12 = (bf16[64,512]{1,0:T(8,128)(2,1)S(1)}, bf16[64,512]{1,0:T(8,128)(2,1)S(1)}, u32[]{:S(2)}, u32[]{:S(2)}) collective-permute-start(bf16[64,512]{1,0:T(8,128)(2,1)S(1)} %fusion.29), channel_id=1, source_target_pairs={{0,2},{1,3},{2,0},{3,1},{4,20},{5,21},{6,22},{7,23},{8,10},{9,11},... | collective-permute-start | bytes 196616 | tf_op jit(solution)/shard_map/ppermute | solution.py:26
  41.7 5.2 %collective-permute-start.13 = (bf16[64,512]{1,0:T(8,128)(2,1)S(1)}, bf16[64,512]{1,0:T(8,128)(2,1)S(1)}, u32[]{:S(2)}, u32[]{:S(2)}) collective-permute-start(bf16[64,512]{1,0:T(8,128)(2,1)S(1)} %fusion.29), channel_id=1, source_target_pairs={{0,1},{1,0},{2,3},{3,2},{4,12},{5,13},{6,14},{7,15},{8,9},{9,8},{1... | collective-permute-start | bytes 196616 | tf_op jit(solution)/shard_map/ppermute | solution.py:26
  46.9 5.2 %collective-permute-start.14 = (bf16[64,512]{1,0:T(8,128)(2,1)S(1)}, bf16[64,512]{1,0:T(8,128)(2,1)S(1)}, u32[]{:S(2)}, u32[]{:S(2)}) collective-permute-start(bf16[64,512]{1,0:T(8,128)(2,1)S(1)} %add_convert_fusion.1), channel_id=1, source_target_pairs={{0,24},{1,25},{2,26},{3,27},{4,7},{5,6},{6,5},{7,4},{8,16},{9,17},... | collective-permute-start | bytes 196616 | tf_op jit(solution)/shard_map/ppermute | solution.py:26
  48.5 4.4 %collective-permute-start.15 = (bf16[64,512]{1,0:T(8,128)(2,1)S(1)}, bf16[64,512]{1,0:T(8,128)(2,1)S(1)}, u32[]{:S(2)}, u32[]{:S(2)}) collective-permute-start(bf16[64,512]{1,0:T(8,128)(2,1)S(1)} %add_convert_fusion.1), channel_id=1, source_target_pairs={{0,16},{1,17},{2,18},{3,19},{4,6},{5,7},{6,4},{7,5},{8,24},{9,25},... | collective-permute-start | bytes 196616 | tf_op jit(solution)/shard_map/ppermute | solution.py:26
  49.2 4.3 %collective-permute-start.16 = (bf16[64,512]{1,0:T(8,128)(2,1)S(1)}, bf16[64,512]{1,0:T(8,128)(2,1)S(1)}, u32[]{:S(2)}, u32[]{:S(2)}) collective-permute-start(bf16[64,512]{1,0:T(8,128)(2,1)S(1)} %add_convert_fusion.1), channel_id=1, source_target_pairs={{0,8},{1,9},{2,10},{3,11},{4,5},{5,4},{6,7},{7,6},{8,0},{9,1},{10,... | collective-permute-start | bytes 196616 | tf_op jit(solution)/shard_map/ppermute | solution.py:26
  53.5 1.6 %collective-permute-start.17 = (bf16[256,512]{1,0:T(8,128)(2,1)S(1)}, bf16[256,512]{1,0:T(8,128)(2,1)S(1)}, u32[]{:S(2)}, u32[]{:S(2)}) collective-permute-start(bf16[256,512]{1,0:T(8,128)(2,1)S(1)} %bitcast.104), channel_id=1, source_target_pairs={{0,4},{4,0},{8,12},{12,8},{16,20},{20,16},{24,28},{28,24},{1,5},{5... | collective-permute-start | bytes 786440 | tf_op jit(solution)/shard_map/ppermute | solution.py:12
  55.2 1.0 %copy-start.2 = (f32[2,256,512]{2,1,0:T(8,128)}, f32[2,256,512]{2,1,0:T(8,128)S(1)}, u32[]{:S(2)}) copy-start(f32[2,256,512]{2,1,0:T(8,128)S(1)} %convert_dynamic-update-slice_fusion) | copy-start | bytes 3145732
  (1 other events, 0.7 us)

commit v3 on v2

v3 whole, which is shorter than its diff:
```python
import functools

import jax
import jax.numpy as jnp
from jax import lax
from jax.experimental import pallas as pl
from jax.experimental.pallas import tpu as pltpu
from jax.sharding import PartitionSpec as P

LIMIT = 8 * 1024 * 1024
VMEM = pl.BlockSpec(memory_space=pltpu.VMEM)
SMEM = pl.BlockSpec(memory_space=pltpu.SMEM)
HBM = pl.BlockSpec(memory_space=pltpu.HBM)


def columns_of(ref, half, size):
    return ref[:, pl.ds(pl.multiple_of(half * size, size), size)]


def grad_half(agg_ref, pre_grad, half, size):
    return lax.dot_general(
        columns_of(agg_ref, half, size),
        pre_grad,
        (((0,), (0,)), ((), ())),
        preferred_element_type=jnp.float32,
    )


def dense_kernel(half_ref, *refs):
    parts, (weight_ref, cot_ref), (agg_ref, preact_ref, pre_ref, sent_ref) = (
        refs[:-6],
        refs[-6:-4],
        refs[-4:],
    )
    total = parts[0][...].astype(jnp.float32)
    for part in parts[1:]:
        total = total + part[...].astype(jnp.float32)
    agg_ref[...] = total.astype(jnp.bfloat16)
    preact = jnp.dot(agg_ref[...], weight_ref[...], preferred_element_type=jnp.float32)
    sigmoid = jax.nn.sigmoid(preact)
    preact_ref[...] = preact
    pre_ref[...] = (
        cot_ref[...].astype(jnp.float32) * sigmoid * (1.0 + preact * (1.0 - sigmoid))
    ).astype(jnp.bfloat16)
    size = sent_ref.shape[0]
    sent_ref[...] = grad_half(agg_ref, pre_ref[...], 1 - half_ref[0], size).astype(jnp.bfloat16)


def kept_kernel(half_ref, agg_ref, pre_ref, preact_ref, kept_ref, act_ref):
    preact = preact_ref[...]
    act_ref[...] = (preact * jax.nn.sigmoid(preact)).astype(jnp.bfloat16)
    kept_ref[...] = grad_half(agg_ref, pre_ref[...], half_ref[0], kept_ref.shape[0])


def first_kernel(half_ref, kept_ref, out_ref, wide_ref, sem):
    wide_ref[...] = kept_ref[...].astype(jnp.float32)
    copy = pltpu.make_async_copy(wide_ref, out_ref.at[half_ref[0]], sem)
    copy.start()
    copy.wait()


def second_kernel(half_ref, other_ref, _, out_ref, wide_ref, sems):
    pieces, size, _ = wide_ref.shape
    copies = []
    for i in range(pieces):
        rows = pl.ds(i * size, size)
        wide_ref[i] = other_ref[rows, :].astype(jnp.float32)
        copies.append(
            pltpu.make_async_copy(wide_ref.at[i], out_ref.at[1 - half_ref[0], rows], sems.at[i])
        )
        copies[-1].start()
    for copy in copies:
        copy.wait()


def write_first(half, kept):
    size, hidden = kept.shape
    return pl.pallas_call(
        first_kernel,
        out_shape=jax.ShapeDtypeStruct((2, size, hidden), jnp.float32),
        in_specs=[SMEM, VMEM],
        out_specs=HBM,
        scratch_shapes=[pltpu.VMEM((size, hidden), jnp.float32), pltpu.SemaphoreType.DMA],
        compiler_params=pltpu.CompilerParams(vmem_limit_bytes=LIMIT),
        cost_estimate=pl.CostEstimate(
            flops=size * hidden, bytes_accessed=6 * size * hidden, transcendentals=0
        ),
    )(half, kept)


def write_second(half, other, out):
    size, hidden = other.shape
    pieces = 4
    return pl.pallas_call(
        second_kernel,
        out_shape=jax.ShapeDtypeStruct(out.shape, out.dtype),
        in_specs=[SMEM, VMEM, HBM],
        out_specs=HBM,
        scratch_shapes=[
            pltpu.VMEM((pieces, size // pieces, hidden), jnp.float32),
            pltpu.SemaphoreType.DMA((pieces,)),
        ],
        input_output_aliases={2: 0},
        compiler_params=pltpu.CompilerParams(vmem_limit_bytes=LIMIT),
        cost_estimate=pl.CostEstimate(
            flops=size * hidden, bytes_accessed=6 * size * hidden, transcendentals=0
        ),
    )(half, other, out)


def dense_part(half, parts, weight, cotangent):
    block, width = parts[0].shape
    hidden = weight.shape[1]
    size = width // 2
    agg, preact, pre, sent = pl.pallas_call(
        dense_kernel,
        out_shape=(
            jax.ShapeDtypeStruct((block, width), jnp.bfloat16),
            jax.ShapeDtypeStruct((block, hidden), jnp.float32),
            jax.ShapeDtypeStruct((block, hidden), jnp.bfloat16),
            jax.ShapeDtypeStruct((size, hidden), jnp.bfloat16),
        ),
        in_specs=[SMEM] + [VMEM] * (len(parts) + 2),
        out_specs=(VMEM,) * 4,
        compiler_params=pltpu.CompilerParams(vmem_limit_bytes=LIMIT),
        cost_estimate=pl.CostEstimate(
            flops=3 * block * width * hidden, bytes_accessed=8 * block * width, transcendentals=0
        ),
    )(half, *parts, weight, cotangent)
    kept, act = pl.pallas_call(
        kept_kernel,
        out_shape=(
            jax.ShapeDtypeStruct((size, hidden), jnp.float32),
            jax.ShapeDtypeStruct((block, hidden), jnp.bfloat16),
        ),
        in_specs=[SMEM] + [VMEM] * 3,
        out_specs=(VMEM,) * 2,
        compiler_params=pltpu.CompilerParams(vmem_limit_bytes=LIMIT),
        cost_estimate=pl.CostEstimate(
            flops=block * width * hidden, bytes_accessed=4 * block * width, transcendentals=0
        ),
    )(half, agg, pre, preact)
    return act, sent, kept


def make_local(rows, cols):
    chips = rows // 2

    def over_row(value, bits):
        return lax.ppermute(value, "row", [(i, i ^ bits) for i in range(rows)])

    def over_col(value, bits):
        return lax.ppermute(value, "col", [(i, i ^ bits) for i in range(cols)])

    masks = [2 * k + bin(k).count("1") % 2 for k in range(chips)]

    def local(features, weight, edge_tiles, tile_col, tile_count, cotangent):
        block, width = features.shape
        row_blocks, slots = edge_tiles.shape[2:4]
        my_row = lax.axis_index("row")
        my_col = lax.axis_index("col")
        chip = my_row // 2

        far = [over_row(features, 2 * k) for k in range(chips - 1, 0, -1)]
        even = jnp.concatenate([features] + far)
        odd = over_row(even, 1)

        order = jnp.arange(row_blocks) ^ my_col
        tiles = edge_tiles[0, 0][order]
        counts = tile_count[0, 0][order]
        position = tile_col[0, 0][order] ^ my_row
        live = jnp.arange(slots)[None, :] < counts[:, None]
        position = jnp.where(live, position, rows)

        def dense(parity):
            places = 2 * (-jnp.arange(chips) % chips) + parity
            pick = position[:, :, None] == places[None, None, :]
            out = jnp.zeros((row_blocks, block, chips, block), jnp.bfloat16)
            for slot in range(slots):
                out = jnp.where(
                    pick[:, slot, None, :, None], tiles[:, slot, :, None, :], out
                )
            return out.reshape(row_blocks, block, chips * block)

        near_part = jnp.dot(
            dense(0).reshape(row_blocks * block, chips * block),
            even,
            preferred_element_type=jnp.float32,
        ).reshape(row_blocks, block, width)
        adjacency = dense(1)

        def term(k):
            part = jnp.dot(adjacency[k], odd, preferred_element_type=jnp.float32)
            return (near_part[k] + part).astype(jnp.bfloat16)

        turns = sorted(range(1, cols), key=lambda k: (k != cols - 1, k))
        got = [over_col(term(k), k) for k in turns]

        half = (my_row + sum((chip >> i) for i in range(chips.bit_length()))) % 2
        half = half.astype(jnp.int32)
        activations, sent, kept = dense_part(half[None], [term(0)] + got, weight, cotangent)

        size, hidden = sent.shape
        kept = kept + over_row(sent, 1).astype(jnp.float32)
        piece = size // chips
        kept = kept.reshape(chips, piece, hidden)
        mine = lax.dynamic_index_in_dim(kept, chip, 0, keepdims=False)
        for k in range(1, chips):
            other = lax.dynamic_index_in_dim(kept, chip ^ k, 0, keepdims=False)
            mine = mine + over_row(other.astype(jnp.bfloat16), masks[k]).astype(jnp.float32)
        mine = mine.astype(jnp.bfloat16)
        parts = [over_col(mine, k) for k in range(cols - 1, 0, -1)] + [mine]
        parts = [part.astype(jnp.float32) for part in parts]
        while len(parts) > 1:
            parts = [parts[i] + parts[i + 1] for i in range(0, len(parts), 2)]
        mine = parts[0].astype(jnp.bfloat16)
        kept = jnp.zeros((chips, piece, hidden), jnp.bfloat16)
        for k in range(chips - 1, 0, -1):
            kept = lax.dynamic_update_index_in_dim(kept, over_row(mine, masks[k]), chip ^ k, 0)
        kept = lax.dynamic_update_index_in_dim(kept, mine, chip, 0)
        kept = kept.reshape(size, hidden)
        other = over_row(kept, 1)
        weight_grad = write_first(half[None], kept)
        weight_grad = write_second(half[None], other, weight_grad)
        return (activations, weight_grad.reshape(width, hidden))

    return local


def solution(mesh):
    return jax.shard_map(
        make_local(mesh.shape["row"], mesh.shape["col"]),
        mesh=mesh,
        in_specs=(
            P(("row", "col"), None),
            P(),
            P("row", "col", None, None, None, None),
            P("row", "col", None, None),
            P("row", "col", None),
            P(("row", "col"), None),
        ),
        out_specs=(P(("row", "col"), None), P()),
        check_vma=False,
    )
```

time: 56.3 us -> 55.4 us (0.984)
  Pallas kernels: 0 us -> 3.03 us
  matrix products: 2.66 us -> 1.35 us
  waiting for transfers between devices: 24.6 us -> 23.3 us
  local copies, waits for them, and re-layouts: 5.65 us -> 4.54 us
    ppermute x9 -> x0, starting transfers between devices: 11.6 us -> none  [by_core(): return lax.ppermute(value, ('row', 'col'), pairs)]
    ppermute x9 -> x0, waiting for transfers between devices: 9.95 us -> none  [by_core(): return lax.ppermute(value, ('row', 'col'), pairs)]
    ppermute x6 -> x12, starting transfers between devices: 4.82 us -> 11.5 us  [over_row(): return lax.ppermute(value, 'row', [(i, i ^ bits) for i in range(rows)])]
    ppermute x3 -> x6, starting transfers between devices: 4.58 us -> 9.47 us  [over_col(): return lax.ppermute(value, 'col', [(i, i ^ bits) for i in range(cols)])]
    ppermute x6 -> x12, waiting for transfers between devices: 4.86 us -> 9.46 us  [over_row(): return lax.ppermute(value, 'row', [(i, i ^ bits) for i in range(rows)])]
    ppermute x3 -> x6, waiting for transfers between devices: 9.76 us -> 13.8 us  [over_col(): return lax.ppermute(value, 'col', [(i, i ^ bits) for i in range(cols)])]
    pallas_call x0 -> x4, Pallas kernels: none -> 3.03 us  [the longest x1 0.87 us: dense_part(): pl.pallas_call(kept_kernel, out_shape=(jax.ShapeDtypeStruct((size, hidden...]
    dot_general x2 -> x0, matrix products: 1.31 us -> none  [the longest x1 0.94 us: local(): preact = jnp.dot(aggregated, weight, preferred_element_type=jnp.float32)]
  transfers between devices with their start and end apart: 18 -> 18, of which waited for: 15 -> 13; matrix products, arithmetic and copies ran while one was open for 8% -> 8% of each run, Pallas kernels for 0% -> 3%
where the time goes in v3:
time: 55.4 us; the launch traced here: 55.2 us
  waiting for transfers between devices  23.3 us (42%)
  starting transfers between devices  20.9 us (38%)
  local copies, waits for them, and re-layouts  4.54 us (8%)
  Pallas kernels  3.03 us (5%)
  matrix products  1.35 us (2%)
  other arithmetic  1.14 us (2%)
  between operations  0.93 us (2%)
    ppermute x6, waiting for transfers between devices, over_col(): return lax.ppermute(value, 'col', [(i, i ^ bits) for i in range(cols)])  13.8 us
    ppermute x12, starting transfers between devices, over_row(): return lax.ppermute(value, 'row', [(i, i ^ bits) for i in range(rows)])  11.5 us
    ppermute x6, starting transfers between devices, over_col(): return lax.ppermute(value, 'col', [(i, i ^ bits) for i in range(cols)])  9.47 us
    ppermute x12, waiting for transfers between devices, over_row(): return lax.ppermute(value, 'row', [(i, i ^ bits) for i in range(rows)])  9.46 us
    unnamed x16, local copies, waits for them, and re-layouts  2.3 us
  transfers between devices with their start and end apart: 18, of which 13 were waited for; matrix products, arithmetic and copies ran while one was open for 8% of the time, Pallas kernels for 3%

profile of v3, /device:TPU:0, one launch (start us, length us, event | category | flops | bytes accessed | tf_op | source)
XLA Modules:
  0.0 55.2 jit_solution(4057367948297769094)
XLA Ops:
  0.6 4.0 %collective-permute-start = (bf16[128,512]{1,0:T(8,128)(2,1)}, bf16[128,512]{1,0:T(8,128)(2,1)S(1)}, u32[]{:S(2)}, u32[]{:S(2)}) collective-permute-start(bf16[128,512]{1,0:T(8,128)(2,1)} %param.6), channel_id=1, source_target_pairs={{0,24},{4,28},{8,16},{12,20},{16,8},{20,12},{24,0},{28,4},{1,25},{... | collective-permute-start | bytes 393224 | tf_op jit(solution)/shard_map/ppermute | solution.py:150
  8.8 0.8 %copy-done.4 = bf16[128,512]{1,0:T(8,128)(2,1)S(1)} copy-done((bf16[128,512]{1,0:T(8,128)(2,1)S(1)}, bf16[128,512]{1,0:T(8,128)(2,1)}, u32[]{:S(2)}) %copy-start.4) | copy-done | bytes 131096
  9.7 1.4 %collective-permute-done.1 = bf16[128,512]{1,0:T(8,128)(2,1)S(1)} collective-permute-done((bf16[128,512]{1,0:T(8,128)(2,1)}, bf16[128,512]{1,0:T(8,128)(2,1)S(1)}, u32[]{:S(2)}, u32[]{:S(2)}) %collective-permute-start.1) | collective-permute-done | bytes 131104 | tf_op jit(solution)/shard_map/ppermute | solution.py:150
  11.5 0.8 %select_select_fusion = (bf16[4,128,4,128]{3,2,1,0:T(4,128)(2,1)S(1)}, bf16[4,128,4,128]{3,2,1,0:T(4,128)(2,1)S(1)}) fusion(pred[4,4]{1,0:T(4,128)(4,1)S(1)} %get-tuple-element.29, pred[4,4]{1,0:T(4,128)(4,1)S(1)} %get-tuple-element.30, pred[4,4]{1,0:T(4,128)(4,1)S(1)} %get-tuple-element.28, bf16[4,128,128]{2,1,0:T(8,128)(2,1)S(1)} %get-tuple-element.25, ...), kind=kLoop, calls=%fused_computation.7 | loop fusion | flops 1572864 | bytes 1441888 | tf_op jit(solution)/shard_map/jit(_where)/select_n | solution.py:180
  13.6 2.7 %collective-permute-start.6 = (bf16[128,512]{1,0:T(8,128)(2,1)S(1)}, bf16[128,512]{1,0:T(8,128)(2,1)S(1)}, u32[]{:S(2)}, u32[]{:S(2)}) collective-permute-start(bf16[128,512]{1,0:T(8,128)(2,1)S(1)} %fusion.3), channel_id=1, source_target_pairs={{0,2},{1,3},{2,0},{3,1},{4,6},{5,7},{6,4},{7,5},{8,10},{9,11},{10,... | collective-permute-start | bytes 393224 | tf_op jit(solution)/shard_map/ppermute | solution.py:153
  16.5 1.6 %collective-permute-start.5 = (bf16[128,512]{1,0:T(8,128)(2,1)S(1)}, bf16[128,512]{1,0:T(8,128)(2,1)S(1)}, u32[]{:S(2)}, u32[]{:S(2)}) collective-permute-start(bf16[128,512]{1,0:T(8,128)(2,1)S(1)} %fusion.4), channel_id=1, source_target_pairs={{0,1},{1,0},{2,3},{3,2},{4,5},{5,4},{6,7},{7,6},{8,9},{9,8},{10,11... | collective-permute-start | bytes 393224 | tf_op jit(solution)/shard_map/ppermute | solution.py:153
  18.9 5.4 %collective-permute-done.6.refs_3_ = bf16[128,512]{1,0:T(8,128)(2,1)S(1)} collective-permute-done((bf16[128,512]{1,0:T(8,128)(2,1)S(1)}, bf16[128,512]{1,0:T(8,128)(2,1)S(1)}, u32[]{:S(2)}, u32[]{:S(2)}) %collective-permute-start.6) | collective-permute-done | bytes 131104 | tf_op jit(solution)/shard_map/ppermute | solution.py:153
  24.3 2.6 %collective-permute-done.4.refs_1_ = bf16[128,512]{1,0:T(8,128)(2,1)S(1)} collective-permute-done((bf16[128,512]{1,0:T(8,128)(2,1)S(1)}, bf16[128,512]{1,0:T(8,128)(2,1)S(1)}, u32[]{:S(2)}, u32[]{:S(2)}) %collective-permute-start.4) | collective-permute-done | bytes 131104 | tf_op jit(solution)/shard_map/ppermute | solution.py:153
  27.5 0.9 %shard_map.78 = (f32[256,512]{1,0:T(8,128)S(1)}, bf16[128,512]{1,0:T(8,128)(2,1)}) custom-call(s32[1]{0:T(128)} %bitcast.half_ref, bf16[128,512]{1,0:T(8,128)(2,1)S(1)} %get-tuple-element.8.agg_ref, bf16[128,512]{1,0:T(8,128)(2,1)S(1)} %get-tuple-element.9.pre_ref, f32[128,512]{1,0:T(8,128)S(1)} %get-tuple-element.10.preact_ref), custom_call_target="tpu_custom_call" | custom-call | flops 33554432 | bytes 262144 | tf_op jit(solution)/shard_map/pallas_call | solution.py:130
  29.1 1.8 %collective-permute-start.10 = (bf16[64,512]{1,0:T(8,128)(2,1)S(1)}, bf16[64,512]{1,0:T(8,128)(2,1)S(1)}, u32[]{:S(2)}, u32[]{:S(2)}) collective-permute-start(bf16[64,512]{1,0:T(8,128)(2,1)S(1)} %get-tuple-element.15), channel_id=1, source_target_pairs={{0,24},{4,28},{8,16},{12,20},{16,8},{20,12},{24,0},{28,4},{1,25},{... | collective-permute-start | bytes 196616 | tf_op jit(solution)/shard_map/ppermute | solution.py:150
  30.9 0.7 %collective-permute-start.8 = (bf16[64,512]{1,0:T(8,128)(2,1)S(1)}, bf16[64,512]{1,0:T(8,128)(2,1)S(1)}, u32[]{:S(2)}, u32[]{:S(2)}) collective-permute-start(bf16[64,512]{1,0:T(8,128)(2,1)S(1)} %get-tuple-element.14), channel_id=1, source_target_pairs={{0,12},{4,8},{8,4},{12,0},{16,28},{20,24},{24,20},{28,16},{1,13},{... | collective-permute-start | bytes 196616 | tf_op jit(solution)/shard_map/ppermute | solution.py:150
  31.6 0.8 %collective-permute-start.9 = (bf16[64,512]{1,0:T(8,128)(2,1)S(1)}, bf16[64,512]{1,0:T(8,128)(2,1)S(1)}, u32[]{:S(2)}, u32[]{:S(2)}) collective-permute-start(bf16[64,512]{1,0:T(8,128)(2,1)S(1)} %get-tuple-element.16), channel_id=1, source_target_pairs={{0,20},{4,16},{8,28},{12,24},{16,4},{20,0},{24,12},{28,8},{1,21},{... | collective-permute-start | bytes 196616 | tf_op jit(solution)/shard_map/ppermute | solution.py:150
  32.4 2.0 %collective-permute-done.10 = bf16[64,512]{1,0:T(8,128)(2,1)S(1)} collective-permute-done((bf16[64,512]{1,0:T(8,128)(2,1)S(1)}, bf16[64,512]{1,0:T(8,128)(2,1)S(1)}, u32[]{:S(2)}, u32[]{:S(2)}) %collective-permute-start.10) | collective-permute-done | bytes 65568 | tf_op jit(solution)/shard_map/ppermute | solution.py:150
  34.3 0.9 %collective-permute-done.8 = bf16[64,512]{1,0:T(8,128)(2,1)S(1)} collective-permute-done((bf16[64,512]{1,0:T(8,128)(2,1)S(1)}, bf16[64,512]{1,0:T(8,128)(2,1)S(1)}, u32[]{:S(2)}, u32[]{:S(2)}) %collective-permute-start.8) | collective-permute-done | bytes 65568 | tf_op jit(solution)/shard_map/ppermute | solution.py:150
  35.3 2.5 %collective-permute-start.11 = (bf16[64,512]{1,0:T(8,128)(2,1)S(1)}, bf16[64,512]{1,0:T(8,128)(2,1)S(1)}, u32[]{:S(2)}, u32[]{:S(2)}) collective-permute-start(bf16[64,512]{1,0:T(8,128)(2,1)S(1)} %fusion.29), channel_id=1, source_target_pairs={{0,3},{1,2},{2,1},{3,0},{4,7},{5,6},{6,5},{7,4},{8,11},{9,10},{10,... | collective-permute-start | bytes 196616 | tf_op jit(solution)/shard_map/ppermute | solution.py:153
  37.9 1.8 %collective-permute-start.12 = (bf16[64,512]{1,0:T(8,128)(2,1)S(1)}, bf16[64,512]{1,0:T(8,128)(2,1)S(1)}, u32[]{:S(2)}, u32[]{:S(2)}) collective-permute-start(bf16[64,512]{1,0:T(8,128)(2,1)S(1)} %fusion.29), channel_id=1, source_target_pairs={{0,2},{1,3},{2,0},{3,1},{4,6},{5,7},{6,4},{7,5},{8,10},{9,11},{10,... | collective-permute-start | bytes 196616 | tf_op jit(solution)/shard_map/ppermute | solution.py:153
  40.2 1.7 %collective-permute-done.11 = bf16[64,512]{1,0:T(8,128)(2,1)S(1)} collective-permute-done((bf16[64,512]{1,0:T(8,128)(2,1)S(1)}, bf16[64,512]{1,0:T(8,128)(2,1)S(1)}, u32[]{:S(2)}, u32[]{:S(2)}) %collective-permute-start.11) | collective-permute-done | bytes 65568 | tf_op jit(solution)/shard_map/ppermute | solution.py:153
  41.9 4.1 %collective-permute-done.12 = bf16[64,512]{1,0:T(8,128)(2,1)S(1)} collective-permute-done((bf16[64,512]{1,0:T(8,128)(2,1)S(1)}, bf16[64,512]{1,0:T(8,128)(2,1)S(1)}, u32[]{:S(2)}, u32[]{:S(2)}) %collective-permute-start.12) | collective-permute-done | bytes 65568 | tf_op jit(solution)/shard_map/ppermute | solution.py:153
  46.1 1.6 %collective-permute-start.14 = (bf16[64,512]{1,0:T(8,128)(2,1)S(1)}, bf16[64,512]{1,0:T(8,128)(2,1)S(1)}, u32[]{:S(2)}, u32[]{:S(2)}) collective-permute-start(bf16[64,512]{1,0:T(8,128)(2,1)S(1)} %add_convert_fusion), channel_id=1, source_target_pairs={{0,24},{4,28},{8,16},{12,20},{16,8},{20,12},{24,0},{28,4},{1,25},{... | collective-permute-start | bytes 196616 | tf_op jit(solution)/shard_map/ppermute | solution.py:150
  48.2 1.2 %collective-permute-start.16 = (bf16[64,512]{1,0:T(8,128)(2,1)S(1)}, bf16[64,512]{1,0:T(8,128)(2,1)S(1)}, u32[]{:S(2)}, u32[]{:S(2)}) collective-permute-start(bf16[64,512]{1,0:T(8,128)(2,1)S(1)} %add_convert_fusion), channel_id=1, source_target_pairs={{0,12},{4,8},{8,4},{12,0},{16,28},{20,24},{24,20},{28,16},{1,13},{... | collective-permute-start | bytes 196616 | tf_op jit(solution)/shard_map/ppermute | solution.py:150
  49.4 2.0 %collective-permute-done.14 = bf16[64,512]{1,0:T(8,128)(2,1)S(1)} collective-permute-done((bf16[64,512]{1,0:T(8,128)(2,1)S(1)}, bf16[64,512]{1,0:T(8,128)(2,1)S(1)}, u32[]{:S(2)}, u32[]{:S(2)}) %collective-permute-start.14) | collective-permute-done | bytes 65568 | tf_op jit(solution)/shard_map/ppermute | solution.py:150
  51.4 1.3 %collective-permute-done.15 = bf16[64,512]{1,0:T(8,128)(2,1)S(1)} collective-permute-done((bf16[64,512]{1,0:T(8,128)(2,1)S(1)}, bf16[64,512]{1,0:T(8,128)(2,1)S(1)}, u32[]{:S(2)}, u32[]{:S(2)}) %collective-permute-start.15) | collective-permute-done | bytes 65568 | tf_op jit(solution)/shard_map/ppermute | solution.py:150
  53.0 0.8 %shard_map.79._ = f32[2,256,512]{2,1,0:T(8,128)} custom-call(s32[1]{0:T(128)} %bitcast.half_ref, bf16[256,512]{1,0:T(8,128)(2,1)S(1)} %bitcast.89), custom_call_target="tpu_custom_call" | custom-call | flops 131072 | bytes 786432 | tf_op jit(solution)/shard_map/pallas_call | solution.py:78
  54.4 0.8 %shard_map.80 = f32[2,256,512]{2,1,0:T(8,128)} custom-call(s32[1]{0:T(128)} %bitcast.half_ref, bf16[256,512]{1,0:T(8,128)(2,1)S(1)} %collective-permute-done.17.other_ref, f32[2,256,512]{2,1,0:T(8,128)} %shard_map.79._), custom_call_target="tpu_custom_call", output_to_operand_aliasing={{}: (2, {})} | custom-call | flops 131072 | bytes 786432 | tf_op jit(solution)/shard_map/pallas_call | solution.py:94
  (61 shorter events, 10.0 us)
Async XLA Ops:
  0.6 7.5 %copy-start = (bf16[1,1,4,3,128,128]{5,4,3,2,1,0:T(8,128)(2,1)S(1)}, bf16[1,1,4,3,128,128]{5,4,3,2,1,0:T(8,128)(2,1)}, u32[]{:S(2)}) copy-start(bf16[1,1,4,3,128,128]{5,4,3,2,1,0:T(8,128)(2,1)} %param.8) | copy-start | bytes 1179652
  0.6 9.1 %collective-permute-start = (bf16[128,512]{1,0:T(8,128)(2,1)}, bf16[128,512]{1,0:T(8,128)(2,1)S(1)}, u32[]{:S(2)}, u32[]{:S(2)}) collective-permute-start(bf16[128,512]{1,0:T(8,128)(2,1)} %param.6), channel_id=1, source_target_pairs={{0,24},{4,28},{8,16},{12,20},{16,8},{20,12},{24,0},{28,4},{1,25},{... | collective-permute-start | bytes 393224 | tf_op jit(solution)/shard_map/ppermute | solution.py:150
  4.6 6.5 %collective-permute-start.1 = (bf16[128,512]{1,0:T(8,128)(2,1)}, bf16[128,512]{1,0:T(8,128)(2,1)S(1)}, u32[]{:S(2)}, u32[]{:S(2)}) collective-permute-start(bf16[128,512]{1,0:T(8,128)(2,1)} %param.6), channel_id=1, source_target_pairs={{0,16},{4,20},{8,24},{12,28},{16,0},{20,4},{24,8},{28,12},{1,17},{... | collective-permute-start | bytes 393224 | tf_op jit(solution)/shard_map/ppermute | solution.py:150
  5.1 6.3 %collective-permute-start.2 = (bf16[128,512]{1,0:T(8,128)(2,1)}, bf16[128,512]{1,0:T(8,128)(2,1)S(1)}, u32[]{:S(2)}, u32[]{:S(2)}) collective-permute-start(bf16[128,512]{1,0:T(8,128)(2,1)} %param.6), channel_id=1, source_target_pairs={{0,8},{4,12},{8,0},{12,4},{16,24},{20,28},{24,16},{28,20},{1,9},{5... | collective-permute-start | bytes 393224 | tf_op jit(solution)/shard_map/ppermute | solution.py:150
  5.3 0.7 %copy-start.5 = (s32[1,1,4,3]{2,1,3,0:T(1,128)S(1)}, s32[1,1,4,3]{2,1,3,0:T(1,128)}, u32[]{:S(2)}) copy-start(s32[1,1,4,3]{2,1,3,0:T(1,128)} %param.9) | copy-start | bytes 148
  6.6 0.7 %copy-start.3 = (s32[1,1,4]{2,1,0:T(1,128)S(1)}, s32[1,1,4]{2,1,0:T(1,128)}, u32[]{:S(2)}) copy-start(s32[1,1,4]{2,1,0:T(1,128)} %param.10) | copy-start | bytes 52
  8.8 0.9 %copy-start.4 = (bf16[128,512]{1,0:T(8,128)(2,1)S(1)}, bf16[128,512]{1,0:T(8,128)(2,1)}, u32[]{:S(2)}) copy-start(bf16[128,512]{1,0:T(8,128)(2,1)} %param.6) | copy-start | bytes 393220
  11.4 2.0 %collective-permute-start.3 = (bf16[512,512]{1,0:T(8,128)(2,1)S(1)}, bf16[512,512]{1,0:T(8,128)(2,1)S(1)}, u32[]{:S(2)}, u32[]{:S(2)}) collective-permute-start(bf16[512,512]{1,0:T(8,128)(2,1)S(1)} %constant_dynamic-update-slice_fusion), channel_id=1, source_target_pairs={{0,4},{4,0},{8,12},{12,8},{16,20},{20,16},{24,28},{28,24},{1,5},{5... | collective-permute-start | bytes 1572872 | tf_op jit(solution)/shard_map/ppermute | solution.py:150
  13.6 10.7 %collective-permute-start.6 = (bf16[128,512]{1,0:T(8,128)(2,1)S(1)}, bf16[128,512]{1,0:T(8,128)(2,1)S(1)}, u32[]{:S(2)}, u32[]{:S(2)}) collective-permute-start(bf16[128,512]{1,0:T(8,128)(2,1)S(1)} %fusion.3), channel_id=1, source_target_pairs={{0,2},{1,3},{2,0},{3,1},{4,6},{5,7},{6,4},{7,5},{8,10},{9,11},{10,... | collective-permute-start | bytes 393224 | tf_op jit(solution)/shard_map/ppermute | solution.py:153
  16.5 7.8 %collective-permute-start.5 = (bf16[128,512]{1,0:T(8,128)(2,1)S(1)}, bf16[128,512]{1,0:T(8,128)(2,1)S(1)}, u32[]{:S(2)}, u32[]{:S(2)}) collective-permute-start(bf16[128,512]{1,0:T(8,128)(2,1)S(1)} %fusion.4), channel_id=1, source_target_pairs={{0,1},{1,0},{2,3},{3,2},{4,5},{5,4},{6,7},{7,6},{8,9},{9,8},{10,11... | collective-permute-start | bytes 393224 | tf_op jit(solution)/shard_map/ppermute | solution.py:153
  18.4 8.5 %collective-permute-start.4 = (bf16[128,512]{1,0:T(8,128)(2,1)S(1)}, bf16[128,512]{1,0:T(8,128)(2,1)S(1)}, u32[]{:S(2)}, u32[]{:S(2)}) collective-permute-start(bf16[128,512]{1,0:T(8,128)(2,1)S(1)} %fusion.5), channel_id=1, source_target_pairs={{0,3},{1,2},{2,1},{3,0},{4,7},{5,6},{6,5},{7,4},{8,11},{9,10},{10,... | collective-permute-start | bytes 393224 | tf_op jit(solution)/shard_map/ppermute | solution.py:153
  18.6 8.2 %copy-start.1 = (bf16[512,512]{1,0:T(8,128)(2,1)S(1)}, bf16[512,512]{1,0:T(8,128)(2,1)}, u32[]{:S(2)}) copy-start(bf16[512,512]{1,0:T(8,128)(2,1)} %refs_4_.1) | copy-start | bytes 1572868
  18.6 8.2 %copy-start.2 = (bf16[128,512]{1,0:T(8,128)(2,1)S(1)}, bf16[128,512]{1,0:T(8,128)(2,1)}, u32[]{:S(2)}) copy-start(bf16[128,512]{1,0:T(8,128)(2,1)} %refs_5_.1) | copy-start | bytes 393220
  27.4 1.6 %collective-permute-start.7 = (bf16[256,512]{1,0:T(8,128)(2,1)S(1)}, bf16[256,512]{1,0:T(8,128)(2,1)S(1)}, u32[]{:S(2)}, u32[]{:S(2)}) collective-permute-start(bf16[256,512]{1,0:T(8,128)(2,1)S(1)} %get-tuple-element.13), channel_id=1, source_target_pairs={{0,4},{4,0},{8,12},{12,8},{16,20},{20,16},{24,28},{28,24},{1,5},{5... | collective-permute-start | bytes 786440 | tf_op jit(solution)/shard_map/ppermute | solution.py:150
  29.1 5.2 %collective-permute-start.10 = (bf16[64,512]{1,0:T(8,128)(2,1)S(1)}, bf16[64,512]{1,0:T(8,128)(2,1)S(1)}, u32[]{:S(2)}, u32[]{:S(2)}) collective-permute-start(bf16[64,512]{1,0:T(8,128)(2,1)S(1)} %get-tuple-element.15), channel_id=1, source_target_pairs={{0,24},{4,28},{8,16},{12,20},{16,8},{20,12},{24,0},{28,4},{1,25},{... | collective-permute-start | bytes 196616 | tf_op jit(solution)/shard_map/ppermute | solution.py:150
  30.9 4.4 %collective-permute-start.8 = (bf16[64,512]{1,0:T(8,128)(2,1)S(1)}, bf16[64,512]{1,0:T(8,128)(2,1)S(1)}, u32[]{:S(2)}, u32[]{:S(2)}) collective-permute-start(bf16[64,512]{1,0:T(8,128)(2,1)S(1)} %get-tuple-element.14), channel_id=1, source_target_pairs={{0,12},{4,8},{8,4},{12,0},{16,28},{20,24},{24,20},{28,16},{1,13},{... | collective-permute-start | bytes 196616 | tf_op jit(solution)/shard_map/ppermute | solution.py:150
  31.6 3.7 %collective-permute-start.9 = (bf16[64,512]{1,0:T(8,128)(2,1)S(1)}, bf16[64,512]{1,0:T(8,128)(2,1)S(1)}, u32[]{:S(2)}, u32[]{:S(2)}) collective-permute-start(bf16[64,512]{1,0:T(8,128)(2,1)S(1)} %get-tuple-element.16), channel_id=1, source_target_pairs={{0,20},{4,16},{8,28},{12,24},{16,4},{20,0},{24,12},{28,8},{1,21},{... | collective-permute-start | bytes 196616 | tf_op jit(solution)/shard_map/ppermute | solution.py:150
  35.3 6.6 %collective-permute-start.11 = (bf16[64,512]{1,0:T(8,128)(2,1)S(1)}, bf16[64,512]{1,0:T(8,128)(2,1)S(1)}, u32[]{:S(2)}, u32[]{:S(2)}) collective-permute-start(bf16[64,512]{1,0:T(8,128)(2,1)S(1)} %fusion.29), channel_id=1, source_target_pairs={{0,3},{1,2},{2,1},{3,0},{4,7},{5,6},{6,5},{7,4},{8,11},{9,10},{10,... | collective-permute-start | bytes 196616 | tf_op jit(solution)/shard_map/ppermute | solution.py:153
  37.9 8.2 %collective-permute-start.12 = (bf16[64,512]{1,0:T(8,128)(2,1)S(1)}, bf16[64,512]{1,0:T(8,128)(2,1)S(1)}, u32[]{:S(2)}, u32[]{:S(2)}) collective-permute-start(bf16[64,512]{1,0:T(8,128)(2,1)S(1)} %fusion.29), channel_id=1, source_target_pairs={{0,2},{1,3},{2,0},{3,1},{4,6},{5,7},{6,4},{7,5},{8,10},{9,11},{10,... | collective-permute-start | bytes 196616 | tf_op jit(solution)/shard_map/ppermute | solution.py:153
  39.7 6.3 %collective-permute-start.13 = (bf16[64,512]{1,0:T(8,128)(2,1)S(1)}, bf16[64,512]{1,0:T(8,128)(2,1)S(1)}, u32[]{:S(2)}, u32[]{:S(2)}) collective-permute-start(bf16[64,512]{1,0:T(8,128)(2,1)S(1)} %fusion.29), channel_id=1, source_target_pairs={{0,1},{1,0},{2,3},{3,2},{4,5},{5,4},{6,7},{7,6},{8,9},{9,8},{10,11... | collective-permute-start | bytes 196616 | tf_op jit(solution)/shard_map/ppermute | solution.py:153
  46.1 5.3 %collective-permute-start.14 = (bf16[64,512]{1,0:T(8,128)(2,1)S(1)}, bf16[64,512]{1,0:T(8,128)(2,1)S(1)}, u32[]{:S(2)}, u32[]{:S(2)}) collective-permute-start(bf16[64,512]{1,0:T(8,128)(2,1)S(1)} %add_convert_fusion), channel_id=1, source_target_pairs={{0,24},{4,28},{8,16},{12,20},{16,8},{20,12},{24,0},{28,4},{1,25},{... | collective-permute-start | bytes 196616 | tf_op jit(solution)/shard_map/ppermute | solution.py:150
  47.7 5.1 %collective-permute-start.15 = (bf16[64,512]{1,0:T(8,128)(2,1)S(1)}, bf16[64,512]{1,0:T(8,128)(2,1)S(1)}, u32[]{:S(2)}, u32[]{:S(2)}) collective-permute-start(bf16[64,512]{1,0:T(8,128)(2,1)S(1)} %add_convert_fusion), channel_id=1, source_target_pairs={{0,20},{4,16},{8,28},{12,24},{16,4},{20,0},{24,12},{28,8},{1,21},{... | collective-permute-start | bytes 196616 | tf_op jit(solution)/shard_map/ppermute | solution.py:150
  48.2 4.6 %collective-permute-start.16 = (bf16[64,512]{1,0:T(8,128)(2,1)S(1)}, bf16[64,512]{1,0:T(8,128)(2,1)S(1)}, u32[]{:S(2)}, u32[]{:S(2)}) collective-permute-start(bf16[64,512]{1,0:T(8,128)(2,1)S(1)} %add_convert_fusion), channel_id=1, source_target_pairs={{0,12},{4,8},{8,4},{12,0},{16,28},{20,24},{24,20},{28,16},{1,13},{... | collective-permute-start | bytes 196616 | tf_op jit(solution)/shard_map/ppermute | solution.py:150
  52.8 1.6 %collective-permute-start.17 = (bf16[256,512]{1,0:T(8,128)(2,1)S(1)}, bf16[256,512]{1,0:T(8,128)(2,1)S(1)}, u32[]{:S(2)}, u32[]{:S(2)}) collective-permute-start(bf16[256,512]{1,0:T(8,128)(2,1)S(1)} %bitcast.88), channel_id=1, source_target_pairs={{0,4},{4,0},{8,12},{12,8},{16,20},{20,16},{24,28},{28,24},{1,5},{5... | collective-permute-start | bytes 786440 | tf_op jit(solution)/shard_map/ppermute | solution.py:150

commit v4 on v3

--- a/solution.py
+++ b/solution.py
@@ -11,6 +11,47 @@
 VMEM = pl.BlockSpec(memory_space=pltpu.VMEM)
 SMEM = pl.BlockSpec(memory_space=pltpu.SMEM)
 HBM = pl.BlockSpec(memory_space=pltpu.HBM)
+
+
+def place_kernel(groups, ids_ref, col_ref, count_ref, tiles_ref, *out_refs):
+    row_blocks, slots, block = tiles_ref.shape[2:5]
+    rows = groups[-1][1] * 2
+    chips = rows // 2
+    for out_ref in out_refs:
+        out_ref[...] = jnp.zeros_like(out_ref)
+    for q in range(row_blocks):
+        a = q ^ ids_ref[1]
+        for k in range(slots):
+            position = (col_ref[0, 0, a, k] ^ ids_ref[0]) & (rows - 1)
+            slot = (chips - position // 2) % chips
+            live = k < count_ref[0, 0, a]
+            for (parity, last, first), out_ref in zip(groups, out_refs):
+                here = (position % 2 == parity) & (slot >= first) & (slot < last)
+
+                @pl.when(live & here)
+                def _(out_ref=out_ref, first=first, q=q, k=k, a=a, slot=slot):
+                    start = pl.multiple_of((slot - first) * block, block)
+                    out_ref[pl.ds(q * block, block), pl.ds(start, block)] = tiles_ref[0, 0, a, k]
+
+
+def placed(ids, tile_col, tile_count, edge_tiles, chips):
+    row_blocks, _, block = edge_tiles.shape[2:5]
+    early = chips // 2
+    groups = ((0, early, 0), (1, early, 0), (0, chips, early), (1, chips, early))
+    held = 4 * edge_tiles.size + 8 * row_blocks * chips * block * block
+    return pl.pallas_call(
+        functools.partial(place_kernel, groups),
+        out_shape=tuple(
+            jax.ShapeDtypeStruct((row_blocks * block, (last - first) * block), jnp.bfloat16)
+            for _, last, first in groups
+        ),
+        in_specs=[SMEM] * 3 + [VMEM],
+        out_specs=(VMEM,) * 4,
+        compiler_params=pltpu.CompilerParams(vmem_limit_bytes=max(LIMIT, held)),
+        cost_estimate=pl.CostEstimate(
+            flops=edge_tiles.size, bytes_accessed=6 * edge_tiles.size, transcendentals=0
+        ),
+    )(ids, tile_col, tile_count, edge_tiles)
 
 
 def columns_of(ref, half, size):
@@ -152,72 +193,74 @@
     def over_col(value, bits):
         return lax.ppermute(value, "col", [(i, i ^ bits) for i in range(cols)])
 
-    masks = [2 * k + bin(k).count("1") % 2 for k in range(chips)]
+    def by_core(value, bits, flip):
+        pairs = []
+        for i in range(rows):
+            for j in range(cols):
+                if i % 2 == flip:
+                    target = (i ^ (2 * bits)) * cols + j
+                else:
+                    target = i * cols + (j ^ bits)
+                pairs.append((i * cols + j, target))
+        return lax.ppermute(value, ("row", "col"), pairs)
 
     def local(features, weight, edge_tiles, tile_col, tile_count, cotangent):
         block, width = features.shape
-        row_blocks, slots = edge_tiles.shape[2:4]
         my_row = lax.axis_index("row")
         my_col = lax.axis_index("col")
         chip = my_row // 2
 
         far = [over_row(features, 2 * k) for k in range(chips - 1, 0, -1)]
-        even = jnp.concatenate([features] + far)
-        odd = over_row(even, 1)
-
-        order = jnp.arange(row_blocks) ^ my_col
-        tiles = edge_tiles[0, 0][order]
-        counts = tile_count[0, 0][order]
-        position = tile_col[0, 0][order] ^ my_row
-        live = jnp.arange(slots)[None, :] < counts[:, None]
-        position = jnp.where(live, position, rows)
-
-        def dense(parity):
-            places = 2 * (-jnp.arange(chips) % chips) + parity
-            pick = position[:, :, None] == places[None, None, :]
-            out = jnp.zeros((row_blocks, block, chips, block), jnp.bfloat16)
-            for slot in range(slots):
-                out = jnp.where(
-                    pick[:, slot, None, :, None], tiles[:, slot, :, None, :], out
-                )
-            return out.reshape(row_blocks, block, chips * block)
-
-        near_part = jnp.dot(
-            dense(0).reshape(row_blocks * block, chips * block),
-            even,
-            preferred_element_type=jnp.float32,
-        ).reshape(row_blocks, block, width)
-        adjacency = dense(1)
+        early = chips // 2
+        even_a = jnp.concatenate([features] + far[: early - 1])
+        odd_a = over_row(even_a, 1)
+        even_b = jnp.concatenate(far[early - 1 :])
+        odd_b = over_row(even_b, 1)
+
+        ids = jnp.stack([my_row, my_col]).astype(jnp.int32)
+        left = placed(ids, tile_col, tile_count, edge_tiles, chips)
+
+        def product(one, other):
+            return jnp.dot(one, other, preferred_element_type=jnp.float32)
+
+        near_part = product(left[0], even_a) + product(left[1], odd_a) + product(left[2], even_b)
 
         def term(k):
-            part = jnp.dot(adjacency[k], odd, preferred_element_type=jnp.float32)
-            return (near_part[k] + part).astype(jnp.bfloat16)
+            at = slice(k * block, (k + 1) * block)
+            return (near_part[at] + product(left[3][at], odd_b)).astype(jnp.bfloat16)
 
         turns = sorted(range(1, cols), key=lambda k: (k != cols - 1, k))
         got = [over_col(term(k), k) for k in turns]
 
-        half = (my_row + sum((chip >> i) for i in range(chips.bit_length()))) % 2
-        half = half.astype(jnp.int32)
+        half = (my_row % 2).astype(jnp.int32)
         activations, sent, kept = dense_part(half[None], [term(0)] + got, weight, cotangent)
 
         size, hidden = sent.shape
         kept = kept + over_row(sent, 1).astype(jnp.float32)
+        if chips == cols:
+            place = jnp.where(my_row % 2 == 0, chip, my_col)
+            first = lambda value, k: by_core(value, k, 0)
+            second = lambda value, k: by_core(value, k, 1)
+        else:
+            place = chip
+            first = lambda value, k: over_row(value, 2 * k)
+            second = over_col
         piece = size // chips
         kept = kept.reshape(chips, piece, hidden)
-        mine = lax.dynamic_index_in_dim(kept, chip, 0, keepdims=False)
+        mine = lax.dynamic_index_in_dim(kept, place, 0, keepdims=False)
         for k in range(1, chips):
-            other = lax.dynamic_index_in_dim(kept, chip ^ k, 0, keepdims=False)
-            mine = mine + over_row(other.astype(jnp.bfloat16), masks[k]).astype(jnp.float32)
+            other = lax.dynamic_index_in_dim(kept, place ^ k, 0, keepdims=False)
+            mine = mine + first(other.astype(jnp.bfloat16), k).astype(jnp.float32)
         mine = mine.astype(jnp.bfloat16)
-        parts = [over_col(mine, k) for k in range(cols - 1, 0, -1)] + [mine]
+        parts = [second(mine, k) for k in range(cols - 1, 0, -1)] + [mine]
         parts = [part.astype(jnp.float32) for part in parts]
         while len(parts) > 1:
             parts = [parts[i] + parts[i + 1] for i in range(0, len(parts), 2)]
         mine = parts[0].astype(jnp.bfloat16)
         kept = jnp.zeros((chips, piece, hidden), jnp.bfloat16)
         for k in range(chips - 1, 0, -1):
-            kept = lax.dynamic_update_index_in_dim(kept, over_row(mine, masks[k]), chip ^ k, 0)
-        kept = lax.dynamic_update_index_in_dim(kept, mine, chip, 0)
+            kept = lax.dynamic_update_index_in_dim(kept, first(mine, k), place ^ k, 0)
+        kept = lax.dynamic_update_index_in_dim(kept, mine, place, 0)
         kept = kept.reshape(size, hidden)
         other = over_row(kept, 1)
         weight_grad = write_first(half[None], kept)

time: 55.4 us -> 53.9 us (0.973)
  waiting for transfers between devices: 23.3 us -> 21.9 us
  local copies, waits for them, and re-layouts: 4.54 us -> 3.33 us
  Pallas kernels: 3.03 us -> 4.23 us
  other arithmetic: 1.14 us -> 0.22 us
    ppermute x0 -> x9, starting transfers between devices: none -> 12 us  [by_core(): return lax.ppermute(value, ('row', 'col'), pairs)]
    ppermute x0 -> x9, waiting for transfers between devices: none -> 10.4 us  [by_core(): return lax.ppermute(value, ('row', 'col'), pairs)]
    ppermute x12 -> x7, starting transfers between devices: 11.5 us -> 4.89 us  [over_row(): return lax.ppermute(value, 'row', [(i, i ^ bits) for i in range(rows)])]
    ppermute x12 -> x7, waiting for transfers between devices: 9.46 us -> 3.38 us  [over_row(): return lax.ppermute(value, 'row', [(i, i ^ bits) for i in range(rows)])]
    ppermute x6 -> x3, waiting for transfers between devices: 13.8 us -> 8.1 us  [over_col(): return lax.ppermute(value, 'col', [(i, i ^ bits) for i in range(cols)])]
    ppermute x6 -> x3, starting transfers between devices: 9.47 us -> 4.58 us  [over_col(): return lax.ppermute(value, 'col', [(i, i ^ bits) for i in range(cols)])]
    gather x3 -> x0, local copies, waits for them, and re-layouts: 1.82 us -> none  [the longest x1 0.64 us: local(): counts = tile_count[0, 0][order]]
    pallas_call x0 -> x1, Pallas kernels: none -> 1.21 us  [placed(): pl.pallas_call(functools.partial(place_kernel, groups), out_shape=tuple((...]
  transfers between devices with their start and end apart: 18 -> 19, of which waited for: 13 -> 16; matrix products, arithmetic and copies ran while one was open for 8% -> 5% of each run, Pallas kernels for 3% -> 5%
where the time goes in v4:
time: 53.9 us; the launch traced here: 53.7 us
  waiting for transfers between devices  21.9 us (41%)
  starting transfers between devices  21.4 us (40%)
  Pallas kernels  4.23 us (8%)
  local copies, waits for them, and re-layouts  3.33 us (6%)
  matrix products  1.63 us (3%)
  between operations  0.91 us (2%)
    ppermute x9, starting transfers between devices, by_core(): return lax.ppermute(value, ('row', 'col'), pairs)  12 us
    ppermute x9, waiting for transfers between devices, by_core(): return lax.ppermute(value, ('row', 'col'), pairs)  10.4 us
    ppermute x3, waiting for transfers between devices, over_col(): return lax.ppermute(value, 'col', [(i, i ^ bits) for i in range(cols)])  8.1 us
    ppermute x7, starting transfers between devices, over_row(): return lax.ppermute(value, 'row', [(i, i ^ bits) for i in range(rows)])  4.89 us
    ppermute x3, starting transfers between devices, over_col(): return lax.ppermute(value, 'col', [(i, i ^ bits) for i in range(cols)])  4.58 us
    ppermute x7, waiting for transfers between devices, over_row(): return lax.ppermute(value, 'row', [(i, i ^ bits) for i in range(rows)])  3.38 us
    unnamed x13, local copies, waits for them, and re-layouts  3.22 us
    dot_general x7, matrix products, product(): return jnp.dot(one, other, preferred_element_type=jnp.float32)  1.63 us
  transfers between devices with their start and end apart: 19, of which 16 were waited for; matrix products, arithmetic and copies ran while one was open for 5% of the time, Pallas kernels for 5%

profile of v4, /device:TPU:0, one launch (start us, length us, event | category | flops | bytes accessed | tf_op | source)
XLA Modules:
  0.0 53.7 jit_solution(5709155855347813424)
XLA Ops:
  0.6 4.0 %collective-permute-start = (bf16[128,512]{1,0:T(8,128)(2,1)}, bf16[128,512]{1,0:T(8,128)(2,1)S(1)}, u32[]{:S(2)}, u32[]{:S(2)}) collective-permute-start(bf16[128,512]{1,0:T(8,128)(2,1)} %param.6), channel_id=1, source_target_pairs={{0,24},{4,28},{8,16},{12,20},{16,8},{20,12},{24,0},{28,4},{1,25},{... | collective-permute-start | bytes 393224 | tf_op jit(solution)/shard_map/ppermute | solution.py:191
  5.2 0.9 %constant_dynamic-update-slice_fusion.1 = bf16[256,512]{1,0:T(8,128)(2,1)S(1)} fusion(bf16[128,512]{1,0:T(8,128)(2,1)} %param.6), kind=kLoop, calls=%fused_computation.35 | loop fusion | bytes 262144
  7.5 1.0 %copy-done.1 = bf16[1,1,4,3,128,128]{5,4,3,2,1,0:T(8,128)(2,1)S(1)} copy-done((bf16[1,1,4,3,128,128]{5,4,3,2,1,0:T(8,128)(2,1)S(1)}, bf16[1,1,4,3,128,128]{5,4,3,2,1,0:T(8,128)(2,1)}, u32[]{:S(2)}) %copy-start.1) | copy-done | bytes 393240
  8.5 1.2 %shard_map.77 = (bf16[512,256]{1,0:T(8,128)(2,1)S(1)}, bf16[512,256]{1,0:T(8,128)(2,1)S(1)}, bf16[512,256]{1,0:T(8,128)(2,1)S(1)}, bf16[512,256]{1,0:T(8,128)(2,1)S(1)}) custom-call(s32[2]{0:T(128)S(1)} %pad_add_fusion.ids_ref, s32[1,1,4,3]{3,2,1,0:T(4,128)S(1)} %copy.9.col_ref, s32[1,1,4]{2,1,0:T(1,128)S(1)} %copy-done.3, ...), custom_call_target="tpu_custom_call" | custom-call | flops 196608 | bytes 1179648 | tf_op jit(solution)/shard_map/pallas_call | solution.py:42
  9.9 1.2 %collective-permute-done.2 = bf16[128,512]{1,0:T(8,128)(2,1)S(1)} collective-permute-done((bf16[128,512]{1,0:T(8,128)(2,1)}, bf16[128,512]{1,0:T(8,128)(2,1)S(1)}, u32[]{:S(2)}, u32[]{:S(2)}) %collective-permute-start.2) | collective-permute-done | bytes 131104 | tf_op jit(solution)/shard_map/ppermute | solution.py:191
  13.2 2.7 %collective-permute-start.7 = (bf16[128,512]{1,0:T(8,128)(2,1)S(1)}, bf16[128,512]{1,0:T(8,128)(2,1)S(1)}, u32[]{:S(2)}, u32[]{:S(2)}) collective-permute-start(bf16[128,512]{1,0:T(8,128)(2,1)S(1)} %fusion.1), channel_id=1, source_target_pairs={{0,2},{1,3},{2,0},{3,1},{4,6},{5,7},{6,4},{7,5},{8,10},{9,11},{10,... | collective-permute-start | bytes 393224 | tf_op jit(solution)/shard_map/ppermute | solution.py:194
  16.0 1.6 %collective-permute-start.6 = (bf16[128,512]{1,0:T(8,128)(2,1)S(1)}, bf16[128,512]{1,0:T(8,128)(2,1)S(1)}, u32[]{:S(2)}, u32[]{:S(2)}) collective-permute-start(bf16[128,512]{1,0:T(8,128)(2,1)S(1)} %fusion.2), channel_id=1, source_target_pairs={{0,1},{1,0},{2,3},{3,2},{4,5},{5,4},{6,7},{7,6},{8,9},{9,8},{10,11... | collective-permute-start | bytes 393224 | tf_op jit(solution)/shard_map/ppermute | solution.py:194
  18.3 5.5 %collective-permute-done.7.refs_3_ = bf16[128,512]{1,0:T(8,128)(2,1)S(1)} collective-permute-done((bf16[128,512]{1,0:T(8,128)(2,1)S(1)}, bf16[128,512]{1,0:T(8,128)(2,1)S(1)}, u32[]{:S(2)}, u32[]{:S(2)}) %collective-permute-start.7) | collective-permute-done | bytes 131104 | tf_op jit(solution)/shard_map/ppermute | solution.py:194
  23.8 2.6 %collective-permute-done.5.refs_1_ = bf16[128,512]{1,0:T(8,128)(2,1)S(1)} collective-permute-done((bf16[128,512]{1,0:T(8,128)(2,1)S(1)}, bf16[128,512]{1,0:T(8,128)(2,1)S(1)}, u32[]{:S(2)}, u32[]{:S(2)}) %collective-permute-start.5) | collective-permute-done | bytes 131104 | tf_op jit(solution)/shard_map/ppermute | solution.py:194
  27.1 0.9 %shard_map.79 = (f32[256,512]{1,0:T(8,128)S(1)}, bf16[128,512]{1,0:T(8,128)(2,1)}) custom-call(s32[1]{0:T(128)} %bitcast.half_ref, bf16[128,512]{1,0:T(8,128)(2,1)S(1)} %get-tuple-element.16.agg_ref, bf16[128,512]{1,0:T(8,128)(2,1)S(1)} %get-tuple-element.17.pre_ref, f32[128,512]{1,0:T(8,128)S(1)} %get-tuple-element.18.preact_ref), custom_call_target="tpu_custom_call" | custom-call | flops 33554432 | bytes 262144 | tf_op jit(solution)/shard_map/pallas_call | solution.py:171
  28.7 1.6 %collective-permute-start.10 = (bf16[64,512]{1,0:T(8,128)(2,1)S(1)}, bf16[64,512]{1,0:T(8,128)(2,1)S(1)}, u32[]{:S(2)}, u32[]{:S(2)}) collective-permute-start(bf16[64,512]{1,0:T(8,128)(2,1)S(1)} %get-tuple-element.24), channel_id=1, source_target_pairs={{0,16},{1,17},{2,18},{3,19},{4,6},{5,7},{6,4},{7,5},{8,24},{9,25},... | collective-permute-start | bytes 196616 | tf_op jit(solution)/shard_map/ppermute | solution.py:205
  30.2 1.5 %collective-permute-start.11 = (bf16[64,512]{1,0:T(8,128)(2,1)S(1)}, bf16[64,512]{1,0:T(8,128)(2,1)S(1)}, u32[]{:S(2)}, u32[]{:S(2)}) collective-permute-start(bf16[64,512]{1,0:T(8,128)(2,1)S(1)} %get-tuple-element.23), channel_id=1, source_target_pairs={{0,24},{1,25},{2,26},{3,27},{4,7},{5,6},{6,5},{7,4},{8,16},{9,17},... | collective-permute-start | bytes 196616 | tf_op jit(solution)/shard_map/ppermute | solution.py:205
  32.2 0.8 %collective-permute-done.10 = bf16[64,512]{1,0:T(8,128)(2,1)S(1)} collective-permute-done((bf16[64,512]{1,0:T(8,128)(2,1)S(1)}, bf16[64,512]{1,0:T(8,128)(2,1)S(1)}, u32[]{:S(2)}, u32[]{:S(2)}) %collective-permute-start.10) | collective-permute-done | bytes 65568 | tf_op jit(solution)/shard_map/ppermute | solution.py:205
  33.0 2.4 %collective-permute-done.11 = bf16[64,512]{1,0:T(8,128)(2,1)S(1)} collective-permute-done((bf16[64,512]{1,0:T(8,128)(2,1)S(1)}, bf16[64,512]{1,0:T(8,128)(2,1)S(1)}, u32[]{:S(2)}, u32[]{:S(2)}) %collective-permute-start.11) | collective-permute-done | bytes 65568 | tf_op jit(solution)/shard_map/ppermute | solution.py:205
  36.0 2.5 %collective-permute-start.12 = (bf16[64,512]{1,0:T(8,128)(2,1)S(1)}, bf16[64,512]{1,0:T(8,128)(2,1)S(1)}, u32[]{:S(2)}, u32[]{:S(2)}) collective-permute-start(bf16[64,512]{1,0:T(8,128)(2,1)S(1)} %fusion.7), channel_id=1, source_target_pairs={{0,3},{1,2},{2,1},{3,0},{4,28},{5,29},{6,30},{7,31},{8,11},{9,10},... | collective-permute-start | bytes 196616 | tf_op jit(solution)/shard_map/ppermute | solution.py:205
  38.6 1.8 %collective-permute-start.13 = (bf16[64,512]{1,0:T(8,128)(2,1)S(1)}, bf16[64,512]{1,0:T(8,128)(2,1)S(1)}, u32[]{:S(2)}, u32[]{:S(2)}) collective-permute-start(bf16[64,512]{1,0:T(8,128)(2,1)S(1)} %fusion.7), channel_id=1, source_target_pairs={{0,2},{1,3},{2,0},{3,1},{4,20},{5,21},{6,22},{7,23},{8,10},{9,11},... | collective-permute-start | bytes 196616 | tf_op jit(solution)/shard_map/ppermute | solution.py:205
  40.9 1.3 %collective-permute-done.12 = bf16[64,512]{1,0:T(8,128)(2,1)S(1)} collective-permute-done((bf16[64,512]{1,0:T(8,128)(2,1)S(1)}, bf16[64,512]{1,0:T(8,128)(2,1)S(1)}, u32[]{:S(2)}, u32[]{:S(2)}) %collective-permute-start.12) | collective-permute-done | bytes 65568 | tf_op jit(solution)/shard_map/ppermute | solution.py:205
  42.2 1.5 %collective-permute-done.13 = bf16[64,512]{1,0:T(8,128)(2,1)S(1)} collective-permute-done((bf16[64,512]{1,0:T(8,128)(2,1)S(1)}, bf16[64,512]{1,0:T(8,128)(2,1)S(1)}, u32[]{:S(2)}, u32[]{:S(2)}) %collective-permute-start.13) | collective-permute-done | bytes 65568 | tf_op jit(solution)/shard_map/ppermute | solution.py:205
  43.7 0.9 %collective-permute-done.14 = bf16[64,512]{1,0:T(8,128)(2,1)S(1)} collective-permute-done((bf16[64,512]{1,0:T(8,128)(2,1)S(1)}, bf16[64,512]{1,0:T(8,128)(2,1)S(1)}, u32[]{:S(2)}, u32[]{:S(2)}) %collective-permute-start.14) | collective-permute-done | bytes 65568 | tf_op jit(solution)/shard_map/ppermute | solution.py:205
  44.7 1.5 %collective-permute-start.15 = (bf16[64,512]{1,0:T(8,128)(2,1)S(1)}, bf16[64,512]{1,0:T(8,128)(2,1)S(1)}, u32[]{:S(2)}, u32[]{:S(2)}) collective-permute-start(bf16[64,512]{1,0:T(8,128)(2,1)S(1)} %add_convert_fusion), channel_id=1, source_target_pairs={{0,24},{1,25},{2,26},{3,27},{4,7},{5,6},{6,5},{7,4},{8,16},{9,17},... | collective-permute-start | bytes 196616 | tf_op jit(solution)/shard_map/ppermute | solution.py:205
  46.9 1.3 %collective-permute-start.17 = (bf16[64,512]{1,0:T(8,128)(2,1)S(1)}, bf16[64,512]{1,0:T(8,128)(2,1)S(1)}, u32[]{:S(2)}, u32[]{:S(2)}) collective-permute-start(bf16[64,512]{1,0:T(8,128)(2,1)S(1)} %add_convert_fusion), channel_id=1, source_target_pairs={{0,8},{1,9},{2,10},{3,11},{4,5},{5,4},{6,7},{7,6},{8,0},{9,1},{10,... | collective-permute-start | bytes 196616 | tf_op jit(solution)/shard_map/ppermute | solution.py:205
  48.3 1.7 %collective-permute-done.15 = bf16[64,512]{1,0:T(8,128)(2,1)S(1)} collective-permute-done((bf16[64,512]{1,0:T(8,128)(2,1)S(1)}, bf16[64,512]{1,0:T(8,128)(2,1)S(1)}, u32[]{:S(2)}, u32[]{:S(2)}) %collective-permute-start.15) | collective-permute-done | bytes 65568 | tf_op jit(solution)/shard_map/ppermute | solution.py:205
  51.3 0.8 %shard_map.80._ = f32[2,256,512]{2,1,0:T(8,128)} custom-call(s32[1]{0:T(128)} %bitcast.half_ref, bf16[256,512]{1,0:T(8,128)(2,1)S(1)} %bitcast.39), custom_call_target="tpu_custom_call" | custom-call | flops 131072 | bytes 786432 | tf_op jit(solution)/shard_map/pallas_call | solution.py:119
  52.8 0.8 %shard_map.81 = f32[2,256,512]{2,1,0:T(8,128)} custom-call(s32[1]{0:T(128)} %bitcast.half_ref, bf16[256,512]{1,0:T(8,128)(2,1)S(1)} %collective-permute-done.18.other_ref, f32[2,256,512]{2,1,0:T(8,128)} %shard_map.80._), custom_call_target="tpu_custom_call", output_to_operand_aliasing={{}: (2, {})} | custom-call | flops 131072 | bytes 786432 | tf_op jit(solution)/shard_map/pallas_call | solution.py:135
  (51 shorter events, 10.6 us)
Async XLA Ops:
  0.6 9.1 %collective-permute-start = (bf16[128,512]{1,0:T(8,128)(2,1)}, bf16[128,512]{1,0:T(8,128)(2,1)S(1)}, u32[]{:S(2)}, u32[]{:S(2)}) collective-permute-start(bf16[128,512]{1,0:T(8,128)(2,1)} %param.6), channel_id=1, source_target_pairs={{0,24},{4,28},{8,16},{12,20},{16,8},{20,12},{24,0},{28,4},{1,25},{... | collective-permute-start | bytes 393224 | tf_op jit(solution)/shard_map/ppermute | solution.py:191
  4.6 6.5 %collective-permute-start.2 = (bf16[128,512]{1,0:T(8,128)(2,1)}, bf16[128,512]{1,0:T(8,128)(2,1)S(1)}, u32[]{:S(2)}, u32[]{:S(2)}) collective-permute-start(bf16[128,512]{1,0:T(8,128)(2,1)} %param.6), channel_id=1, source_target_pairs={{0,16},{4,20},{8,24},{12,28},{16,0},{20,4},{24,8},{28,12},{1,17},{... | collective-permute-start | bytes 393224 | tf_op jit(solution)/shard_map/ppermute | solution.py:191
  5.1 6.3 %collective-permute-start.3 = (bf16[128,512]{1,0:T(8,128)(2,1)}, bf16[128,512]{1,0:T(8,128)(2,1)S(1)}, u32[]{:S(2)}, u32[]{:S(2)}) collective-permute-start(bf16[128,512]{1,0:T(8,128)(2,1)} %param.6), channel_id=1, source_target_pairs={{0,8},{4,12},{8,0},{12,4},{16,24},{20,28},{24,16},{28,20},{1,9},{5... | collective-permute-start | bytes 393224 | tf_op jit(solution)/shard_map/ppermute | solution.py:191
  6.2 0.7 %copy-start.4 = (s32[1,1,4,3]{2,1,3,0:T(1,128)S(1)}, s32[1,1,4,3]{2,1,3,0:T(1,128)}, u32[]{:S(2)}) copy-start(s32[1,1,4,3]{2,1,3,0:T(1,128)} %param.9) | copy-start | bytes 148
  6.9 0.7 %copy-start.3 = (s32[1,1,4]{2,1,0:T(1,128)S(1)}, s32[1,1,4]{2,1,0:T(1,128)}, u32[]{:S(2)}) copy-start(s32[1,1,4]{2,1,0:T(1,128)} %count_ref.1) | copy-start | bytes 52
  7.5 1.0 %copy-start.1 = (bf16[1,1,4,3,128,128]{5,4,3,2,1,0:T(8,128)(2,1)S(1)}, bf16[1,1,4,3,128,128]{5,4,3,2,1,0:T(8,128)(2,1)}, u32[]{:S(2)}) copy-start(bf16[1,1,4,3,128,128]{5,4,3,2,1,0:T(8,128)(2,1)} %tiles_ref.1) | copy-start | bytes 1179652
  9.8 2.0 %collective-permute-start.1 = (bf16[256,512]{1,0:T(8,128)(2,1)S(1)}, bf16[256,512]{1,0:T(8,128)(2,1)S(1)}, u32[]{:S(2)}, u32[]{:S(2)}) collective-permute-start(bf16[256,512]{1,0:T(8,128)(2,1)S(1)} %constant_dynamic-update-slice_fusion), channel_id=1, source_target_pairs={{0,4},{4,0},{8,12},{12,8},{16,20},{20,16},{24,28},{28,24},{1,5},{5... | collective-permute-start | bytes 786440 | tf_op jit(solution)/shard_map/ppermute | solution.py:191
  11.4 1.6 %collective-permute-start.4 = (bf16[256,512]{1,0:T(8,128)(2,1)S(1)}, bf16[256,512]{1,0:T(8,128)(2,1)S(1)}, u32[]{:S(2)}, u32[]{:S(2)}) collective-permute-start(bf16[256,512]{1,0:T(8,128)(2,1)S(1)} %constant_dynamic-update-slice_fusion.2), channel_id=1, source_target_pairs={{0,4},{4,0},{8,12},{12,8},{16,20},{20,16},{24,28},{28,24},{1,5},{5... | collective-permute-start | bytes 786440 | tf_op jit(solution)/shard_map/ppermute | solution.py:191
  13.2 10.7 %collective-permute-start.7 = (bf16[128,512]{1,0:T(8,128)(2,1)S(1)}, bf16[128,512]{1,0:T(8,128)(2,1)S(1)}, u32[]{:S(2)}, u32[]{:S(2)}) collective-permute-start(bf16[128,512]{1,0:T(8,128)(2,1)S(1)} %fusion.1), channel_id=1, source_target_pairs={{0,2},{1,3},{2,0},{3,1},{4,6},{5,7},{6,4},{7,5},{8,10},{9,11},{10,... | collective-permute-start | bytes 393224 | tf_op jit(solution)/shard_map/ppermute | solution.py:194
  16.0 7.8 %collective-permute-start.6 = (bf16[128,512]{1,0:T(8,128)(2,1)S(1)}, bf16[128,512]{1,0:T(8,128)(2,1)S(1)}, u32[]{:S(2)}, u32[]{:S(2)}) collective-permute-start(bf16[128,512]{1,0:T(8,128)(2,1)S(1)} %fusion.2), channel_id=1, source_target_pairs={{0,1},{1,0},{2,3},{3,2},{4,5},{5,4},{6,7},{7,6},{8,9},{9,8},{10,11... | collective-permute-start | bytes 393224 | tf_op jit(solution)/shard_map/ppermute | solution.py:194
  17.8 8.6 %copy-start = (bf16[512,512]{1,0:T(8,128)(2,1)S(1)}, bf16[512,512]{1,0:T(8,128)(2,1)}, u32[]{:S(2)}) copy-start(bf16[512,512]{1,0:T(8,128)(2,1)} %refs_4_.1) | copy-start | bytes 1572868
  17.9 8.6 %copy-start.2 = (bf16[128,512]{1,0:T(8,128)(2,1)S(1)}, bf16[128,512]{1,0:T(8,128)(2,1)}, u32[]{:S(2)}) copy-start(bf16[128,512]{1,0:T(8,128)(2,1)} %refs_5_.1) | copy-start | bytes 393220
  17.9 8.6 %collective-permute-start.5 = (bf16[128,512]{1,0:T(8,128)(2,1)S(1)}, bf16[128,512]{1,0:T(8,128)(2,1)S(1)}, u32[]{:S(2)}, u32[]{:S(2)}) collective-permute-start(bf16[128,512]{1,0:T(8,128)(2,1)S(1)} %fusion.3), channel_id=1, source_target_pairs={{0,3},{1,2},{2,1},{3,0},{4,7},{5,6},{6,5},{7,4},{8,11},{9,10},{10,... | collective-permute-start | bytes 393224 | tf_op jit(solution)/shard_map/ppermute | solution.py:194
  26.9 1.6 %collective-permute-start.8 = (bf16[256,512]{1,0:T(8,128)(2,1)S(1)}, bf16[256,512]{1,0:T(8,128)(2,1)S(1)}, u32[]{:S(2)}, u32[]{:S(2)}) collective-permute-start(bf16[256,512]{1,0:T(8,128)(2,1)S(1)} %get-tuple-element.21), channel_id=1, source_target_pairs={{0,4},{4,0},{8,12},{12,8},{16,20},{20,16},{24,28},{28,24},{1,5},{5... | collective-permute-start | bytes 786440 | tf_op jit(solution)/shard_map/ppermute | solution.py:191
  28.7 4.3 %collective-permute-start.10 = (bf16[64,512]{1,0:T(8,128)(2,1)S(1)}, bf16[64,512]{1,0:T(8,128)(2,1)S(1)}, u32[]{:S(2)}, u32[]{:S(2)}) collective-permute-start(bf16[64,512]{1,0:T(8,128)(2,1)S(1)} %get-tuple-element.24), channel_id=1, source_target_pairs={{0,16},{1,17},{2,18},{3,19},{4,6},{5,7},{6,4},{7,5},{8,24},{9,25},... | collective-permute-start | bytes 196616 | tf_op jit(solution)/shard_map/ppermute | solution.py:205
  30.2 5.2 %collective-permute-start.11 = (bf16[64,512]{1,0:T(8,128)(2,1)S(1)}, bf16[64,512]{1,0:T(8,128)(2,1)S(1)}, u32[]{:S(2)}, u32[]{:S(2)}) collective-permute-start(bf16[64,512]{1,0:T(8,128)(2,1)S(1)} %get-tuple-element.23), channel_id=1, source_target_pairs={{0,24},{1,25},{2,26},{3,27},{4,7},{5,6},{6,5},{7,4},{8,16},{9,17},... | collective-permute-start | bytes 196616 | tf_op jit(solution)/shard_map/ppermute | solution.py:205
  31.7 4.3 %collective-permute-start.9 = (bf16[64,512]{1,0:T(8,128)(2,1)S(1)}, bf16[64,512]{1,0:T(8,128)(2,1)S(1)}, u32[]{:S(2)}, u32[]{:S(2)}) collective-permute-start(bf16[64,512]{1,0:T(8,128)(2,1)S(1)} %get-tuple-element.22), channel_id=1, source_target_pairs={{0,8},{1,9},{2,10},{3,11},{4,5},{5,4},{6,7},{7,6},{8,0},{9,1},{10,... | collective-permute-start | bytes 196616 | tf_op jit(solution)/shard_map/ppermute | solution.py:205
  36.0 6.2 %collective-permute-start.12 = (bf16[64,512]{1,0:T(8,128)(2,1)S(1)}, bf16[64,512]{1,0:T(8,128)(2,1)S(1)}, u32[]{:S(2)}, u32[]{:S(2)}) collective-permute-start(bf16[64,512]{1,0:T(8,128)(2,1)S(1)} %fusion.7), channel_id=1, source_target_pairs={{0,3},{1,2},{2,1},{3,0},{4,28},{5,29},{6,30},{7,31},{8,11},{9,10},... | collective-permute-start | bytes 196616 | tf_op jit(solution)/shard_map/ppermute | solution.py:205
  38.6 5.2 %collective-permute-start.13 = (bf16[64,512]{1,0:T(8,128)(2,1)S(1)}, bf16[64,512]{1,0:T(8,128)(2,1)S(1)}, u32[]{:S(2)}, u32[]{:S(2)}) collective-permute-start(bf16[64,512]{1,0:T(8,128)(2,1)S(1)} %fusion.7), channel_id=1, source_target_pairs={{0,2},{1,3},{2,0},{3,1},{4,20},{5,21},{6,22},{7,23},{8,10},{9,11},... | collective-permute-start | bytes 196616 | tf_op jit(solution)/shard_map/ppermute | solution.py:205
  40.4 4.3 %collective-permute-start.14 = (bf16[64,512]{1,0:T(8,128)(2,1)S(1)}, bf16[64,512]{1,0:T(8,128)(2,1)S(1)}, u32[]{:S(2)}, u32[]{:S(2)}) collective-permute-start(bf16[64,512]{1,0:T(8,128)(2,1)S(1)} %fusion.7), channel_id=1, source_target_pairs={{0,1},{1,0},{2,3},{3,2},{4,12},{5,13},{6,14},{7,15},{8,9},{9,8},{1... | collective-permute-start | bytes 196616 | tf_op jit(solution)/shard_map/ppermute | solution.py:205
  44.7 5.2 %collective-permute-start.15 = (bf16[64,512]{1,0:T(8,128)(2,1)S(1)}, bf16[64,512]{1,0:T(8,128)(2,1)S(1)}, u32[]{:S(2)}, u32[]{:S(2)}) collective-permute-start(bf16[64,512]{1,0:T(8,128)(2,1)S(1)} %add_convert_fusion), channel_id=1, source_target_pairs={{0,24},{1,25},{2,26},{3,27},{4,7},{5,6},{6,5},{7,4},{8,16},{9,17},... | collective-permute-start | bytes 196616 | tf_op jit(solution)/shard_map/ppermute | solution.py:205
  46.2 4.4 %collective-permute-start.16 = (bf16[64,512]{1,0:T(8,128)(2,1)S(1)}, bf16[64,512]{1,0:T(8,128)(2,1)S(1)}, u32[]{:S(2)}, u32[]{:S(2)}) collective-permute-start(bf16[64,512]{1,0:T(8,128)(2,1)S(1)} %add_convert_fusion), channel_id=1, source_target_pairs={{0,16},{1,17},{2,18},{3,19},{4,6},{5,7},{6,4},{7,5},{8,24},{9,25},... | collective-permute-start | bytes 196616 | tf_op jit(solution)/shard_map/ppermute | solution.py:205
  46.9 4.3 %collective-permute-start.17 = (bf16[64,512]{1,0:T(8,128)(2,1)S(1)}, bf16[64,512]{1,0:T(8,128)(2,1)S(1)}, u32[]{:S(2)}, u32[]{:S(2)}) collective-permute-start(bf16[64,512]{1,0:T(8,128)(2,1)S(1)} %add_convert_fusion), channel_id=1, source_target_pairs={{0,8},{1,9},{2,10},{3,11},{4,5},{5,4},{6,7},{7,6},{8,0},{9,1},{10,... | collective-permute-start | bytes 196616 | tf_op jit(solution)/shard_map/ppermute | solution.py:205
  51.2 1.6 %collective-permute-start.18 = (bf16[256,512]{1,0:T(8,128)(2,1)S(1)}, bf16[256,512]{1,0:T(8,128)(2,1)S(1)}, u32[]{:S(2)}, u32[]{:S(2)}) collective-permute-start(bf16[256,512]{1,0:T(8,128)(2,1)S(1)} %bitcast.38), channel_id=1, source_target_pairs={{0,4},{4,0},{8,12},{12,8},{16,20},{20,16},{24,28},{28,24},{1,5},{5... | collective-permute-start | bytes 786440 | tf_op jit(solution)/shard_map/ppermute | solution.py:191

commit v5 on v4

--- a/solution.py
+++ b/solution.py
@@ -93,60 +93,42 @@
     kept_ref[...] = grad_half(agg_ref, pre_ref[...], half_ref[0], kept_ref.shape[0])
 
 
-def first_kernel(half_ref, kept_ref, out_ref, wide_ref, sem):
-    wide_ref[...] = kept_ref[...].astype(jnp.float32)
-    copy = pltpu.make_async_copy(wide_ref, out_ref.at[half_ref[0]], sem)
-    copy.start()
-    copy.wait()
-
-
-def second_kernel(half_ref, other_ref, _, out_ref, wide_ref, sems):
-    pieces, size, _ = wide_ref.shape
+def write_kernel(turns, half_ref, own_ref, other_ref, *refs):
+    sources, (out_ref, wide_ref, sems) = refs[: len(turns)], refs[-3:]
+    size = wide_ref.shape[1]
     copies = []
-    for i in range(pieces):
-        rows = pl.ds(i * size, size)
-        wide_ref[i] = other_ref[rows, :].astype(jnp.float32)
-        copies.append(
-            pltpu.make_async_copy(wide_ref.at[i], out_ref.at[1 - half_ref[0], rows], sems.at[i])
-        )
-        copies[-1].start()
+    for (flip, partners), source in zip(turns, sources):
+        half = 1 - half_ref[0] if flip else half_ref[0]
+        place = other_ref[0] if flip else own_ref[0]
+        for i, k in enumerate(partners):
+            n = len(copies)
+            wide_ref[n] = source[pl.ds(i * size, size), :].astype(jnp.float32)
+            target = out_ref.at[half, place ^ k]
+            copies.append(pltpu.make_async_copy(wide_ref.at[n], target, sems.at[n]))
+            copies[-1].start()
     for copy in copies:
         copy.wait()
 
 
-def write_first(half, kept):
-    size, hidden = kept.shape
+def write(where, turns, sources, shape, out=None):
+    size, hidden = shape[2:]
+    total = sum(len(partners) for _, partners in turns)
+    earlier = [] if out is None else [out]
     return pl.pallas_call(
-        first_kernel,
-        out_shape=jax.ShapeDtypeStruct((2, size, hidden), jnp.float32),
-        in_specs=[SMEM, VMEM],
-        out_specs=HBM,
-        scratch_shapes=[pltpu.VMEM((size, hidden), jnp.float32), pltpu.SemaphoreType.DMA],
-        compiler_params=pltpu.CompilerParams(vmem_limit_bytes=LIMIT),
-        cost_estimate=pl.CostEstimate(
-            flops=size * hidden, bytes_accessed=6 * size * hidden, transcendentals=0
-        ),
-    )(half, kept)
-
-
-def write_second(half, other, out):
-    size, hidden = other.shape
-    pieces = 4
-    return pl.pallas_call(
-        second_kernel,
-        out_shape=jax.ShapeDtypeStruct(out.shape, out.dtype),
-        in_specs=[SMEM, VMEM, HBM],
+        functools.partial(write_kernel, turns),
+        out_shape=jax.ShapeDtypeStruct(shape, jnp.float32),
+        in_specs=[SMEM] * 3 + [VMEM] * len(sources) + [HBM] * len(earlier),
         out_specs=HBM,
         scratch_shapes=[
-            pltpu.VMEM((pieces, size // pieces, hidden), jnp.float32),
-            pltpu.SemaphoreType.DMA((pieces,)),
+            pltpu.VMEM((total, size, hidden), jnp.float32),
+            pltpu.SemaphoreType.DMA((total,)),
         ],
-        input_output_aliases={2: 0},
+        input_output_aliases={3 + len(sources): 0} if earlier else {},
         compiler_params=pltpu.CompilerParams(vmem_limit_bytes=LIMIT),
         cost_estimate=pl.CostEstimate(
-            flops=size * hidden, bytes_accessed=6 * size * hidden, transcendentals=0
-        ),
-    )(half, other, out)
+            flops=total * size * hidden, bytes_accessed=6 * total * size * hidden, transcendentals=0
+        ),
+    )(*where, *sources, *earlier)
 
 
 def dense_part(half, parts, weight, cotangent):
@@ -239,10 +221,11 @@
         kept = kept + over_row(sent, 1).astype(jnp.float32)
         if chips == cols:
             place = jnp.where(my_row % 2 == 0, chip, my_col)
+            place_other = jnp.where(my_row % 2 == 0, my_col, chip)
             first = lambda value, k: by_core(value, k, 0)
             second = lambda value, k: by_core(value, k, 1)
         else:
-            place = chip
+            place = place_other = chip
             first = lambda value, k: over_row(value, 2 * k)
             second = over_col
         piece = size // chips
@@ -257,14 +240,18 @@
         while len(parts) > 1:
             parts = [parts[i] + parts[i + 1] for i in range(0, len(parts), 2)]
         mine = parts[0].astype(jnp.bfloat16)
-        kept = jnp.zeros((chips, piece, hidden), jnp.bfloat16)
-        for k in range(chips - 1, 0, -1):
-            kept = lax.dynamic_update_index_in_dim(kept, first(mine, k), place ^ k, 0)
-        kept = lax.dynamic_update_index_in_dim(kept, mine, place, 0)
-        kept = kept.reshape(size, hidden)
-        other = over_row(kept, 1)
-        weight_grad = write_first(half[None], kept)
-        weight_grad = write_second(half[None], other, weight_grad)
+        gathered = [first(mine, k) for k in range(chips - 1, 0, -1)]
+        soon = [0] + list(range(chips - 1, early, -1))
+        late = list(range(early, 0, -1))
+        kept_a = jnp.concatenate([mine] + gathered[: early - 1])
+        other_a = over_row(kept_a, 1)
+        kept_b = jnp.concatenate(gathered[early - 1 :])
+        other_b = over_row(kept_b, 1)
+        where = [value.astype(jnp.int32)[None] for value in (half, place, place_other)]
+        shape = (2, chips, piece, hidden)
+        turns = ((0, soon), (0, late), (1, soon))
+        weight_grad = write(where, turns, [kept_a, kept_b, other_a], shape)
+        weight_grad = write(where, ((1, late),), [other_b], shape, weight_grad)
         return (activations, weight_grad.reshape(width, hidden))
 
     return local

time: 53.9 us -> 53.5 us (level)
    ppermute x7 -> x8, waiting for transfers between devices: 3.38 us -> 3.09 us  [over_row(): return lax.ppermute(value, 'row', [(i, i ^ bits) for i in range(rows)])]
    unnamed x13 -> x14, local copies, waits for them, and re-layouts: 3.22 us -> 3.22 us
    ppermute x7 -> x8, starting transfers between devices: 4.89 us -> 4.89 us  [over_row(): return lax.ppermute(value, 'row', [(i, i ^ bits) for i in range(rows)])]
  transfers between devices with their start and end apart: 19 -> 20, of which waited for: 16 -> 17; matrix products, arithmetic and copies ran while one was open for 5% -> 5% of each run, Pallas kernels for 5% -> 6%
where the time goes in v5:
time: 53.5 us; the launch traced here: 53.3 us
  waiting for transfers between devices  21.6 us (40%)
  starting transfers between devices  21.4 us (40%)
  Pallas kernels  4.22 us (8%)
  local copies, waits for them, and re-layouts  3.28 us (6%)
  matrix products  1.63 us (3%)
  between operations  0.9 us (2%)
    ppermute x9, starting transfers between devices, by_core(): return lax.ppermute(value, ('row', 'col'), pairs)  12 us
    ppermute x9, waiting for transfers between devices, by_core(): return lax.ppermute(value, ('row', 'col'), pairs)  10.4 us
    ppermute x3, waiting for transfers between devices, over_col(): return lax.ppermute(value, 'col', [(i, i ^ bits) for i in range(cols)])  8.1 us
    ppermute x8, starting transfers between devices, over_row(): return lax.ppermute(value, 'row', [(i, i ^ bits) for i in range(rows)])  4.89 us
    ppermute x3, starting transfers between devices, over_col(): return lax.ppermute(value, 'col', [(i, i ^ bits) for i in range(cols)])  4.58 us
    unnamed x14, local copies, waits for them, and re-layouts  3.22 us
    ppermute x8, waiting for transfers between devices, over_row(): return lax.ppermute(value, 'row', [(i, i ^ bits) for i in range(rows)])  3.09 us
    pallas_call x2, Pallas kernels, write(): pl.pallas_call(functools.partial(write_kernel, turns), out_shape=jax.Shap...  1.65 us
  transfers between devices with their start and end apart: 20, of which 17 were waited for; matrix products, arithmetic and copies ran while one was open for 5% of the time, Pallas kernels for 6%

profile of v5, /device:TPU:0, one launch (start us, length us, event | category | flops | bytes accessed | tf_op | source)
XLA Modules:
  0.0 53.3 jit_solution(8702759419919268669)
XLA Ops:
  0.6 4.0 %collective-permute-start = (bf16[128,512]{1,0:T(8,128)(2,1)}, bf16[128,512]{1,0:T(8,128)(2,1)S(1)}, u32[]{:S(2)}, u32[]{:S(2)}) collective-permute-start(bf16[128,512]{1,0:T(8,128)(2,1)} %param.6), channel_id=1, source_target_pairs={{0,24},{4,28},{8,16},{12,20},{16,8},{20,12},{24,0},{28,4},{1,25},{... | collective-permute-start | bytes 393224 | tf_op jit(solution)/shard_map/ppermute | solution.py:173
  5.2 0.9 %constant_dynamic-update-slice_fusion.1 = bf16[256,512]{1,0:T(8,128)(2,1)S(1)} fusion(bf16[128,512]{1,0:T(8,128)(2,1)} %param.6), kind=kLoop, calls=%fused_computation.32 | loop fusion | bytes 262144
  7.5 1.0 %copy-done.1 = bf16[1,1,4,3,128,128]{5,4,3,2,1,0:T(8,128)(2,1)S(1)} copy-done((bf16[1,1,4,3,128,128]{5,4,3,2,1,0:T(8,128)(2,1)S(1)}, bf16[1,1,4,3,128,128]{5,4,3,2,1,0:T(8,128)(2,1)}, u32[]{:S(2)}) %copy-start.1) | copy-done | bytes 393240
  8.5 1.2 %shard_map.77 = (bf16[512,256]{1,0:T(8,128)(2,1)S(1)}, bf16[512,256]{1,0:T(8,128)(2,1)S(1)}, bf16[512,256]{1,0:T(8,128)(2,1)S(1)}, bf16[512,256]{1,0:T(8,128)(2,1)S(1)}) custom-call(s32[2]{0:T(128)S(1)} %pad_add_fusion.ids_ref, s32[1,1,4,3]{3,2,1,0:T(4,128)S(1)} %copy.9.col_ref, s32[1,1,4]{2,1,0:T(1,128)S(1)} %copy-done.3, ...), custom_call_target="tpu_custom_call" | custom-call | flops 196608 | bytes 1179648 | tf_op jit(solution)/shard_map/pallas_call | solution.py:42
  9.9 1.2 %collective-permute-done.2 = bf16[128,512]{1,0:T(8,128)(2,1)S(1)} collective-permute-done((bf16[128,512]{1,0:T(8,128)(2,1)}, bf16[128,512]{1,0:T(8,128)(2,1)S(1)}, u32[]{:S(2)}, u32[]{:S(2)}) %collective-permute-start.2) | collective-permute-done | bytes 131104 | tf_op jit(solution)/shard_map/ppermute | solution.py:173
  13.2 2.7 %collective-permute-start.7 = (bf16[128,512]{1,0:T(8,128)(2,1)S(1)}, bf16[128,512]{1,0:T(8,128)(2,1)S(1)}, u32[]{:S(2)}, u32[]{:S(2)}) collective-permute-start(bf16[128,512]{1,0:T(8,128)(2,1)S(1)} %fusion.1), channel_id=1, source_target_pairs={{0,2},{1,3},{2,0},{3,1},{4,6},{5,7},{6,4},{7,5},{8,10},{9,11},{10,... | collective-permute-start | bytes 393224 | tf_op jit(solution)/shard_map/ppermute | solution.py:176
  16.0 1.6 %collective-permute-start.6 = (bf16[128,512]{1,0:T(8,128)(2,1)S(1)}, bf16[128,512]{1,0:T(8,128)(2,1)S(1)}, u32[]{:S(2)}, u32[]{:S(2)}) collective-permute-start(bf16[128,512]{1,0:T(8,128)(2,1)S(1)} %fusion.2), channel_id=1, source_target_pairs={{0,1},{1,0},{2,3},{3,2},{4,5},{5,4},{6,7},{7,6},{8,9},{9,8},{10,11... | collective-permute-start | bytes 393224 | tf_op jit(solution)/shard_map/ppermute | solution.py:176
  18.3 5.5 %collective-permute-done.7.refs_3_ = bf16[128,512]{1,0:T(8,128)(2,1)S(1)} collective-permute-done((bf16[128,512]{1,0:T(8,128)(2,1)S(1)}, bf16[128,512]{1,0:T(8,128)(2,1)S(1)}, u32[]{:S(2)}, u32[]{:S(2)}) %collective-permute-start.7) | collective-permute-done | bytes 131104 | tf_op jit(solution)/shard_map/ppermute | solution.py:176
  23.8 2.6 %collective-permute-done.5.refs_1_ = bf16[128,512]{1,0:T(8,128)(2,1)S(1)} collective-permute-done((bf16[128,512]{1,0:T(8,128)(2,1)S(1)}, bf16[128,512]{1,0:T(8,128)(2,1)S(1)}, u32[]{:S(2)}, u32[]{:S(2)}) %collective-permute-start.5) | collective-permute-done | bytes 131104 | tf_op jit(solution)/shard_map/ppermute | solution.py:176
  27.1 0.9 %shard_map.79 = (f32[256,512]{1,0:T(8,128)S(1)}, bf16[128,512]{1,0:T(8,128)(2,1)}) custom-call(s32[1]{0:T(128)} %bitcast.half_ref, bf16[128,512]{1,0:T(8,128)(2,1)S(1)} %get-tuple-element.16.agg_ref, bf16[128,512]{1,0:T(8,128)(2,1)S(1)} %get-tuple-element.17.pre_ref, f32[128,512]{1,0:T(8,128)S(1)} %get-tuple-element.18.preact_ref), custom_call_target="tpu_custom_call" | custom-call | flops 33554432 | bytes 262144 | tf_op jit(solution)/shard_map/pallas_call | solution.py:153
  28.7 1.6 %collective-permute-start.10 = (bf16[64,512]{1,0:T(8,128)(2,1)S(1)}, bf16[64,512]{1,0:T(8,128)(2,1)S(1)}, u32[]{:S(2)}, u32[]{:S(2)}) collective-permute-start(bf16[64,512]{1,0:T(8,128)(2,1)S(1)} %get-tuple-element.24), channel_id=1, source_target_pairs={{0,16},{1,17},{2,18},{3,19},{4,6},{5,7},{6,4},{7,5},{8,24},{9,25},... | collective-permute-start | bytes 196616 | tf_op jit(solution)/shard_map/ppermute | solution.py:187
  30.2 1.5 %collective-permute-start.11 = (bf16[64,512]{1,0:T(8,128)(2,1)S(1)}, bf16[64,512]{1,0:T(8,128)(2,1)S(1)}, u32[]{:S(2)}, u32[]{:S(2)}) collective-permute-start(bf16[64,512]{1,0:T(8,128)(2,1)S(1)} %get-tuple-element.23), channel_id=1, source_target_pairs={{0,24},{1,25},{2,26},{3,27},{4,7},{5,6},{6,5},{7,4},{8,16},{9,17},... | collective-permute-start | bytes 196616 | tf_op jit(solution)/shard_map/ppermute | solution.py:187
  32.2 0.8 %collective-permute-done.10 = bf16[64,512]{1,0:T(8,128)(2,1)S(1)} collective-permute-done((bf16[64,512]{1,0:T(8,128)(2,1)S(1)}, bf16[64,512]{1,0:T(8,128)(2,1)S(1)}, u32[]{:S(2)}, u32[]{:S(2)}) %collective-permute-start.10) | collective-permute-done | bytes 65568 | tf_op jit(solution)/shard_map/ppermute | solution.py:187
  33.0 2.4 %collective-permute-done.11 = bf16[64,512]{1,0:T(8,128)(2,1)S(1)} collective-permute-done((bf16[64,512]{1,0:T(8,128)(2,1)S(1)}, bf16[64,512]{1,0:T(8,128)(2,1)S(1)}, u32[]{:S(2)}, u32[]{:S(2)}) %collective-permute-start.11) | collective-permute-done | bytes 65568 | tf_op jit(solution)/shard_map/ppermute | solution.py:187
  36.0 2.5 %collective-permute-start.12 = (bf16[64,512]{1,0:T(8,128)(2,1)S(1)}, bf16[64,512]{1,0:T(8,128)(2,1)S(1)}, u32[]{:S(2)}, u32[]{:S(2)}) collective-permute-start(bf16[64,512]{1,0:T(8,128)(2,1)S(1)} %fusion.7), channel_id=1, source_target_pairs={{0,3},{1,2},{2,1},{3,0},{4,28},{5,29},{6,30},{7,31},{8,11},{9,10},... | collective-permute-start | bytes 196616 | tf_op jit(solution)/shard_map/ppermute | solution.py:187
  38.6 1.8 %collective-permute-start.13 = (bf16[64,512]{1,0:T(8,128)(2,1)S(1)}, bf16[64,512]{1,0:T(8,128)(2,1)S(1)}, u32[]{:S(2)}, u32[]{:S(2)}) collective-permute-start(bf16[64,512]{1,0:T(8,128)(2,1)S(1)} %fusion.7), channel_id=1, source_target_pairs={{0,2},{1,3},{2,0},{3,1},{4,20},{5,21},{6,22},{7,23},{8,10},{9,11},... | collective-permute-start | bytes 196616 | tf_op jit(solution)/shard_map/ppermute | solution.py:187
  40.9 1.3 %collective-permute-done.12 = bf16[64,512]{1,0:T(8,128)(2,1)S(1)} collective-permute-done((bf16[64,512]{1,0:T(8,128)(2,1)S(1)}, bf16[64,512]{1,0:T(8,128)(2,1)S(1)}, u32[]{:S(2)}, u32[]{:S(2)}) %collective-permute-start.12) | collective-permute-done | bytes 65568 | tf_op jit(solution)/shard_map/ppermute | solution.py:187
  42.2 1.5 %collective-permute-done.13 = bf16[64,512]{1,0:T(8,128)(2,1)S(1)} collective-permute-done((bf16[64,512]{1,0:T(8,128)(2,1)S(1)}, bf16[64,512]{1,0:T(8,128)(2,1)S(1)}, u32[]{:S(2)}, u32[]{:S(2)}) %collective-permute-start.13) | collective-permute-done | bytes 65568 | tf_op jit(solution)/shard_map/ppermute | solution.py:187
  43.7 0.9 %collective-permute-done.14 = bf16[64,512]{1,0:T(8,128)(2,1)S(1)} collective-permute-done((bf16[64,512]{1,0:T(8,128)(2,1)S(1)}, bf16[64,512]{1,0:T(8,128)(2,1)S(1)}, u32[]{:S(2)}, u32[]{:S(2)}) %collective-permute-start.14) | collective-permute-done | bytes 65568 | tf_op jit(solution)/shard_map/ppermute | solution.py:187
  44.7 1.5 %collective-permute-start.18 = (bf16[64,512]{1,0:T(8,128)(2,1)S(1)}, bf16[64,512]{1,0:T(8,128)(2,1)S(1)}, u32[]{:S(2)}, u32[]{:S(2)}) collective-permute-start(bf16[64,512]{1,0:T(8,128)(2,1)S(1)} %add_convert_fusion), channel_id=1, source_target_pairs={{0,24},{1,25},{2,26},{3,27},{4,7},{5,6},{6,5},{7,4},{8,16},{9,17},... | collective-permute-start | bytes 196616 | tf_op jit(solution)/shard_map/ppermute | solution.py:187
  46.2 0.7 %collective-permute-start.15 = (bf16[64,512]{1,0:T(8,128)(2,1)S(1)}, bf16[64,512]{1,0:T(8,128)(2,1)S(1)}, u32[]{:S(2)}, u32[]{:S(2)}) collective-permute-start(bf16[64,512]{1,0:T(8,128)(2,1)S(1)} %add_convert_fusion), channel_id=1, source_target_pairs={{0,16},{1,17},{2,18},{3,19},{4,6},{5,7},{6,4},{7,5},{8,24},{9,25},... | collective-permute-start | bytes 196616 | tf_op jit(solution)/shard_map/ppermute | solution.py:187
  46.9 1.3 %collective-permute-start.16 = (bf16[64,512]{1,0:T(8,128)(2,1)S(1)}, bf16[64,512]{1,0:T(8,128)(2,1)S(1)}, u32[]{:S(2)}, u32[]{:S(2)}) collective-permute-start(bf16[64,512]{1,0:T(8,128)(2,1)S(1)} %add_convert_fusion), channel_id=1, source_target_pairs={{0,8},{1,9},{2,10},{3,11},{4,5},{5,4},{6,7},{7,6},{8,0},{9,1},{10,... | collective-permute-start | bytes 196616 | tf_op jit(solution)/shard_map/ppermute | solution.py:187
  48.3 1.7 %collective-permute-done.18 = bf16[64,512]{1,0:T(8,128)(2,1)S(1)} collective-permute-done((bf16[64,512]{1,0:T(8,128)(2,1)S(1)}, bf16[64,512]{1,0:T(8,128)(2,1)S(1)}, u32[]{:S(2)}, u32[]{:S(2)}) %collective-permute-start.18) | collective-permute-done | bytes 65568 | tf_op jit(solution)/shard_map/ppermute | solution.py:187
  51.4 0.9 %shard_map.80.refs_1_ = f32[2,4,64,512]{3,2,1,0:T(8,128)} custom-call(s32[1]{0:T(128)} %bitcast.half_ref, s32[1]{0:T(128)} %bitcast.3.own_ref, s32[1]{0:T(128)} %bitcast.4.other_ref, bf16[128,512]{1,0:T(8,128)(2,1)S(1)} %pad_maximum_fusion.refs_0_, bf16[128,512]{1,0:T(8,128)(2,1)S(1)} %constant_dynamic-update-slice_fusion.4.refs_1_, ...), custom_call_target="tpu_custom_call" | custom-call | flops 196608 | bytes 1179648 | tf_op jit(solution)/shard_map/pallas_call | solution.py:117
  (51 shorter events, 10.2 us)
Async XLA Ops:
  0.6 9.1 %collective-permute-start = (bf16[128,512]{1,0:T(8,128)(2,1)}, bf16[128,512]{1,0:T(8,128)(2,1)S(1)}, u32[]{:S(2)}, u32[]{:S(2)}) collective-permute-start(bf16[128,512]{1,0:T(8,128)(2,1)} %param.6), channel_id=1, source_target_pairs={{0,24},{4,28},{8,16},{12,20},{16,8},{20,12},{24,0},{28,4},{1,25},{... | collective-permute-start | bytes 393224 | tf_op jit(solution)/shard_map/ppermute | solution.py:173
  4.6 6.5 %collective-permute-start.2 = (bf16[128,512]{1,0:T(8,128)(2,1)}, bf16[128,512]{1,0:T(8,128)(2,1)S(1)}, u32[]{:S(2)}, u32[]{:S(2)}) collective-permute-start(bf16[128,512]{1,0:T(8,128)(2,1)} %param.6), channel_id=1, source_target_pairs={{0,16},{4,20},{8,24},{12,28},{16,0},{20,4},{24,8},{28,12},{1,17},{... | collective-permute-start | bytes 393224 | tf_op jit(solution)/shard_map/ppermute | solution.py:173
  5.1 6.3 %collective-permute-start.3 = (bf16[128,512]{1,0:T(8,128)(2,1)}, bf16[128,512]{1,0:T(8,128)(2,1)S(1)}, u32[]{:S(2)}, u32[]{:S(2)}) collective-permute-start(bf16[128,512]{1,0:T(8,128)(2,1)} %param.6), channel_id=1, source_target_pairs={{0,8},{4,12},{8,0},{12,4},{16,24},{20,28},{24,16},{28,20},{1,9},{5... | collective-permute-start | bytes 393224 | tf_op jit(solution)/shard_map/ppermute | solution.py:173
  6.2 0.7 %copy-start.4 = (s32[1,1,4,3]{2,1,3,0:T(1,128)S(1)}, s32[1,1,4,3]{2,1,3,0:T(1,128)}, u32[]{:S(2)}) copy-start(s32[1,1,4,3]{2,1,3,0:T(1,128)} %param.9) | copy-start | bytes 148
  7.5 1.0 %copy-start.1 = (bf16[1,1,4,3,128,128]{5,4,3,2,1,0:T(8,128)(2,1)S(1)}, bf16[1,1,4,3,128,128]{5,4,3,2,1,0:T(8,128)(2,1)}, u32[]{:S(2)}) copy-start(bf16[1,1,4,3,128,128]{5,4,3,2,1,0:T(8,128)(2,1)} %tiles_ref.1) | copy-start | bytes 1179652
  9.8 2.0 %collective-permute-start.1 = (bf16[256,512]{1,0:T(8,128)(2,1)S(1)}, bf16[256,512]{1,0:T(8,128)(2,1)S(1)}, u32[]{:S(2)}, u32[]{:S(2)}) collective-permute-start(bf16[256,512]{1,0:T(8,128)(2,1)S(1)} %constant_dynamic-update-slice_fusion), channel_id=1, source_target_pairs={{0,4},{4,0},{8,12},{12,8},{16,20},{20,16},{24,28},{28,24},{1,5},{5... | collective-permute-start | bytes 786440 | tf_op jit(solution)/shard_map/ppermute | solution.py:173
  11.4 1.6 %collective-permute-start.4 = (bf16[256,512]{1,0:T(8,128)(2,1)S(1)}, bf16[256,512]{1,0:T(8,128)(2,1)S(1)}, u32[]{:S(2)}, u32[]{:S(2)}) collective-permute-start(bf16[256,512]{1,0:T(8,128)(2,1)S(1)} %constant_dynamic-update-slice_fusion.2), channel_id=1, source_target_pairs={{0,4},{4,0},{8,12},{12,8},{16,20},{20,16},{24,28},{28,24},{1,5},{5... | collective-permute-start | bytes 786440 | tf_op jit(solution)/shard_map/ppermute | solution.py:173
  13.2 10.7 %collective-permute-start.7 = (bf16[128,512]{1,0:T(8,128)(2,1)S(1)}, bf16[128,512]{1,0:T(8,128)(2,1)S(1)}, u32[]{:S(2)}, u32[]{:S(2)}) collective-permute-start(bf16[128,512]{1,0:T(8,128)(2,1)S(1)} %fusion.1), channel_id=1, source_target_pairs={{0,2},{1,3},{2,0},{3,1},{4,6},{5,7},{6,4},{7,5},{8,10},{9,11},{10,... | collective-permute-start | bytes 393224 | tf_op jit(solution)/shard_map/ppermute | solution.py:176
  16.0 7.8 %collective-permute-start.6 = (bf16[128,512]{1,0:T(8,128)(2,1)S(1)}, bf16[128,512]{1,0:T(8,128)(2,1)S(1)}, u32[]{:S(2)}, u32[]{:S(2)}) collective-permute-start(bf16[128,512]{1,0:T(8,128)(2,1)S(1)} %fusion.2), channel_id=1, source_target_pairs={{0,1},{1,0},{2,3},{3,2},{4,5},{5,4},{6,7},{7,6},{8,9},{9,8},{10,11... | collective-permute-start | bytes 393224 | tf_op jit(solution)/shard_map/ppermute | solution.py:176
  17.8 8.6 %copy-start = (bf16[512,512]{1,0:T(8,128)(2,1)S(1)}, bf16[512,512]{1,0:T(8,128)(2,1)}, u32[]{:S(2)}) copy-start(bf16[512,512]{1,0:T(8,128)(2,1)} %refs_4_.1) | copy-start | bytes 1572868
  17.9 8.6 %copy-start.2 = (bf16[128,512]{1,0:T(8,128)(2,1)S(1)}, bf16[128,512]{1,0:T(8,128)(2,1)}, u32[]{:S(2)}) copy-start(bf16[128,512]{1,0:T(8,128)(2,1)} %refs_5_.1) | copy-start | bytes 393220
  17.9 8.6 %collective-permute-start.5 = (bf16[128,512]{1,0:T(8,128)(2,1)S(1)}, bf16[128,512]{1,0:T(8,128)(2,1)S(1)}, u32[]{:S(2)}, u32[]{:S(2)}) collective-permute-start(bf16[128,512]{1,0:T(8,128)(2,1)S(1)} %fusion.3), channel_id=1, source_target_pairs={{0,3},{1,2},{2,1},{3,0},{4,7},{5,6},{6,5},{7,4},{8,11},{9,10},{10,... | collective-permute-start | bytes 393224 | tf_op jit(solution)/shard_map/ppermute | solution.py:176
  26.9 1.6 %collective-permute-start.8 = (bf16[256,512]{1,0:T(8,128)(2,1)S(1)}, bf16[256,512]{1,0:T(8,128)(2,1)S(1)}, u32[]{:S(2)}, u32[]{:S(2)}) collective-permute-start(bf16[256,512]{1,0:T(8,128)(2,1)S(1)} %get-tuple-element.21), channel_id=1, source_target_pairs={{0,4},{4,0},{8,12},{12,8},{16,20},{20,16},{24,28},{28,24},{1,5},{5... | collective-permute-start | bytes 786440 | tf_op jit(solution)/shard_map/ppermute | solution.py:173
  28.7 4.3 %collective-permute-start.10 = (bf16[64,512]{1,0:T(8,128)(2,1)S(1)}, bf16[64,512]{1,0:T(8,128)(2,1)S(1)}, u32[]{:S(2)}, u32[]{:S(2)}) collective-permute-start(bf16[64,512]{1,0:T(8,128)(2,1)S(1)} %get-tuple-element.24), channel_id=1, source_target_pairs={{0,16},{1,17},{2,18},{3,19},{4,6},{5,7},{6,4},{7,5},{8,24},{9,25},... | collective-permute-start | bytes 196616 | tf_op jit(solution)/shard_map/ppermute | solution.py:187
  30.2 5.2 %collective-permute-start.11 = (bf16[64,512]{1,0:T(8,128)(2,1)S(1)}, bf16[64,512]{1,0:T(8,128)(2,1)S(1)}, u32[]{:S(2)}, u32[]{:S(2)}) collective-permute-start(bf16[64,512]{1,0:T(8,128)(2,1)S(1)} %get-tuple-element.23), channel_id=1, source_target_pairs={{0,24},{1,25},{2,26},{3,27},{4,7},{5,6},{6,5},{7,4},{8,16},{9,17},... | collective-permute-start | bytes 196616 | tf_op jit(solution)/shard_map/ppermute | solution.py:187
  31.7 4.3 %collective-permute-start.9 = (bf16[64,512]{1,0:T(8,128)(2,1)S(1)}, bf16[64,512]{1,0:T(8,128)(2,1)S(1)}, u32[]{:S(2)}, u32[]{:S(2)}) collective-permute-start(bf16[64,512]{1,0:T(8,128)(2,1)S(1)} %get-tuple-element.22), channel_id=1, source_target_pairs={{0,8},{1,9},{2,10},{3,11},{4,5},{5,4},{6,7},{7,6},{8,0},{9,1},{10,... | collective-permute-start | bytes 196616 | tf_op jit(solution)/shard_map/ppermute | solution.py:187
  36.0 6.2 %collective-permute-start.12 = (bf16[64,512]{1,0:T(8,128)(2,1)S(1)}, bf16[64,512]{1,0:T(8,128)(2,1)S(1)}, u32[]{:S(2)}, u32[]{:S(2)}) collective-permute-start(bf16[64,512]{1,0:T(8,128)(2,1)S(1)} %fusion.7), channel_id=1, source_target_pairs={{0,3},{1,2},{2,1},{3,0},{4,28},{5,29},{6,30},{7,31},{8,11},{9,10},... | collective-permute-start | bytes 196616 | tf_op jit(solution)/shard_map/ppermute | solution.py:187
  38.6 5.2 %collective-permute-start.13 = (bf16[64,512]{1,0:T(8,128)(2,1)S(1)}, bf16[64,512]{1,0:T(8,128)(2,1)S(1)}, u32[]{:S(2)}, u32[]{:S(2)}) collective-permute-start(bf16[64,512]{1,0:T(8,128)(2,1)S(1)} %fusion.7), channel_id=1, source_target_pairs={{0,2},{1,3},{2,0},{3,1},{4,20},{5,21},{6,22},{7,23},{8,10},{9,11},... | collective-permute-start | bytes 196616 | tf_op jit(solution)/shard_map/ppermute | solution.py:187
  40.4 4.3 %collective-permute-start.14 = (bf16[64,512]{1,0:T(8,128)(2,1)S(1)}, bf16[64,512]{1,0:T(8,128)(2,1)S(1)}, u32[]{:S(2)}, u32[]{:S(2)}) collective-permute-start(bf16[64,512]{1,0:T(8,128)(2,1)S(1)} %fusion.7), channel_id=1, source_target_pairs={{0,1},{1,0},{2,3},{3,2},{4,12},{5,13},{6,14},{7,15},{8,9},{9,8},{1... | collective-permute-start | bytes 196616 | tf_op jit(solution)/shard_map/ppermute | solution.py:187
  44.7 5.2 %collective-permute-start.18 = (bf16[64,512]{1,0:T(8,128)(2,1)S(1)}, bf16[64,512]{1,0:T(8,128)(2,1)S(1)}, u32[]{:S(2)}, u32[]{:S(2)}) collective-permute-start(bf16[64,512]{1,0:T(8,128)(2,1)S(1)} %add_convert_fusion), channel_id=1, source_target_pairs={{0,24},{1,25},{2,26},{3,27},{4,7},{5,6},{6,5},{7,4},{8,16},{9,17},... | collective-permute-start | bytes 196616 | tf_op jit(solution)/shard_map/ppermute | solution.py:187
  46.2 4.4 %collective-permute-start.15 = (bf16[64,512]{1,0:T(8,128)(2,1)S(1)}, bf16[64,512]{1,0:T(8,128)(2,1)S(1)}, u32[]{:S(2)}, u32[]{:S(2)}) collective-permute-start(bf16[64,512]{1,0:T(8,128)(2,1)S(1)} %add_convert_fusion), channel_id=1, source_target_pairs={{0,16},{1,17},{2,18},{3,19},{4,6},{5,7},{6,4},{7,5},{8,24},{9,25},... | collective-permute-start | bytes 196616 | tf_op jit(solution)/shard_map/ppermute | solution.py:187
  46.9 4.3 %collective-permute-start.16 = (bf16[64,512]{1,0:T(8,128)(2,1)S(1)}, bf16[64,512]{1,0:T(8,128)(2,1)S(1)}, u32[]{:S(2)}, u32[]{:S(2)}) collective-permute-start(bf16[64,512]{1,0:T(8,128)(2,1)S(1)} %add_convert_fusion), channel_id=1, source_target_pairs={{0,8},{1,9},{2,10},{3,11},{4,5},{5,4},{6,7},{7,6},{8,0},{9,1},{10,... | collective-permute-start | bytes 196616 | tf_op jit(solution)/shard_map/ppermute | solution.py:187
  50.0 1.4 %collective-permute-start.19 = (bf16[128,512]{1,0:T(8,128)(2,1)S(1)}, bf16[128,512]{1,0:T(8,128)(2,1)S(1)}, u32[]{:S(2)}, u32[]{:S(2)}) collective-permute-start(bf16[128,512]{1,0:T(8,128)(2,1)S(1)} %pad_maximum_fusion.refs_0_), channel_id=1, source_target_pairs={{0,4},{4,0},{8,12},{12,8},{16,20},{20,16},{24,28},{28,24},{1,5},{5... | collective-permute-start | bytes 393224 | tf_op jit(solution)/shard_map/ppermute | solution.py:173
  51.2 1.3 %collective-permute-start.17 = (bf16[128,512]{1,0:T(8,128)(2,1)S(1)}, bf16[128,512]{1,0:T(8,128)(2,1)S(1)}, u32[]{:S(2)}, u32[]{:S(2)}) collective-permute-start(bf16[128,512]{1,0:T(8,128)(2,1)S(1)} %constant_dynamic-update-slice_fusion.4.refs_1_), channel_id=1, source_target_pairs={{0,4},{4,0},{8,12},{12,8},{16,20},{20,16},{24,28},{28,24},{1,5},{5... | collective-permute-start | bytes 393224 | tf_op jit(solution)/shard_map/ppermute | solution.py:173
  (1 other events, 0.7 us)

commit v6 on v5

--- a/solution.py
+++ b/solution.py
@@ -231,7 +231,7 @@
         piece = size // chips
         kept = kept.reshape(chips, piece, hidden)
         mine = lax.dynamic_index_in_dim(kept, place, 0, keepdims=False)
-        for k in range(1, chips):
+        for k in [1] + list(range(chips - 1, 1, -1)):
             other = lax.dynamic_index_in_dim(kept, place ^ k, 0, keepdims=False)
             mine = mine + first(other.astype(jnp.bfloat16), k).astype(jnp.float32)
         mine = mine.astype(jnp.bfloat16)

time: 53.5 us -> 53.3 us (level)
  transfers between devices with their start and end apart: 20 -> 20, of which waited for: 17 -> 16; matrix products, arithmetic and copies ran while one was open for 5% -> 5% of each run, Pallas kernels for 6% -> 6%
where the time goes in v6:
time: 53.3 us; the launch traced here: 53.1 us
  starting transfers between devices  21.4 us (40%)
  waiting for transfers between devices  21.4 us (40%)
  Pallas kernels  4.22 us (8%)
  local copies, waits for them, and re-layouts  3.28 us (6%)
  matrix products  1.63 us (3%)
  between operations  0.9 us (2%)
    ppermute x9, starting transfers between devices, by_core(): return lax.ppermute(value, ('row', 'col'), pairs)  12 us
    ppermute x9, waiting for transfers between devices, by_core(): return lax.ppermute(value, ('row', 'col'), pairs)  10.2 us
    ppermute x3, waiting for transfers between devices, over_col(): return lax.ppermute(value, 'col', [(i, i ^ bits) for i in range(cols)])  8.1 us
    ppermute x8, starting transfers between devices, over_row(): return lax.ppermute(value, 'row', [(i, i ^ bits) for i in range(rows)])  4.89 us
    ppermute x3, starting transfers between devices, over_col(): return lax.ppermute(value, 'col', [(i, i ^ bits) for i in range(cols)])  4.58 us
    unnamed x14, local copies, waits for them, and re-layouts  3.22 us
    ppermute x8, waiting for transfers between devices, over_row(): return lax.ppermute(value, 'row', [(i, i ^ bits) for i in range(rows)])  3.1 us
    pallas_call x2, Pallas kernels, write(): pl.pallas_call(functools.partial(write_kernel, turns), out_shape=jax.Shap...  1.65 us
  transfers between devices with their start and end apart: 20, of which 16 were waited for; matrix products, arithmetic and copies ran while one was open for 5% of the time, Pallas kernels for 6%

profile of v6, /device:TPU:0, one launch (start us, length us, event | category | flops | bytes accessed | tf_op | source)
XLA Modules:
  0.0 53.1 jit_solution(17446808315371748740)
XLA Ops:
  0.6 4.0 %collective-permute-start = (bf16[128,512]{1,0:T(8,128)(2,1)}, bf16[128,512]{1,0:T(8,128)(2,1)S(1)}, u32[]{:S(2)}, u32[]{:S(2)}) collective-permute-start(bf16[128,512]{1,0:T(8,128)(2,1)} %param.6), channel_id=1, source_target_pairs={{0,24},{4,28},{8,16},{12,20},{16,8},{20,12},{24,0},{28,4},{1,25},{... | collective-permute-start | bytes 393224 | tf_op jit(solution)/shard_map/ppermute | solution.py:173
  5.2 0.9 %constant_dynamic-update-slice_fusion.1 = bf16[256,512]{1,0:T(8,128)(2,1)S(1)} fusion(bf16[128,512]{1,0:T(8,128)(2,1)} %param.6), kind=kLoop, calls=%fused_computation.32 | loop fusion | bytes 262144
  7.5 1.0 %copy-done.1 = bf16[1,1,4,3,128,128]{5,4,3,2,1,0:T(8,128)(2,1)S(1)} copy-done((bf16[1,1,4,3,128,128]{5,4,3,2,1,0:T(8,128)(2,1)S(1)}, bf16[1,1,4,3,128,128]{5,4,3,2,1,0:T(8,128)(2,1)}, u32[]{:S(2)}) %copy-start.1) | copy-done | bytes 393240
  8.5 1.2 %shard_map.77 = (bf16[512,256]{1,0:T(8,128)(2,1)S(1)}, bf16[512,256]{1,0:T(8,128)(2,1)S(1)}, bf16[512,256]{1,0:T(8,128)(2,1)S(1)}, bf16[512,256]{1,0:T(8,128)(2,1)S(1)}) custom-call(s32[2]{0:T(128)S(1)} %pad_add_fusion.ids_ref, s32[1,1,4,3]{3,2,1,0:T(4,128)S(1)} %copy.9.col_ref, s32[1,1,4]{2,1,0:T(1,128)S(1)} %copy-done.3, ...), custom_call_target="tpu_custom_call" | custom-call | flops 196608 | bytes 1179648 | tf_op jit(solution)/shard_map/pallas_call | solution.py:42
  9.9 1.2 %collective-permute-done.2 = bf16[128,512]{1,0:T(8,128)(2,1)S(1)} collective-permute-done((bf16[128,512]{1,0:T(8,128)(2,1)}, bf16[128,512]{1,0:T(8,128)(2,1)S(1)}, u32[]{:S(2)}, u32[]{:S(2)}) %collective-permute-start.2) | collective-permute-done | bytes 131104 | tf_op jit(solution)/shard_map/ppermute | solution.py:173
  13.2 2.7 %collective-permute-start.7 = (bf16[128,512]{1,0:T(8,128)(2,1)S(1)}, bf16[128,512]{1,0:T(8,128)(2,1)S(1)}, u32[]{:S(2)}, u32[]{:S(2)}) collective-permute-start(bf16[128,512]{1,0:T(8,128)(2,1)S(1)} %fusion.1), channel_id=1, source_target_pairs={{0,2},{1,3},{2,0},{3,1},{4,6},{5,7},{6,4},{7,5},{8,10},{9,11},{10,... | collective-permute-start | bytes 393224 | tf_op jit(solution)/shard_map/ppermute | solution.py:176
  16.0 1.6 %collective-permute-start.6 = (bf16[128,512]{1,0:T(8,128)(2,1)S(1)}, bf16[128,512]{1,0:T(8,128)(2,1)S(1)}, u32[]{:S(2)}, u32[]{:S(2)}) collective-permute-start(bf16[128,512]{1,0:T(8,128)(2,1)S(1)} %fusion.2), channel_id=1, source_target_pairs={{0,1},{1,0},{2,3},{3,2},{4,5},{5,4},{6,7},{7,6},{8,9},{9,8},{10,11... | collective-permute-start | bytes 393224 | tf_op jit(solution)/shard_map/ppermute | solution.py:176
  18.3 5.5 %collective-permute-done.7.refs_3_ = bf16[128,512]{1,0:T(8,128)(2,1)S(1)} collective-permute-done((bf16[128,512]{1,0:T(8,128)(2,1)S(1)}, bf16[128,512]{1,0:T(8,128)(2,1)S(1)}, u32[]{:S(2)}, u32[]{:S(2)}) %collective-permute-start.7) | collective-permute-done | bytes 131104 | tf_op jit(solution)/shard_map/ppermute | solution.py:176
  23.8 2.6 %collective-permute-done.5.refs_1_ = bf16[128,512]{1,0:T(8,128)(2,1)S(1)} collective-permute-done((bf16[128,512]{1,0:T(8,128)(2,1)S(1)}, bf16[128,512]{1,0:T(8,128)(2,1)S(1)}, u32[]{:S(2)}, u32[]{:S(2)}) %collective-permute-start.5) | collective-permute-done | bytes 131104 | tf_op jit(solution)/shard_map/ppermute | solution.py:176
  27.1 0.9 %shard_map.79 = (f32[256,512]{1,0:T(8,128)S(1)}, bf16[128,512]{1,0:T(8,128)(2,1)}) custom-call(s32[1]{0:T(128)} %bitcast.half_ref, bf16[128,512]{1,0:T(8,128)(2,1)S(1)} %get-tuple-element.16.agg_ref, bf16[128,512]{1,0:T(8,128)(2,1)S(1)} %get-tuple-element.17.pre_ref, f32[128,512]{1,0:T(8,128)S(1)} %get-tuple-element.18.preact_ref), custom_call_target="tpu_custom_call" | custom-call | flops 33554432 | bytes 262144 | tf_op jit(solution)/shard_map/pallas_call | solution.py:153
  28.7 1.9 %collective-permute-start.10 = (bf16[64,512]{1,0:T(8,128)(2,1)S(1)}, bf16[64,512]{1,0:T(8,128)(2,1)S(1)}, u32[]{:S(2)}, u32[]{:S(2)}) collective-permute-start(bf16[64,512]{1,0:T(8,128)(2,1)S(1)} %get-tuple-element.24), channel_id=1, source_target_pairs={{0,24},{1,25},{2,26},{3,27},{4,7},{5,6},{6,5},{7,4},{8,16},{9,17},... | collective-permute-start | bytes 196616 | tf_op jit(solution)/shard_map/ppermute | solution.py:187
  30.6 1.2 %collective-permute-start.11 = (bf16[64,512]{1,0:T(8,128)(2,1)S(1)}, bf16[64,512]{1,0:T(8,128)(2,1)S(1)}, u32[]{:S(2)}, u32[]{:S(2)}) collective-permute-start(bf16[64,512]{1,0:T(8,128)(2,1)S(1)} %get-tuple-element.23), channel_id=1, source_target_pairs={{0,16},{1,17},{2,18},{3,19},{4,6},{5,7},{6,4},{7,5},{8,24},{9,25},... | collective-permute-start | bytes 196616 | tf_op jit(solution)/shard_map/ppermute | solution.py:187
  32.2 1.7 %collective-permute-done.10 = bf16[64,512]{1,0:T(8,128)(2,1)S(1)} collective-permute-done((bf16[64,512]{1,0:T(8,128)(2,1)S(1)}, bf16[64,512]{1,0:T(8,128)(2,1)S(1)}, u32[]{:S(2)}, u32[]{:S(2)}) %collective-permute-start.10) | collective-permute-done | bytes 65568 | tf_op jit(solution)/shard_map/ppermute | solution.py:187
  33.9 0.9 %collective-permute-done.11 = bf16[64,512]{1,0:T(8,128)(2,1)S(1)} collective-permute-done((bf16[64,512]{1,0:T(8,128)(2,1)S(1)}, bf16[64,512]{1,0:T(8,128)(2,1)S(1)}, u32[]{:S(2)}, u32[]{:S(2)}) %collective-permute-start.11) | collective-permute-done | bytes 65568 | tf_op jit(solution)/shard_map/ppermute | solution.py:187
  34.8 1.2 %collective-permute-done.9 = bf16[64,512]{1,0:T(8,128)(2,1)S(1)} collective-permute-done((bf16[64,512]{1,0:T(8,128)(2,1)S(1)}, bf16[64,512]{1,0:T(8,128)(2,1)S(1)}, u32[]{:S(2)}, u32[]{:S(2)}) %collective-permute-start.9) | collective-permute-done | bytes 65568 | tf_op jit(solution)/shard_map/ppermute | solution.py:187
  36.0 2.5 %collective-permute-start.12 = (bf16[64,512]{1,0:T(8,128)(2,1)S(1)}, bf16[64,512]{1,0:T(8,128)(2,1)S(1)}, u32[]{:S(2)}, u32[]{:S(2)}) collective-permute-start(bf16[64,512]{1,0:T(8,128)(2,1)S(1)} %fusion.7), channel_id=1, source_target_pairs={{0,3},{1,2},{2,1},{3,0},{4,28},{5,29},{6,30},{7,31},{8,11},{9,10},... | collective-permute-start | bytes 196616 | tf_op jit(solution)/shard_map/ppermute | solution.py:187
  38.6 1.8 %collective-permute-start.13 = (bf16[64,512]{1,0:T(8,128)(2,1)S(1)}, bf16[64,512]{1,0:T(8,128)(2,1)S(1)}, u32[]{:S(2)}, u32[]{:S(2)}) collective-permute-start(bf16[64,512]{1,0:T(8,128)(2,1)S(1)} %fusion.7), channel_id=1, source_target_pairs={{0,2},{1,3},{2,0},{3,1},{4,20},{5,21},{6,22},{7,23},{8,10},{9,11},... | collective-permute-start | bytes 196616 | tf_op jit(solution)/shard_map/ppermute | solution.py:187
  40.9 1.3 %collective-permute-done.12 = bf16[64,512]{1,0:T(8,128)(2,1)S(1)} collective-permute-done((bf16[64,512]{1,0:T(8,128)(2,1)S(1)}, bf16[64,512]{1,0:T(8,128)(2,1)S(1)}, u32[]{:S(2)}, u32[]{:S(2)}) %collective-permute-start.12) | collective-permute-done | bytes 65568 | tf_op jit(solution)/shard_map/ppermute | solution.py:187
  42.2 1.5 %collective-permute-done.13 = bf16[64,512]{1,0:T(8,128)(2,1)S(1)} collective-permute-done((bf16[64,512]{1,0:T(8,128)(2,1)S(1)}, bf16[64,512]{1,0:T(8,128)(2,1)S(1)}, u32[]{:S(2)}, u32[]{:S(2)}) %collective-permute-start.13) | collective-permute-done | bytes 65568 | tf_op jit(solution)/shard_map/ppermute | solution.py:187
  43.7 0.9 %collective-permute-done.14 = bf16[64,512]{1,0:T(8,128)(2,1)S(1)} collective-permute-done((bf16[64,512]{1,0:T(8,128)(2,1)S(1)}, bf16[64,512]{1,0:T(8,128)(2,1)S(1)}, u32[]{:S(2)}, u32[]{:S(2)}) %collective-permute-start.14) | collective-permute-done | bytes 65568 | tf_op jit(solution)/shard_map/ppermute | solution.py:187
  44.7 1.5 %collective-permute-start.18 = (bf16[64,512]{1,0:T(8,128)(2,1)S(1)}, bf16[64,512]{1,0:T(8,128)(2,1)S(1)}, u32[]{:S(2)}, u32[]{:S(2)}) collective-permute-start(bf16[64,512]{1,0:T(8,128)(2,1)S(1)} %add_convert_fusion), channel_id=1, source_target_pairs={{0,24},{1,25},{2,26},{3,27},{4,7},{5,6},{6,5},{7,4},{8,16},{9,17},... | collective-permute-start | bytes 196616 | tf_op jit(solution)/shard_map/ppermute | solution.py:187
  46.7 1.5 %collective-permute-start.16 = (bf16[64,512]{1,0:T(8,128)(2,1)S(1)}, bf16[64,512]{1,0:T(8,128)(2,1)S(1)}, u32[]{:S(2)}, u32[]{:S(2)}) collective-permute-start(bf16[64,512]{1,0:T(8,128)(2,1)S(1)} %add_convert_fusion), channel_id=1, source_target_pairs={{0,8},{1,9},{2,10},{3,11},{4,5},{5,4},{6,7},{7,6},{8,0},{9,1},{10,... | collective-permute-start | bytes 196616 | tf_op jit(solution)/shard_map/ppermute | solution.py:187
  48.3 1.7 %collective-permute-done.18 = bf16[64,512]{1,0:T(8,128)(2,1)S(1)} collective-permute-done((bf16[64,512]{1,0:T(8,128)(2,1)S(1)}, bf16[64,512]{1,0:T(8,128)(2,1)S(1)}, u32[]{:S(2)}, u32[]{:S(2)}) %collective-permute-start.18) | collective-permute-done | bytes 65568 | tf_op jit(solution)/shard_map/ppermute | solution.py:187
  51.4 0.9 %shard_map.80.refs_1_ = f32[2,4,64,512]{3,2,1,0:T(8,128)} custom-call(s32[1]{0:T(128)} %bitcast.half_ref, s32[1]{0:T(128)} %bitcast.3.own_ref, s32[1]{0:T(128)} %bitcast.4.other_ref, bf16[128,512]{1,0:T(8,128)(2,1)S(1)} %pad_maximum_fusion.refs_0_, bf16[128,512]{1,0:T(8,128)(2,1)S(1)} %constant_dynamic-update-slice_fusion.4.refs_1_, ...), custom_call_target="tpu_custom_call" | custom-call | flops 196608 | bytes 1179648 | tf_op jit(solution)/shard_map/pallas_call | solution.py:117
  (51 shorter events, 9.9 us)
Async XLA Ops:
  0.6 9.1 %collective-permute-start = (bf16[128,512]{1,0:T(8,128)(2,1)}, bf16[128,512]{1,0:T(8,128)(2,1)S(1)}, u32[]{:S(2)}, u32[]{:S(2)}) collective-permute-start(bf16[128,512]{1,0:T(8,128)(2,1)} %param.6), channel_id=1, source_target_pairs={{0,24},{4,28},{8,16},{12,20},{16,8},{20,12},{24,0},{28,4},{1,25},{... | collective-permute-start | bytes 393224 | tf_op jit(solution)/shard_map/ppermute | solution.py:173
  4.6 6.5 %collective-permute-start.2 = (bf16[128,512]{1,0:T(8,128)(2,1)}, bf16[128,512]{1,0:T(8,128)(2,1)S(1)}, u32[]{:S(2)}, u32[]{:S(2)}) collective-permute-start(bf16[128,512]{1,0:T(8,128)(2,1)} %param.6), channel_id=1, source_target_pairs={{0,16},{4,20},{8,24},{12,28},{16,0},{20,4},{24,8},{28,12},{1,17},{... | collective-permute-start | bytes 393224 | tf_op jit(solution)/shard_map/ppermute | solution.py:173
  5.1 6.3 %collective-permute-start.3 = (bf16[128,512]{1,0:T(8,128)(2,1)}, bf16[128,512]{1,0:T(8,128)(2,1)S(1)}, u32[]{:S(2)}, u32[]{:S(2)}) collective-permute-start(bf16[128,512]{1,0:T(8,128)(2,1)} %param.6), channel_id=1, source_target_pairs={{0,8},{4,12},{8,0},{12,4},{16,24},{20,28},{24,16},{28,20},{1,9},{5... | collective-permute-start | bytes 393224 | tf_op jit(solution)/shard_map/ppermute | solution.py:173
  6.2 0.7 %copy-start.4 = (s32[1,1,4,3]{2,1,3,0:T(1,128)S(1)}, s32[1,1,4,3]{2,1,3,0:T(1,128)}, u32[]{:S(2)}) copy-start(s32[1,1,4,3]{2,1,3,0:T(1,128)} %param.9) | copy-start | bytes 148
  7.5 1.0 %copy-start.1 = (bf16[1,1,4,3,128,128]{5,4,3,2,1,0:T(8,128)(2,1)S(1)}, bf16[1,1,4,3,128,128]{5,4,3,2,1,0:T(8,128)(2,1)}, u32[]{:S(2)}) copy-start(bf16[1,1,4,3,128,128]{5,4,3,2,1,0:T(8,128)(2,1)} %tiles_ref.1) | copy-start | bytes 1179652
  9.8 2.0 %collective-permute-start.1 = (bf16[256,512]{1,0:T(8,128)(2,1)S(1)}, bf16[256,512]{1,0:T(8,128)(2,1)S(1)}, u32[]{:S(2)}, u32[]{:S(2)}) collective-permute-start(bf16[256,512]{1,0:T(8,128)(2,1)S(1)} %constant_dynamic-update-slice_fusion), channel_id=1, source_target_pairs={{0,4},{4,0},{8,12},{12,8},{16,20},{20,16},{24,28},{28,24},{1,5},{5... | collective-permute-start | bytes 786440 | tf_op jit(solution)/shard_map/ppermute | solution.py:173
  11.4 1.6 %collective-permute-start.4 = (bf16[256,512]{1,0:T(8,128)(2,1)S(1)}, bf16[256,512]{1,0:T(8,128)(2,1)S(1)}, u32[]{:S(2)}, u32[]{:S(2)}) collective-permute-start(bf16[256,512]{1,0:T(8,128)(2,1)S(1)} %constant_dynamic-update-slice_fusion.2), channel_id=1, source_target_pairs={{0,4},{4,0},{8,12},{12,8},{16,20},{20,16},{24,28},{28,24},{1,5},{5... | collective-permute-start | bytes 786440 | tf_op jit(solution)/shard_map/ppermute | solution.py:173
  13.2 10.7 %collective-permute-start.7 = (bf16[128,512]{1,0:T(8,128)(2,1)S(1)}, bf16[128,512]{1,0:T(8,128)(2,1)S(1)}, u32[]{:S(2)}, u32[]{:S(2)}) collective-permute-start(bf16[128,512]{1,0:T(8,128)(2,1)S(1)} %fusion.1), channel_id=1, source_target_pairs={{0,2},{1,3},{2,0},{3,1},{4,6},{5,7},{6,4},{7,5},{8,10},{9,11},{10,... | collective-permute-start | bytes 393224 | tf_op jit(solution)/shard_map/ppermute | solution.py:176
  16.0 7.8 %collective-permute-start.6 = (bf16[128,512]{1,0:T(8,128)(2,1)S(1)}, bf16[128,512]{1,0:T(8,128)(2,1)S(1)}, u32[]{:S(2)}, u32[]{:S(2)}) collective-permute-start(bf16[128,512]{1,0:T(8,128)(2,1)S(1)} %fusion.2), channel_id=1, source_target_pairs={{0,1},{1,0},{2,3},{3,2},{4,5},{5,4},{6,7},{7,6},{8,9},{9,8},{10,11... | collective-permute-start | bytes 393224 | tf_op jit(solution)/shard_map/ppermute | solution.py:176
  17.8 8.6 %copy-start = (bf16[512,512]{1,0:T(8,128)(2,1)S(1)}, bf16[512,512]{1,0:T(8,128)(2,1)}, u32[]{:S(2)}) copy-start(bf16[512,512]{1,0:T(8,128)(2,1)} %refs_4_.1) | copy-start | bytes 1572868
  17.9 8.6 %copy-start.2 = (bf16[128,512]{1,0:T(8,128)(2,1)S(1)}, bf16[128,512]{1,0:T(8,128)(2,1)}, u32[]{:S(2)}) copy-start(bf16[128,512]{1,0:T(8,128)(2,1)} %refs_5_.1) | copy-start | bytes 393220
  17.9 8.6 %collective-permute-start.5 = (bf16[128,512]{1,0:T(8,128)(2,1)S(1)}, bf16[128,512]{1,0:T(8,128)(2,1)S(1)}, u32[]{:S(2)}, u32[]{:S(2)}) collective-permute-start(bf16[128,512]{1,0:T(8,128)(2,1)S(1)} %fusion.3), channel_id=1, source_target_pairs={{0,3},{1,2},{2,1},{3,0},{4,7},{5,6},{6,5},{7,4},{8,11},{9,10},{10,... | collective-permute-start | bytes 393224 | tf_op jit(solution)/shard_map/ppermute | solution.py:176
  26.9 1.6 %collective-permute-start.8 = (bf16[256,512]{1,0:T(8,128)(2,1)S(1)}, bf16[256,512]{1,0:T(8,128)(2,1)S(1)}, u32[]{:S(2)}, u32[]{:S(2)}) collective-permute-start(bf16[256,512]{1,0:T(8,128)(2,1)S(1)} %get-tuple-element.21), channel_id=1, source_target_pairs={{0,4},{4,0},{8,12},{12,8},{16,20},{20,16},{24,28},{28,24},{1,5},{5... | collective-permute-start | bytes 786440 | tf_op jit(solution)/shard_map/ppermute | solution.py:173
  28.7 5.2 %collective-permute-start.10 = (bf16[64,512]{1,0:T(8,128)(2,1)S(1)}, bf16[64,512]{1,0:T(8,128)(2,1)S(1)}, u32[]{:S(2)}, u32[]{:S(2)}) collective-permute-start(bf16[64,512]{1,0:T(8,128)(2,1)S(1)} %get-tuple-element.24), channel_id=1, source_target_pairs={{0,24},{1,25},{2,26},{3,27},{4,7},{5,6},{6,5},{7,4},{8,16},{9,17},... | collective-permute-start | bytes 196616 | tf_op jit(solution)/shard_map/ppermute | solution.py:187
  30.6 4.3 %collective-permute-start.11 = (bf16[64,512]{1,0:T(8,128)(2,1)S(1)}, bf16[64,512]{1,0:T(8,128)(2,1)S(1)}, u32[]{:S(2)}, u32[]{:S(2)}) collective-permute-start(bf16[64,512]{1,0:T(8,128)(2,1)S(1)} %get-tuple-element.23), channel_id=1, source_target_pairs={{0,16},{1,17},{2,18},{3,19},{4,6},{5,7},{6,4},{7,5},{8,24},{9,25},... | collective-permute-start | bytes 196616 | tf_op jit(solution)/shard_map/ppermute | solution.py:187
  31.7 4.3 %collective-permute-start.9 = (bf16[64,512]{1,0:T(8,128)(2,1)S(1)}, bf16[64,512]{1,0:T(8,128)(2,1)S(1)}, u32[]{:S(2)}, u32[]{:S(2)}) collective-permute-start(bf16[64,512]{1,0:T(8,128)(2,1)S(1)} %get-tuple-element.22), channel_id=1, source_target_pairs={{0,8},{1,9},{2,10},{3,11},{4,5},{5,4},{6,7},{7,6},{8,0},{9,1},{10,... | collective-permute-start | bytes 196616 | tf_op jit(solution)/shard_map/ppermute | solution.py:187
  36.0 6.2 %collective-permute-start.12 = (bf16[64,512]{1,0:T(8,128)(2,1)S(1)}, bf16[64,512]{1,0:T(8,128)(2,1)S(1)}, u32[]{:S(2)}, u32[]{:S(2)}) collective-permute-start(bf16[64,512]{1,0:T(8,128)(2,1)S(1)} %fusion.7), channel_id=1, source_target_pairs={{0,3},{1,2},{2,1},{3,0},{4,28},{5,29},{6,30},{7,31},{8,11},{9,10},... | collective-permute-start | bytes 196616 | tf_op jit(solution)/shard_map/ppermute | solution.py:187
  38.6 5.2 %collective-permute-start.13 = (bf16[64,512]{1,0:T(8,128)(2,1)S(1)}, bf16[64,512]{1,0:T(8,128)(2,1)S(1)}, u32[]{:S(2)}, u32[]{:S(2)}) collective-permute-start(bf16[64,512]{1,0:T(8,128)(2,1)S(1)} %fusion.7), channel_id=1, source_target_pairs={{0,2},{1,3},{2,0},{3,1},{4,20},{5,21},{6,22},{7,23},{8,10},{9,11},... | collective-permute-start | bytes 196616 | tf_op jit(solution)/shard_map/ppermute | solution.py:187
  40.4 4.3 %collective-permute-start.14 = (bf16[64,512]{1,0:T(8,128)(2,1)S(1)}, bf16[64,512]{1,0:T(8,128)(2,1)S(1)}, u32[]{:S(2)}, u32[]{:S(2)}) collective-permute-start(bf16[64,512]{1,0:T(8,128)(2,1)S(1)} %fusion.7), channel_id=1, source_target_pairs={{0,1},{1,0},{2,3},{3,2},{4,12},{5,13},{6,14},{7,15},{8,9},{9,8},{1... | collective-permute-start | bytes 196616 | tf_op jit(solution)/shard_map/ppermute | solution.py:187
  44.7 5.2 %collective-permute-start.18 = (bf16[64,512]{1,0:T(8,128)(2,1)S(1)}, bf16[64,512]{1,0:T(8,128)(2,1)S(1)}, u32[]{:S(2)}, u32[]{:S(2)}) collective-permute-start(bf16[64,512]{1,0:T(8,128)(2,1)S(1)} %add_convert_fusion), channel_id=1, source_target_pairs={{0,24},{1,25},{2,26},{3,27},{4,7},{5,6},{6,5},{7,4},{8,16},{9,17},... | collective-permute-start | bytes 196616 | tf_op jit(solution)/shard_map/ppermute | solution.py:187
  46.2 4.4 %collective-permute-start.15 = (bf16[64,512]{1,0:T(8,128)(2,1)S(1)}, bf16[64,512]{1,0:T(8,128)(2,1)S(1)}, u32[]{:S(2)}, u32[]{:S(2)}) collective-permute-start(bf16[64,512]{1,0:T(8,128)(2,1)S(1)} %add_convert_fusion), channel_id=1, source_target_pairs={{0,16},{1,17},{2,18},{3,19},{4,6},{5,7},{6,4},{7,5},{8,24},{9,25},... | collective-permute-start | bytes 196616 | tf_op jit(solution)/shard_map/ppermute | solution.py:187
  46.7 4.3 %collective-permute-start.16 = (bf16[64,512]{1,0:T(8,128)(2,1)S(1)}, bf16[64,512]{1,0:T(8,128)(2,1)S(1)}, u32[]{:S(2)}, u32[]{:S(2)}) collective-permute-start(bf16[64,512]{1,0:T(8,128)(2,1)S(1)} %add_convert_fusion), channel_id=1, source_target_pairs={{0,8},{1,9},{2,10},{3,11},{4,5},{5,4},{6,7},{7,6},{8,0},{9,1},{10,... | collective-permute-start | bytes 196616 | tf_op jit(solution)/shard_map/ppermute | solution.py:187
  50.0 1.4 %collective-permute-start.19 = (bf16[128,512]{1,0:T(8,128)(2,1)S(1)}, bf16[128,512]{1,0:T(8,128)(2,1)S(1)}, u32[]{:S(2)}, u32[]{:S(2)}) collective-permute-start(bf16[128,512]{1,0:T(8,128)(2,1)S(1)} %pad_maximum_fusion.refs_0_), channel_id=1, source_target_pairs={{0,4},{4,0},{8,12},{12,8},{16,20},{20,16},{24,28},{28,24},{1,5},{5... | collective-permute-start | bytes 393224 | tf_op jit(solution)/shard_map/ppermute | solution.py:173
  51.0 1.3 %collective-permute-start.17 = (bf16[128,512]{1,0:T(8,128)(2,1)S(1)}, bf16[128,512]{1,0:T(8,128)(2,1)S(1)}, u32[]{:S(2)}, u32[]{:S(2)}) collective-permute-start(bf16[128,512]{1,0:T(8,128)(2,1)S(1)} %constant_dynamic-update-slice_fusion.4.refs_1_), channel_id=1, source_target_pairs={{0,4},{4,0},{8,12},{12,8},{16,20},{20,16},{24,28},{28,24},{1,5},{5... | collective-permute-start | bytes 393224 | tf_op jit(solution)/shard_map/ppermute | solution.py:173
  (1 other events, 0.7 us)

commit v7 on v6

--- a/solution.py
+++ b/solution.py
@@ -7,22 +7,22 @@
 from jax.experimental.pallas import tpu as pltpu
 from jax.sharding import PartitionSpec as P
 
-LIMIT = 8 * 1024 * 1024
+LIMIT = 4 * 1024 * 1024
 VMEM = pl.BlockSpec(memory_space=pltpu.VMEM)
 SMEM = pl.BlockSpec(memory_space=pltpu.SMEM)
 HBM = pl.BlockSpec(memory_space=pltpu.HBM)
 
 
-def place_kernel(groups, ids_ref, col_ref, count_ref, tiles_ref, *out_refs):
+def place_kernel(groups, row_ref, at_ref, col_ref, count_ref, tiles_ref, *out_refs):
     row_blocks, slots, block = tiles_ref.shape[2:5]
     rows = groups[-1][1] * 2
     chips = rows // 2
     for out_ref in out_refs:
         out_ref[...] = jnp.zeros_like(out_ref)
     for q in range(row_blocks):
-        a = q ^ ids_ref[1]
+        a = q ^ at_ref[0]
         for k in range(slots):
-            position = (col_ref[0, 0, a, k] ^ ids_ref[0]) & (rows - 1)
+            position = (col_ref[0, 0, a, k] ^ row_ref[0]) & (rows - 1)
             slot = (chips - position // 2) % chips
             live = k < count_ref[0, 0, a]
             for (parity, last, first), out_ref in zip(groups, out_refs):
@@ -45,13 +45,13 @@
             jax.ShapeDtypeStruct((row_blocks * block, (last - first) * block), jnp.bfloat16)
             for _, last, first in groups
         ),
-        in_specs=[SMEM] * 3 + [VMEM],
+        in_specs=[SMEM] * 4 + [VMEM],
         out_specs=(VMEM,) * 4,
         compiler_params=pltpu.CompilerParams(vmem_limit_bytes=max(LIMIT, held)),
         cost_estimate=pl.CostEstimate(
             flops=edge_tiles.size, bytes_accessed=6 * edge_tiles.size, transcendentals=0
         ),
-    )(ids, tile_col, tile_count, edge_tiles)
+    )(*ids, tile_col, tile_count, edge_tiles)
 
 
 def columns_of(ref, half, size):
@@ -199,7 +199,7 @@
         even_b = jnp.concatenate(far[early - 1 :])
         odd_b = over_row(even_b, 1)
 
-        ids = jnp.stack([my_row, my_col]).astype(jnp.int32)
+        ids = [value.astype(jnp.int32)[None] for value in (my_row, my_col)]
         left = placed(ids, tile_col, tile_count, edge_tiles, chips)
 
         def product(one, other):

time: 53.3 us -> 53.3 us (level)
  no operation moved by 1% of the time
where the time goes in v7:
time: 53.3 us; the launch traced here: 53.1 us
  starting transfers between devices  21.4 us (40%)
  waiting for transfers between devices  21.3 us (40%)
  Pallas kernels  4.19 us (8%)
  local copies, waits for them, and re-layouts  3.45 us (6%)
  matrix products  1.63 us (3%)
  between operations  0.9 us (2%)
    ppermute x9, starting transfers between devices, by_core(): return lax.ppermute(value, ('row', 'col'), pairs)  12 us
    ppermute x9, waiting for transfers between devices, by_core(): return lax.ppermute(value, ('row', 'col'), pairs)  10.2 us
    ppermute x3, waiting for transfers between devices, over_col(): return lax.ppermute(value, 'col', [(i, i ^ bits) for i in range(cols)])  8.1 us
    ppermute x8, starting transfers between devices, over_row(): return lax.ppermute(value, 'row', [(i, i ^ bits) for i in range(rows)])  4.89 us
    ppermute x3, starting transfers between devices, over_col(): return lax.ppermute(value, 'col', [(i, i ^ bits) for i in range(cols)])  4.58 us
    unnamed x14, local copies, waits for them, and re-layouts  3.39 us
    ppermute x8, waiting for transfers between devices, over_row(): return lax.ppermute(value, 'row', [(i, i ^ bits) for i in range(rows)])  3.04 us
    pallas_call x2, Pallas kernels, write(): pl.pallas_call(functools.partial(write_kernel, turns), out_shape=jax.Shap...  1.65 us
  transfers between devices with their start and end apart: 20, of which 16 were waited for; matrix products, arithmetic and copies ran while one was open for 5% of the time, Pallas kernels for 6%

profile of v7, /device:TPU:0, one launch (start us, length us, event | category | flops | bytes accessed | tf_op | source)
XLA Modules:
  0.0 53.1 jit_solution(11208186469121835757)
XLA Ops:
  0.6 4.0 %collective-permute-start = (bf16[128,512]{1,0:T(8,128)(2,1)}, bf16[128,512]{1,0:T(8,128)(2,1)S(1)}, u32[]{:S(2)}, u32[]{:S(2)}) collective-permute-start(bf16[128,512]{1,0:T(8,128)(2,1)} %param.6), channel_id=1, source_target_pairs={{0,24},{4,28},{8,16},{12,20},{16,8},{20,12},{24,0},{28,4},{1,25},{... | collective-permute-start | bytes 393224 | tf_op jit(solution)/shard_map/ppermute | solution.py:173
  5.2 0.9 %constant_dynamic-update-slice_fusion.1 = bf16[256,512]{1,0:T(8,128)(2,1)S(1)} fusion(bf16[128,512]{1,0:T(8,128)(2,1)} %param.6), kind=kLoop, calls=%fused_computation.32 | loop fusion | bytes 262144
  7.6 1.0 %copy-done.1 = bf16[1,1,4,3,128,128]{5,4,3,2,1,0:T(8,128)(2,1)S(1)} copy-done((bf16[1,1,4,3,128,128]{5,4,3,2,1,0:T(8,128)(2,1)S(1)}, bf16[1,1,4,3,128,128]{5,4,3,2,1,0:T(8,128)(2,1)}, u32[]{:S(2)}) %copy-start.1) | copy-done | bytes 393240
  8.6 1.2 %shard_map.77 = (bf16[512,256]{1,0:T(8,128)(2,1)S(1)}, bf16[512,256]{1,0:T(8,128)(2,1)S(1)}, bf16[512,256]{1,0:T(8,128)(2,1)S(1)}, bf16[512,256]{1,0:T(8,128)(2,1)S(1)}) custom-call(s32[1]{0:T(128)} %bitcast.1.row_ref, s32[1]{0:T(128)} %bitcast.2.at_ref, s32[1,1,4,3]{3,2,1,0:T(4,128)S(1)} %copy.9.col_ref, s32[1,1,4]{2,1,0:T(1,128)S(1)} %copy-done.3, ...), custom_call_target="tpu_custom_call" | custom-call | flops 196608 | bytes 1179648 | tf_op jit(solution)/shard_map/pallas_call | solution.py:42
  9.9 1.2 %collective-permute-done.2 = bf16[128,512]{1,0:T(8,128)(2,1)S(1)} collective-permute-done((bf16[128,512]{1,0:T(8,128)(2,1)}, bf16[128,512]{1,0:T(8,128)(2,1)S(1)}, u32[]{:S(2)}, u32[]{:S(2)}) %collective-permute-start.2) | collective-permute-done | bytes 131104 | tf_op jit(solution)/shard_map/ppermute | solution.py:173
  13.2 2.7 %collective-permute-start.7 = (bf16[128,512]{1,0:T(8,128)(2,1)S(1)}, bf16[128,512]{1,0:T(8,128)(2,1)S(1)}, u32[]{:S(2)}, u32[]{:S(2)}) collective-permute-start(bf16[128,512]{1,0:T(8,128)(2,1)S(1)} %fusion.1), channel_id=1, source_target_pairs={{0,2},{1,3},{2,0},{3,1},{4,6},{5,7},{6,4},{7,5},{8,10},{9,11},{10,... | collective-permute-start | bytes 393224 | tf_op jit(solution)/shard_map/ppermute | solution.py:176
  16.0 1.6 %collective-permute-start.6 = (bf16[128,512]{1,0:T(8,128)(2,1)S(1)}, bf16[128,512]{1,0:T(8,128)(2,1)S(1)}, u32[]{:S(2)}, u32[]{:S(2)}) collective-permute-start(bf16[128,512]{1,0:T(8,128)(2,1)S(1)} %fusion.2), channel_id=1, source_target_pairs={{0,1},{1,0},{2,3},{3,2},{4,5},{5,4},{6,7},{7,6},{8,9},{9,8},{10,11... | collective-permute-start | bytes 393224 | tf_op jit(solution)/shard_map/ppermute | solution.py:176
  18.3 5.5 %collective-permute-done.7.refs_3_ = bf16[128,512]{1,0:T(8,128)(2,1)S(1)} collective-permute-done((bf16[128,512]{1,0:T(8,128)(2,1)S(1)}, bf16[128,512]{1,0:T(8,128)(2,1)S(1)}, u32[]{:S(2)}, u32[]{:S(2)}) %collective-permute-start.7) | collective-permute-done | bytes 131104 | tf_op jit(solution)/shard_map/ppermute | solution.py:176
  23.8 2.6 %collective-permute-done.5.refs_1_ = bf16[128,512]{1,0:T(8,128)(2,1)S(1)} collective-permute-done((bf16[128,512]{1,0:T(8,128)(2,1)S(1)}, bf16[128,512]{1,0:T(8,128)(2,1)S(1)}, u32[]{:S(2)}, u32[]{:S(2)}) %collective-permute-start.5) | collective-permute-done | bytes 131104 | tf_op jit(solution)/shard_map/ppermute | solution.py:176
  27.1 0.9 %shard_map.79 = (f32[256,512]{1,0:T(8,128)S(1)}, bf16[128,512]{1,0:T(8,128)(2,1)}) custom-call(s32[1]{0:T(128)} %bitcast.half_ref, bf16[128,512]{1,0:T(8,128)(2,1)S(1)} %get-tuple-element.16.agg_ref, bf16[128,512]{1,0:T(8,128)(2,1)S(1)} %get-tuple-element.17.pre_ref, f32[128,512]{1,0:T(8,128)S(1)} %get-tuple-element.18.preact_ref), custom_call_target="tpu_custom_call" | custom-call | flops 33554432 | bytes 262144 | tf_op jit(solution)/shard_map/pallas_call | solution.py:153
  28.7 2.0 %collective-permute-start.10 = (bf16[64,512]{1,0:T(8,128)(2,1)S(1)}, bf16[64,512]{1,0:T(8,128)(2,1)S(1)}, u32[]{:S(2)}, u32[]{:S(2)}) collective-permute-start(bf16[64,512]{1,0:T(8,128)(2,1)S(1)} %get-tuple-element.24), channel_id=1, source_target_pairs={{0,24},{1,25},{2,26},{3,27},{4,7},{5,6},{6,5},{7,4},{8,16},{9,17},... | collective-permute-start | bytes 196616 | tf_op jit(solution)/shard_map/ppermute | solution.py:187
  30.7 1.1 %collective-permute-start.11 = (bf16[64,512]{1,0:T(8,128)(2,1)S(1)}, bf16[64,512]{1,0:T(8,128)(2,1)S(1)}, u32[]{:S(2)}, u32[]{:S(2)}) collective-permute-start(bf16[64,512]{1,0:T(8,128)(2,1)S(1)} %get-tuple-element.23), channel_id=1, source_target_pairs={{0,16},{1,17},{2,18},{3,19},{4,6},{5,7},{6,4},{7,5},{8,24},{9,25},... | collective-permute-start | bytes 196616 | tf_op jit(solution)/shard_map/ppermute | solution.py:187
  32.2 1.7 %collective-permute-done.10 = bf16[64,512]{1,0:T(8,128)(2,1)S(1)} collective-permute-done((bf16[64,512]{1,0:T(8,128)(2,1)S(1)}, bf16[64,512]{1,0:T(8,128)(2,1)S(1)}, u32[]{:S(2)}, u32[]{:S(2)}) %collective-permute-start.10) | collective-permute-done | bytes 65568 | tf_op jit(solution)/shard_map/ppermute | solution.py:187
  33.9 1.0 %collective-permute-done.11 = bf16[64,512]{1,0:T(8,128)(2,1)S(1)} collective-permute-done((bf16[64,512]{1,0:T(8,128)(2,1)S(1)}, bf16[64,512]{1,0:T(8,128)(2,1)S(1)}, u32[]{:S(2)}, u32[]{:S(2)}) %collective-permute-start.11) | collective-permute-done | bytes 65568 | tf_op jit(solution)/shard_map/ppermute | solution.py:187
  34.9 1.1 %collective-permute-done.9 = bf16[64,512]{1,0:T(8,128)(2,1)S(1)} collective-permute-done((bf16[64,512]{1,0:T(8,128)(2,1)S(1)}, bf16[64,512]{1,0:T(8,128)(2,1)S(1)}, u32[]{:S(2)}, u32[]{:S(2)}) %collective-permute-start.9) | collective-permute-done | bytes 65568 | tf_op jit(solution)/shard_map/ppermute | solution.py:187
  36.0 2.5 %collective-permute-start.12 = (bf16[64,512]{1,0:T(8,128)(2,1)S(1)}, bf16[64,512]{1,0:T(8,128)(2,1)S(1)}, u32[]{:S(2)}, u32[]{:S(2)}) collective-permute-start(bf16[64,512]{1,0:T(8,128)(2,1)S(1)} %fusion.7), channel_id=1, source_target_pairs={{0,3},{1,2},{2,1},{3,0},{4,28},{5,29},{6,30},{7,31},{8,11},{9,10},... | collective-permute-start | bytes 196616 | tf_op jit(solution)/shard_map/ppermute | solution.py:187
  38.6 1.8 %collective-permute-start.13 = (bf16[64,512]{1,0:T(8,128)(2,1)S(1)}, bf16[64,512]{1,0:T(8,128)(2,1)S(1)}, u32[]{:S(2)}, u32[]{:S(2)}) collective-permute-start(bf16[64,512]{1,0:T(8,128)(2,1)S(1)} %fusion.7), channel_id=1, source_target_pairs={{0,2},{1,3},{2,0},{3,1},{4,20},{5,21},{6,22},{7,23},{8,10},{9,11},... | collective-permute-start | bytes 196616 | tf_op jit(solution)/shard_map/ppermute | solution.py:187
  40.9 1.3 %collective-permute-done.12 = bf16[64,512]{1,0:T(8,128)(2,1)S(1)} collective-permute-done((bf16[64,512]{1,0:T(8,128)(2,1)S(1)}, bf16[64,512]{1,0:T(8,128)(2,1)S(1)}, u32[]{:S(2)}, u32[]{:S(2)}) %collective-permute-start.12) | collective-permute-done | bytes 65568 | tf_op jit(solution)/shard_map/ppermute | solution.py:187
  42.2 1.5 %collective-permute-done.13 = bf16[64,512]{1,0:T(8,128)(2,1)S(1)} collective-permute-done((bf16[64,512]{1,0:T(8,128)(2,1)S(1)}, bf16[64,512]{1,0:T(8,128)(2,1)S(1)}, u32[]{:S(2)}, u32[]{:S(2)}) %collective-permute-start.13) | collective-permute-done | bytes 65568 | tf_op jit(solution)/shard_map/ppermute | solution.py:187
  43.7 0.9 %collective-permute-done.14 = bf16[64,512]{1,0:T(8,128)(2,1)S(1)} collective-permute-done((bf16[64,512]{1,0:T(8,128)(2,1)S(1)}, bf16[64,512]{1,0:T(8,128)(2,1)S(1)}, u32[]{:S(2)}, u32[]{:S(2)}) %collective-permute-start.14) | collective-permute-done | bytes 65568 | tf_op jit(solution)/shard_map/ppermute | solution.py:187
  44.7 1.5 %collective-permute-start.18 = (bf16[64,512]{1,0:T(8,128)(2,1)S(1)}, bf16[64,512]{1,0:T(8,128)(2,1)S(1)}, u32[]{:S(2)}, u32[]{:S(2)}) collective-permute-start(bf16[64,512]{1,0:T(8,128)(2,1)S(1)} %add_convert_fusion), channel_id=1, source_target_pairs={{0,24},{1,25},{2,26},{3,27},{4,7},{5,6},{6,5},{7,4},{8,16},{9,17},... | collective-permute-start | bytes 196616 | tf_op jit(solution)/shard_map/ppermute | solution.py:187
  46.7 1.5 %collective-permute-start.16 = (bf16[64,512]{1,0:T(8,128)(2,1)S(1)}, bf16[64,512]{1,0:T(8,128)(2,1)S(1)}, u32[]{:S(2)}, u32[]{:S(2)}) collective-permute-start(bf16[64,512]{1,0:T(8,128)(2,1)S(1)} %add_convert_fusion), channel_id=1, source_target_pairs={{0,8},{1,9},{2,10},{3,11},{4,5},{5,4},{6,7},{7,6},{8,0},{9,1},{10,... | collective-permute-start | bytes 196616 | tf_op jit(solution)/shard_map/ppermute | solution.py:187
  48.3 1.7 %collective-permute-done.18 = bf16[64,512]{1,0:T(8,128)(2,1)S(1)} collective-permute-done((bf16[64,512]{1,0:T(8,128)(2,1)S(1)}, bf16[64,512]{1,0:T(8,128)(2,1)S(1)}, u32[]{:S(2)}, u32[]{:S(2)}) %collective-permute-start.18) | collective-permute-done | bytes 65568 | tf_op jit(solution)/shard_map/ppermute | solution.py:187
  51.4 0.9 %shard_map.80.refs_1_ = f32[2,4,64,512]{3,2,1,0:T(8,128)} custom-call(s32[1]{0:T(128)} %bitcast.half_ref, s32[1]{0:T(128)} %bitcast.3.own_ref, s32[1]{0:T(128)} %bitcast.4.other_ref, bf16[128,512]{1,0:T(8,128)(2,1)S(1)} %pad_maximum_fusion.refs_0_, bf16[128,512]{1,0:T(8,128)(2,1)S(1)} %constant_dynamic-update-slice_fusion.4.refs_1_, ...), custom_call_target="tpu_custom_call" | custom-call | flops 196608 | bytes 1179648 | tf_op jit(solution)/shard_map/pallas_call | solution.py:117
  (50 shorter events, 10.0 us)
Async XLA Ops:
  0.6 9.2 %collective-permute-start = (bf16[128,512]{1,0:T(8,128)(2,1)}, bf16[128,512]{1,0:T(8,128)(2,1)S(1)}, u32[]{:S(2)}, u32[]{:S(2)}) collective-permute-start(bf16[128,512]{1,0:T(8,128)(2,1)} %param.6), channel_id=1, source_target_pairs={{0,24},{4,28},{8,16},{12,20},{16,8},{20,12},{24,0},{28,4},{1,25},{... | collective-permute-start | bytes 393224 | tf_op jit(solution)/shard_map/ppermute | solution.py:173
  4.6 6.5 %collective-permute-start.2 = (bf16[128,512]{1,0:T(8,128)(2,1)}, bf16[128,512]{1,0:T(8,128)(2,1)S(1)}, u32[]{:S(2)}, u32[]{:S(2)}) collective-permute-start(bf16[128,512]{1,0:T(8,128)(2,1)} %param.6), channel_id=1, source_target_pairs={{0,16},{4,20},{8,24},{12,28},{16,0},{20,4},{24,8},{28,12},{1,17},{... | collective-permute-start | bytes 393224 | tf_op jit(solution)/shard_map/ppermute | solution.py:173
  5.1 6.3 %collective-permute-start.3 = (bf16[128,512]{1,0:T(8,128)(2,1)}, bf16[128,512]{1,0:T(8,128)(2,1)S(1)}, u32[]{:S(2)}, u32[]{:S(2)}) collective-permute-start(bf16[128,512]{1,0:T(8,128)(2,1)} %param.6), channel_id=1, source_target_pairs={{0,8},{4,12},{8,0},{12,4},{16,24},{20,28},{24,16},{28,20},{1,9},{5... | collective-permute-start | bytes 393224 | tf_op jit(solution)/shard_map/ppermute | solution.py:173
  6.2 0.7 %copy-start.4 = (s32[1,1,4,3]{2,1,3,0:T(1,128)S(1)}, s32[1,1,4,3]{2,1,3,0:T(1,128)}, u32[]{:S(2)}) copy-start(s32[1,1,4,3]{2,1,3,0:T(1,128)} %param.9) | copy-start | bytes 148
  7.6 1.0 %copy-start.1 = (bf16[1,1,4,3,128,128]{5,4,3,2,1,0:T(8,128)(2,1)S(1)}, bf16[1,1,4,3,128,128]{5,4,3,2,1,0:T(8,128)(2,1)}, u32[]{:S(2)}) copy-start(bf16[1,1,4,3,128,128]{5,4,3,2,1,0:T(8,128)(2,1)} %tiles_ref.1) | copy-start | bytes 1179652
  9.8 1.9 %collective-permute-start.1 = (bf16[256,512]{1,0:T(8,128)(2,1)S(1)}, bf16[256,512]{1,0:T(8,128)(2,1)S(1)}, u32[]{:S(2)}, u32[]{:S(2)}) collective-permute-start(bf16[256,512]{1,0:T(8,128)(2,1)S(1)} %constant_dynamic-update-slice_fusion), channel_id=1, source_target_pairs={{0,4},{4,0},{8,12},{12,8},{16,20},{20,16},{24,28},{28,24},{1,5},{5... | collective-permute-start | bytes 786440 | tf_op jit(solution)/shard_map/ppermute | solution.py:173
  11.4 1.6 %collective-permute-start.4 = (bf16[256,512]{1,0:T(8,128)(2,1)S(1)}, bf16[256,512]{1,0:T(8,128)(2,1)S(1)}, u32[]{:S(2)}, u32[]{:S(2)}) collective-permute-start(bf16[256,512]{1,0:T(8,128)(2,1)S(1)} %constant_dynamic-update-slice_fusion.2), channel_id=1, source_target_pairs={{0,4},{4,0},{8,12},{12,8},{16,20},{20,16},{24,28},{28,24},{1,5},{5... | collective-permute-start | bytes 786440 | tf_op jit(solution)/shard_map/ppermute | solution.py:173
  13.2 10.7 %collective-permute-start.7 = (bf16[128,512]{1,0:T(8,128)(2,1)S(1)}, bf16[128,512]{1,0:T(8,128)(2,1)S(1)}, u32[]{:S(2)}, u32[]{:S(2)}) collective-permute-start(bf16[128,512]{1,0:T(8,128)(2,1)S(1)} %fusion.1), channel_id=1, source_target_pairs={{0,2},{1,3},{2,0},{3,1},{4,6},{5,7},{6,4},{7,5},{8,10},{9,11},{10,... | collective-permute-start | bytes 393224 | tf_op jit(solution)/shard_map/ppermute | solution.py:176
  16.0 7.8 %collective-permute-start.6 = (bf16[128,512]{1,0:T(8,128)(2,1)S(1)}, bf16[128,512]{1,0:T(8,128)(2,1)S(1)}, u32[]{:S(2)}, u32[]{:S(2)}) collective-permute-start(bf16[128,512]{1,0:T(8,128)(2,1)S(1)} %fusion.2), channel_id=1, source_target_pairs={{0,1},{1,0},{2,3},{3,2},{4,5},{5,4},{6,7},{7,6},{8,9},{9,8},{10,11... | collective-permute-start | bytes 393224 | tf_op jit(solution)/shard_map/ppermute | solution.py:176
  17.8 8.6 %copy-start = (bf16[512,512]{1,0:T(8,128)(2,1)S(1)}, bf16[512,512]{1,0:T(8,128)(2,1)}, u32[]{:S(2)}) copy-start(bf16[512,512]{1,0:T(8,128)(2,1)} %refs_4_.1) | copy-start | bytes 1572868
  17.9 8.6 %copy-start.2 = (bf16[128,512]{1,0:T(8,128)(2,1)S(1)}, bf16[128,512]{1,0:T(8,128)(2,1)}, u32[]{:S(2)}) copy-start(bf16[128,512]{1,0:T(8,128)(2,1)} %refs_5_.1) | copy-start | bytes 393220
  17.9 8.6 %collective-permute-start.5 = (bf16[128,512]{1,0:T(8,128)(2,1)S(1)}, bf16[128,512]{1,0:T(8,128)(2,1)S(1)}, u32[]{:S(2)}, u32[]{:S(2)}) collective-permute-start(bf16[128,512]{1,0:T(8,128)(2,1)S(1)} %fusion.3), channel_id=1, source_target_pairs={{0,3},{1,2},{2,1},{3,0},{4,7},{5,6},{6,5},{7,4},{8,11},{9,10},{10,... | collective-permute-start | bytes 393224 | tf_op jit(solution)/shard_map/ppermute | solution.py:176
  26.9 1.6 %collective-permute-start.8 = (bf16[256,512]{1,0:T(8,128)(2,1)S(1)}, bf16[256,512]{1,0:T(8,128)(2,1)S(1)}, u32[]{:S(2)}, u32[]{:S(2)}) collective-permute-start(bf16[256,512]{1,0:T(8,128)(2,1)S(1)} %get-tuple-element.21), channel_id=1, source_target_pairs={{0,4},{4,0},{8,12},{12,8},{16,20},{20,16},{24,28},{28,24},{1,5},{5... | collective-permute-start | bytes 786440 | tf_op jit(solution)/shard_map/ppermute | solution.py:173
  28.7 5.2 %collective-permute-start.10 = (bf16[64,512]{1,0:T(8,128)(2,1)S(1)}, bf16[64,512]{1,0:T(8,128)(2,1)S(1)}, u32[]{:S(2)}, u32[]{:S(2)}) collective-permute-start(bf16[64,512]{1,0:T(8,128)(2,1)S(1)} %get-tuple-element.24), channel_id=1, source_target_pairs={{0,24},{1,25},{2,26},{3,27},{4,7},{5,6},{6,5},{7,4},{8,16},{9,17},... | collective-permute-start | bytes 196616 | tf_op jit(solution)/shard_map/ppermute | solution.py:187
  30.7 4.3 %collective-permute-start.11 = (bf16[64,512]{1,0:T(8,128)(2,1)S(1)}, bf16[64,512]{1,0:T(8,128)(2,1)S(1)}, u32[]{:S(2)}, u32[]{:S(2)}) collective-permute-start(bf16[64,512]{1,0:T(8,128)(2,1)S(1)} %get-tuple-element.23), channel_id=1, source_target_pairs={{0,16},{1,17},{2,18},{3,19},{4,6},{5,7},{6,4},{7,5},{8,24},{9,25},... | collective-permute-start | bytes 196616 | tf_op jit(solution)/shard_map/ppermute | solution.py:187
  31.7 4.3 %collective-permute-start.9 = (bf16[64,512]{1,0:T(8,128)(2,1)S(1)}, bf16[64,512]{1,0:T(8,128)(2,1)S(1)}, u32[]{:S(2)}, u32[]{:S(2)}) collective-permute-start(bf16[64,512]{1,0:T(8,128)(2,1)S(1)} %get-tuple-element.22), channel_id=1, source_target_pairs={{0,8},{1,9},{2,10},{3,11},{4,5},{5,4},{6,7},{7,6},{8,0},{9,1},{10,... | collective-permute-start | bytes 196616 | tf_op jit(solution)/shard_map/ppermute | solution.py:187
  36.0 6.2 %collective-permute-start.12 = (bf16[64,512]{1,0:T(8,128)(2,1)S(1)}, bf16[64,512]{1,0:T(8,128)(2,1)S(1)}, u32[]{:S(2)}, u32[]{:S(2)}) collective-permute-start(bf16[64,512]{1,0:T(8,128)(2,1)S(1)} %fusion.7), channel_id=1, source_target_pairs={{0,3},{1,2},{2,1},{3,0},{4,28},{5,29},{6,30},{7,31},{8,11},{9,10},... | collective-permute-start | bytes 196616 | tf_op jit(solution)/shard_map/ppermute | solution.py:187
  38.6 5.2 %collective-permute-start.13 = (bf16[64,512]{1,0:T(8,128)(2,1)S(1)}, bf16[64,512]{1,0:T(8,128)(2,1)S(1)}, u32[]{:S(2)}, u32[]{:S(2)}) collective-permute-start(bf16[64,512]{1,0:T(8,128)(2,1)S(1)} %fusion.7), channel_id=1, source_target_pairs={{0,2},{1,3},{2,0},{3,1},{4,20},{5,21},{6,22},{7,23},{8,10},{9,11},... | collective-permute-start | bytes 196616 | tf_op jit(solution)/shard_map/ppermute | solution.py:187
  40.4 4.3 %collective-permute-start.14 = (bf16[64,512]{1,0:T(8,128)(2,1)S(1)}, bf16[64,512]{1,0:T(8,128)(2,1)S(1)}, u32[]{:S(2)}, u32[]{:S(2)}) collective-permute-start(bf16[64,512]{1,0:T(8,128)(2,1)S(1)} %fusion.7), channel_id=1, source_target_pairs={{0,1},{1,0},{2,3},{3,2},{4,12},{5,13},{6,14},{7,15},{8,9},{9,8},{1... | collective-permute-start | bytes 196616 | tf_op jit(solution)/shard_map/ppermute | solution.py:187
  44.7 5.2 %collective-permute-start.18 = (bf16[64,512]{1,0:T(8,128)(2,1)S(1)}, bf16[64,512]{1,0:T(8,128)(2,1)S(1)}, u32[]{:S(2)}, u32[]{:S(2)}) collective-permute-start(bf16[64,512]{1,0:T(8,128)(2,1)S(1)} %add_convert_fusion), channel_id=1, source_target_pairs={{0,24},{1,25},{2,26},{3,27},{4,7},{5,6},{6,5},{7,4},{8,16},{9,17},... | collective-permute-start | bytes 196616 | tf_op jit(solution)/shard_map/ppermute | solution.py:187
  46.2 4.4 %collective-permute-start.15 = (bf16[64,512]{1,0:T(8,128)(2,1)S(1)}, bf16[64,512]{1,0:T(8,128)(2,1)S(1)}, u32[]{:S(2)}, u32[]{:S(2)}) collective-permute-start(bf16[64,512]{1,0:T(8,128)(2,1)S(1)} %add_convert_fusion), channel_id=1, source_target_pairs={{0,16},{1,17},{2,18},{3,19},{4,6},{5,7},{6,4},{7,5},{8,24},{9,25},... | collective-permute-start | bytes 196616 | tf_op jit(solution)/shard_map/ppermute | solution.py:187
  46.7 4.3 %collective-permute-start.16 = (bf16[64,512]{1,0:T(8,128)(2,1)S(1)}, bf16[64,512]{1,0:T(8,128)(2,1)S(1)}, u32[]{:S(2)}, u32[]{:S(2)}) collective-permute-start(bf16[64,512]{1,0:T(8,128)(2,1)S(1)} %add_convert_fusion), channel_id=1, source_target_pairs={{0,8},{1,9},{2,10},{3,11},{4,5},{5,4},{6,7},{7,6},{8,0},{9,1},{10,... | collective-permute-start | bytes 196616 | tf_op jit(solution)/shard_map/ppermute | solution.py:187
  50.0 1.4 %collective-permute-start.19 = (bf16[128,512]{1,0:T(8,128)(2,1)S(1)}, bf16[128,512]{1,0:T(8,128)(2,1)S(1)}, u32[]{:S(2)}, u32[]{:S(2)}) collective-permute-start(bf16[128,512]{1,0:T(8,128)(2,1)S(1)} %pad_maximum_fusion.refs_0_), channel_id=1, source_target_pairs={{0,4},{4,0},{8,12},{12,8},{16,20},{20,16},{24,28},{28,24},{1,5},{5... | collective-permute-start | bytes 393224 | tf_op jit(solution)/shard_map/ppermute | solution.py:173
  51.0 1.3 %collective-permute-start.17 = (bf16[128,512]{1,0:T(8,128)(2,1)S(1)}, bf16[128,512]{1,0:T(8,128)(2,1)S(1)}, u32[]{:S(2)}, u32[]{:S(2)}) collective-permute-start(bf16[128,512]{1,0:T(8,128)(2,1)S(1)} %constant_dynamic-update-slice_fusion.4.refs_1_), channel_id=1, source_target_pairs={{0,4},{4,0},{8,12},{12,8},{16,20},{20,16},{24,28},{28,24},{1,5},{5... | collective-permute-start | bytes 393224 | tf_op jit(solution)/shard_map/ppermute | solution.py:173
  (1 other events, 0.7 us)
